TPU v7x, 32 devices: a whole 2x2x4 slice. The times are simulated.
32 devices in a mesh: wide: 16 (over z, x, core), narrow: 2 (over y).
Axes of the slice: x: 2, y: 2, z: 4, core: 2. Of those that a mesh axis runs over, the one named last changes fastest.
Arguments:
- joint_in: bfloat16 [20480, 768], P(('wide', 'narrow')), may hold values from -6 to 6
- cotangent: bfloat16 [20480, 768], P(('wide', 'narrow')), may hold values from -6 to 6
- segment_ids: int32 [20480], replicated, may hold values from 0 to 31, never falling along the last dimension, each value on 1 to 1280 neighbouring positions
- layer_index: int32 [1], replicated, may hold values from 0 to 11
- step_index: int32 [1], replicated, may hold values from 0 to 99999
- gain_one: float32 [768], P(('wide', 'narrow')), may hold values from 0.5 to 1.5
- w_qkv: float32 [768, 2304], P(('wide', 'narrow')), may hold values from -0.21875 to 0.21875
- w_attn_out: float32 [768, 768], P(('wide', 'narrow')), may hold values from -0.875 to 0.875
- gain_two: float32 [768], P(('wide', 'narrow')), may hold values from 0.5 to 1.5
- w_hidden: float32 [768, 3072], P(('wide', 'narrow')), may hold values from -0.21875 to 0.21875
- w_proj: float32 [3072, 768], P(('wide', 'narrow')), may hold values from -0.109375 to 0.109375
- mom_gain_one: float32 [768], P(('wide', 'narrow')), may hold values from -96 to 96
- mom_qkv: float32 [768, 2304], P(('wide', 'narrow')), may hold values from -6 to 6
- mom_attn_out: float32 [768, 768], P(('wide', 'narrow')), may hold values from -6 to 6
- mom_gain_two: float32 [768], P(('wide', 'narrow')), may hold values from -96 to 96
- mom_hidden: float32 [768, 3072], P(('wide', 'narrow')), may hold values from -96 to 96
- mom_proj: float32 [3072, 768], P(('wide', 'narrow')), may hold values from -192 to 192
Outputs:
- joint_out: bfloat16 [20480, 768], P(('wide', 'narrow'))
- grad_in: bfloat16 [20480, 768], P(('wide', 'narrow'))
- step_gain_one: float32 [768], P(('wide', 'narrow'))
- step_qkv: float32 [768, 2304], P(('wide', 'narrow'))
- step_attn_out: float32 [768, 768], P(('wide', 'narrow'))
- step_gain_two: float32 [768], P(('wide', 'narrow'))
- step_hidden: float32 [768, 3072], P(('wide', 'narrow'))
- step_proj: float32 [3072, 768], P(('wide', 'narrow'))
- next_gain_one: float32 [768], P(('wide', 'narrow'))
- next_qkv: float32 [768, 2304], P(('wide', 'narrow'))
- next_attn_out: float32 [768, 768], P(('wide', 'narrow'))
- next_gain_two: float32 [768], P(('wide', 'narrow'))
- next_hidden: float32 [768, 3072], P(('wide', 'narrow'))
- next_proj: float32 [3072, 768], P(('wide', 'narrow'))
Inputs may be any that keep to these rules, and one draw needn't show every extreme that they name: `segment_ids`: segment ids never fall along the rows; each sequence has 1 to 1280 tokens and one has exactly 1280.
All inputs are finite; a program needn't handle non-finite values.
Results may differ from a plain program's by a relative error of at most 0.013.
The roundings to bfloat16 on the way count: a program that leaves them out, or rounds other values in their place, can miss the bound.
Values may be sent and summed in bfloat16 or wider, within the bound.
No kernel may reach another device: no remote copies, remote signals or barrier semaphores. Data moves between devices by JAX's collectives and lax.ppermute only.
A program may use at most 256 MiB of HBM per device.

v0:
```python
import functools

import jax
import jax.numpy as jnp
from jax import lax
from jax.experimental import pallas as pl
from jax.experimental.pallas import tpu as pltpu
from jax.sharding import PartitionSpec as P

HEAD = 64
PAIR = 2 * HEAD
QT = 128
KT = 320
GROUP = 3
BRIEF = pl.CostEstimate(flops=1, bytes_accessed=1, transcendentals=0)

eps = 1e-06
base_rate = 0.01
decay_rate = 0.65
total_steps = 100000.0
momentum_rate = 0.9

bf = jnp.bfloat16
f32 = jnp.float32


def dot(left, right):
    return jnp.dot(left, right, preferred_element_type=f32)


def contract_rows(left, right):
    return lax.dot_general(
        left, right, (((0,), (0,)), ((), ())), preferred_element_type=f32
    )


def contract_cols(left, right):
    return lax.dot_general(
        left, right, (((1,), (1,)), ((), ())), preferred_element_type=f32
    )


def normalize_parts(values):
    centre = jnp.mean(values, axis=-1, keepdims=True)
    centred = values - centre
    inverse = lax.rsqrt(jnp.mean(centred * centred, axis=-1, keepdims=True) + eps)
    return (centred * inverse, inverse)


def normalize_back(grad_out, normed, inverse, gain):
    grad_normed = grad_out * gain
    inner = grad_normed - jnp.mean(grad_normed, axis=-1, keepdims=True)
    inner = inner - normed * jnp.mean(grad_normed * normed, axis=-1, keepdims=True)
    return inverse * inner


def diag_wide(block):
    row = lax.broadcasted_iota(jnp.int32, block.shape, 0)
    zero = jnp.zeros_like(block)
    return jnp.concatenate(
        [jnp.where(row < HEAD, block, zero), jnp.where(row >= HEAD, block, zero)], axis=1
    )


def diag_tall(block):
    col = lax.broadcasted_iota(jnp.int32, block.shape, 1)
    zero = jnp.zeros_like(block)
    return jnp.concatenate(
        [jnp.where(col < HEAD, block, zero), jnp.where(col >= HEAD, block, zero)], axis=0
    )


def tile_bias(kseg_ref, qseg_ref, t):
    bias = jnp.where(kseg_ref[...] == qseg_ref[t, 0:1, :], 0.0, -1e30).astype(f32)
    return jnp.concatenate([bias, bias], axis=1)


def columns_of(pair):
    return slice(pair * PAIR, (pair + 1) * PAIR)


def copy_rows(odd, step, refs, out):
    for ref, at in zip(refs, block_starts(odd)):
        @pl.when((step >= at) & (step < at + 2))
        def _(ref=ref):
            out[...] = ref[...]


def block_starts(odd):
    return (0, 6 - 4 * odd, 2 + 4 * odd, 8)


def attend_kernel(begin, end, odd, *refs, pieces):
    blocks, (kseg_ref, own_ref, qseg_ref, order_ref) = refs[:4], refs[4:8]
    parts = refs[8:8 + 2 * pieces]
    (w_ref, gains_ref, a_ref, k_ref, v_ref, q_ref, o_ref, lse_ref,
     qbd, top, total, acc, x_ref, rel_ref) = refs[8 + 2 * pieces:]
    step = pl.program_id(0)
    width = x_ref.shape[1]
    pairs = width // PAIR
    tiles = qseg_ref.shape[0]
    scale = HEAD ** (-0.5)

    @pl.when(step == 0)
    def _():
        rows = parts[0].shape[0] // 2
        cut = parts[0].shape[1]
        for j in range(pieces):
            for h in range(2):
                of = slice(h * rows, (h + 1) * rows)
                core, other = j // 2 * 4 * rows, j % 2
                lo = core + (2 * h + other) * rows
                rel_ref[lo:lo + rows, :cut] = parts[j][of, :]
                lo = core + (2 * other + h) * rows
                rel_ref[lo:lo + rows, cut:] = parts[pieces + j][of, :]
        w_ref[...] = dot(order_ref[...], rel_ref[...]).astype(bf)
        gains_ref[...] = w_ref[:, 3 * width:].astype(f32).T[:8]
        n, _ = normalize_parts(own_ref[...].astype(f32))
        q = dot((n * gains_ref[0:1, :]).astype(bf), w_ref[:, :width]).astype(bf)
        q_ref[...] = q
        q = q.astype(f32) * scale
        for t in range(tiles):
            for p in range(pairs):
                qbd[t, p] = diag_wide(q[t * QT:(t + 1) * QT, columns_of(p)].T.astype(bf))
        top[...] = jnp.full(top.shape, -1e30, f32)
        total[...] = jnp.zeros(total.shape, f32)
        acc[...] = jnp.zeros(acc.shape, f32)

    def visit(queries):
        group = [(t, p) for t in queries for p in range(pairs)]
        bias = {i: tile_bias(kseg_ref, qseg_ref, t) for i, t in enumerate(queries)}
        scores = [
            dot(k_ref[:, columns_of(p)], qbd[t, p]) + bias[j // pairs]
            for j, (t, p) in enumerate(group)
        ]
        olds = [top[t, p:p + 1, :] for t, p in group]
        news = [jnp.maximum(old, jnp.max(s, axis=0, keepdims=True)) for old, s in zip(olds, scores)]
        expo = [jnp.exp(s - new) for s, new in zip(scores, news)]
        shrinks = [jnp.exp(old - new) for old, new in zip(olds, news)]
        sums = [
            total[t, p:p + 1, :] * shrink + jnp.sum(e, axis=0, keepdims=True)
            for (t, p), shrink, e in zip(group, shrinks, expo)
        ]
        gots = [
            contract_rows(v_ref[:, columns_of(p)], e.astype(bf)) for (t, p), e in zip(group, expo)
        ]
        for (t, p), new, shrink, summed, got in zip(group, news, shrinks, sums, gots):
            top[t, p:p + 1, :] = new
            total[t, p:p + 1, :] = summed
            lo, mid, hi = p * PAIR, p * PAIR + HEAD, (p + 1) * PAIR
            acc[t, lo:mid, :] = acc[t, lo:mid, :] * shrink[:, :QT] + got[:HEAD, :QT]
            acc[t, mid:hi, :] = acc[t, mid:hi, :] * shrink[:, QT:] + got[HEAD:, QT:]

    def visits(first, last):
        twos = (last - first) // 2

        def two(j, carry):
            visit([first + 2 * j, first + 2 * j + 1])
            return carry

        lax.fori_loop(0, twos, two, 0)

        @pl.when(first + 2 * twos < last)
        def _():
            visit([last - 1])

    @pl.when(begin[step] < end[step])
    def _():
        copy_rows(odd[0], step, blocks, x_ref)

        @pl.when((step >= 4) & (step < 6))
        def _():
            x_ref[...] = own_ref[pl.ds(pl.multiple_of((step - 4) * KT, KT), KT), :]

        n, _ = normalize_parts(x_ref[...].astype(f32))
        a = (n * gains_ref[0:1, :]).astype(bf)
        a_ref[...] = a
        k_ref[...] = dot(a, w_ref[:, width:2 * width]).astype(bf)
        v_ref[...] = dot(a, w_ref[:, 2 * width:3 * width]).astype(bf)
        visits(begin[step], end[step])

    @pl.when(step == pl.num_programs(0) - 1)
    def _():
        for t in range(tiles):
            for p in range(pairs):
                sums = total[t, p:p + 1, :]
                lse_ref[t, p] = top[t, p:p + 1, :] + jnp.log(sums)
                inv = 1.0 / sums
                lo, mid, hi = p * PAIR, p * PAIR + HEAD, (p + 1) * PAIR
                out = jnp.concatenate(
                    [acc[t, lo:mid, :] * inv[:, :QT], acc[t, mid:hi, :] * inv[:, QT:]], axis=0
                )
                o_ref[t * QT:(t + 1) * QT, lo:hi] = out.T.astype(bf)


def block_specs(width, key):
    def spec(number):
        def index(step, begin, end, span, odd):
            return (jnp.clip(key(step) - block_starts(odd[0])[number], 0, 1), 0)

        return pl.BlockSpec((KT, width), index)

    return [spec(number) for number in range(4)]


def attend(scalars, blocks, kseg, x_own, qseg, order, ones, twos):
    rows, width = x_own.shape
    window = 5 * rows
    tiles = rows // QT
    pairs = width // PAIR
    columns = ones[0].shape[1] + twos[0].shape[1]
    whole = pl.BlockSpec(memory_space=pltpu.VMEM)

    def at_used(j, begin, end, span, odd):
        return (jnp.clip(j, span[0], span[1] - 1), 0)

    def kernel(begin, end, span, odd, *refs):
        attend_kernel(begin, end, odd, *refs, pieces=len(ones))

    tile = pl.BlockSpec((KT, width), at_used)
    return pl.pallas_call(
        kernel,
        grid_spec=pltpu.PrefetchScalarGridSpec(
            num_scalar_prefetch=4,
            grid=(window // KT,),
            in_specs=block_specs(width, lambda j: j)
            + [pl.BlockSpec((KT, QT), at_used)]
            + [whole] * (3 + 2 * len(ones)),
            out_specs=[whole, whole, tile, tile, tile, whole, whole, whole],
            scratch_shapes=[
                pltpu.VMEM((tiles, pairs, PAIR, 2 * QT), bf),
                pltpu.VMEM((tiles, 8, 2 * QT), f32),
                pltpu.VMEM((tiles, 8, 2 * QT), f32),
                pltpu.VMEM((tiles, width, QT), f32),
                pltpu.VMEM((KT, width), bf),
                pltpu.VMEM((width, columns), bf),
            ],
        ),
        out_shape=[
            jax.ShapeDtypeStruct((width, columns), bf),
            jax.ShapeDtypeStruct((8, width), f32),
            jax.ShapeDtypeStruct((window, width), bf),
            jax.ShapeDtypeStruct((window, width), bf),
            jax.ShapeDtypeStruct((window, width), bf),
            jax.ShapeDtypeStruct((rows, width), bf),
            jax.ShapeDtypeStruct((rows, width), bf),
            jax.ShapeDtypeStruct((tiles, pairs, 1, 2 * QT), f32),
        ],
        compiler_params=pltpu.CompilerParams(vmem_limit_bytes=56 * 1024 * 1024),
        cost_estimate=BRIEF,
        name="attend",
    )(*scalars, *blocks, kseg, x_own, qseg, order, *ones, *twos)


def back_tile(begin, end, j, refs, scratch):
    k_ref, v_ref, kseg_ref, qseg_ref, lse_ref = refs
    qbd, dobd, qn, don, delta, dq_acc, dk_acc, dv_acc = scratch
    pairs = qbd.shape[1]
    dk_acc[...] = jnp.zeros(dk_acc.shape, f32)
    dv_acc[...] = jnp.zeros(dv_acc.shape, f32)

    def visit(t):
        bias = tile_bias(kseg_ref, qseg_ref, t)
        for base in range(0, pairs, GROUP):
            group = range(base, min(pairs, base + GROUP))
            keys = [k_ref[:, columns_of(p)] for p in group]
            scores = [dot(kp, qbd[t, p]) for kp, p in zip(keys, group)]
            dprobs = [dot(v_ref[:, columns_of(p)], dobd[t, p]) for p in group]
            probs = [jnp.exp(s + bias - lse_ref[t, p]) for s, p in zip(scores, group)]
            ds = [
                (pr * (dp - delta[t, p:p + 1, :])).astype(bf)
                for pr, dp, p in zip(probs, dprobs, group)
            ]
            got_v = [dot(pr.astype(bf), don[t, p]) for pr, p in zip(probs, group)]
            got_k = [dot(d, qn[t, p]) for d, p in zip(ds, group)]
            got_q = [contract_rows(kp, d) for kp, d in zip(keys, ds)]
            for i, p in enumerate(group):
                lo, mid, hi = p * PAIR, p * PAIR + HEAD, (p + 1) * PAIR
                dv_acc[:, lo:hi] += got_v[i]
                dk_acc[:, lo:hi] += got_k[i]
                dq_acc[t, lo:mid, :] += got_q[i][:HEAD, :QT]
                dq_acc[t, mid:hi, :] += got_q[i][HEAD:, QT:]

    first = begin[j]
    twos = (end[j] - first) // 2

    def two(i, carry):
        visit(first + 2 * i)
        visit(first + 2 * i + 1)
        return carry

    lax.fori_loop(0, twos, two, 0)

    @pl.when(first + 2 * twos < end[j])
    def _():
        visit(end[j] - 1)

    return dk_acc[...].astype(bf), dv_acc[...].astype(bf)


def back_prepare(q_ref, do_ref, o_ref, scratch):
    qbd, dobd, qn, don, delta = scratch
    tiles, pairs = qbd.shape[:2]
    scale = HEAD ** (-0.5)
    for t in range(tiles):
        at = slice(t * QT, (t + 1) * QT)
        for p in range(pairs):
            cols = columns_of(p)
            q = q_ref[at, cols].astype(f32) * scale
            do = do_ref[at, cols].astype(f32)
            do_t = do.T
            qbd[t, p] = diag_wide(q.T.astype(bf))
            dobd[t, p] = diag_wide(do_t.astype(bf))
            qn[t, p] = diag_tall(q.astype(bf))
            don[t, p] = diag_tall(do.astype(bf))
            both = do_t * o_ref[at, cols].astype(f32).T
            delta[t, p:p + 1, :QT] = jnp.sum(both[:HEAD], axis=0, keepdims=True)
            delta[t, p:p + 1, QT:] = jnp.sum(both[HEAD:], axis=0, keepdims=True)


def back_share(dk, dv, a, w_ref, acc):
    width = dk.shape[1]
    da = contract_cols(dk, w_ref[:, width:2 * width]) + contract_cols(dv, w_ref[:, 2 * width:3 * width])
    acc[:, :width] += contract_rows(a, dk)
    acc[:, width:] += contract_rows(a, dv)
    return da


def outer_kernel(begin, end, span, odd, k_ref, v_ref, a_ref, kseg_ref, q_ref, do_ref, o_ref,
                 lse_ref, qseg_ref, w_ref, b0, b1, b2, b3, *refs, own):
    da_refs = refs[-15:-11]
    acc_ref, dq_ref, gg_ref, qbd, dobd, qn, don, delta, dk_acc, dv_acc, x_ref = refs[-11:]
    step = pl.program_id(0)
    j = jnp.where(step < own[0], step, step + own[1] - own[0])

    @pl.when(step == 0)
    def _():
        back_prepare(q_ref, do_ref, o_ref, (qbd, dobd, qn, don, delta))
        acc_ref[...] = jnp.zeros(acc_ref.shape, f32)
        dq_ref[...] = jnp.zeros(dq_ref.shape, f32)
        gg_ref[...] = jnp.zeros(gg_ref.shape, f32)

    used = begin[j] < end[j]

    def put(value):
        for ref, at in zip(da_refs, block_starts(odd[0])):
            @pl.when((j >= at) & (j < at + 2))
            def _(ref=ref):
                ref[...] = value

    @pl.when(used)
    def _():
        dk, dv = back_tile(
            begin, end, j, (k_ref, v_ref, kseg_ref, qseg_ref, lse_ref),
            (qbd, dobd, qn, don, delta, dq_ref, dk_acc, dv_acc),
        )
        da = back_share(dk, dv, a_ref[...], w_ref, acc_ref)
        put(da.astype(bf))
        copy_rows(odd[0], j, (b0, b1, b2, b3), x_ref)
        n, _ = normalize_parts(x_ref[...].astype(f32))
        gg_ref[0:1, :] += jnp.sum(da * n, axis=0, keepdims=True)

    @pl.when(jnp.logical_not(used))
    def _():
        put(jnp.zeros(x_ref.shape, bf))


def inner_kernel(begin, end, span, odd, k_ref, v_ref, a_ref, kseg_ref, q_ref, do_ref, o_ref,
                 lse_ref, qseg_ref, w_ref, x_ref, order_ref, gb_ref, acc_in, dq_in, gg_in,
                 *refs, own):
    (da_ref, keep_ref, send_ref,
     qbd, dobd, qn, don, delta, dk_acc, dv_acc, acc, dq_acc, gg, dq_all, a_all) = refs[-15:]
    step = pl.program_id(0)
    width = k_ref.shape[1]
    half = width // 2
    tiles, pairs = qbd.shape[:2]

    @pl.when(step == 0)
    def _():
        back_prepare(q_ref, do_ref, o_ref, (qbd, dobd, qn, don, delta))
        acc[...] = acc_in[...]
        dq_acc[...] = dq_in[...]
        gg[...] = jnp.zeros(gg.shape, f32)
        gg[0:1, :] = gg_in[0:1, :]
        gg[1:2, :] = gb_ref[0:1, :]

    dk, dv = back_tile(
        begin, end, step + own[0], (k_ref, v_ref, kseg_ref, qseg_ref, lse_ref),
        (qbd, dobd, qn, don, delta, dq_acc, dk_acc, dv_acc),
    )
    at = pl.ds(pl.multiple_of(step * KT, KT), KT)
    da_ref[at, :] = back_share(dk, dv, a_ref[...], w_ref, acc)
    a_all[at, :] = a_ref[...]

    @pl.when(step == pl.num_programs(0) - 1)
    def _():
        scale = HEAD ** (-0.5)
        for t in range(tiles):
            for p in range(pairs):
                cols = columns_of(p)
                dq_all[t * QT:(t + 1) * QT, cols] = (dq_acc[t, cols, :] * scale).T.astype(bf)
        dq = dq_all[...]
        da = da_ref[...] + contract_cols(dq, w_ref[:, :width])
        da_ref[...] = da
        n, _ = normalize_parts(x_ref[...].astype(f32))
        gg[0:1, :] += jnp.sum(da * n, axis=0, keepdims=True)
        order = order_ref[...]

        def put(lo, grad):
            both = contract_rows(order, grad.astype(bf)).astype(bf)
            keep_ref[:, lo:lo + both.shape[1]] = both[:half]
            send_ref[:, lo:lo + both.shape[1]] = both[half:]

        put(0, contract_rows(a_all[...], dq))
        put(width, acc[...])
        put(3 * width, gg[...].T)


def back_specs(window, rows, width, own, at_key):
    tiles = rows // QT
    pairs = width // PAIR
    whole = pl.BlockSpec(memory_space=pltpu.VMEM)
    tile = pl.BlockSpec((KT, width), at_key)
    specs = [tile, tile, tile, pl.BlockSpec((KT, QT), at_key)] + [whole] * 6
    scratch = [
        pltpu.VMEM((tiles, pairs, PAIR, 2 * QT), bf),
        pltpu.VMEM((tiles, pairs, PAIR, 2 * QT), bf),
        pltpu.VMEM((tiles, pairs, 2 * QT, PAIR), bf),
        pltpu.VMEM((tiles, pairs, 2 * QT, PAIR), bf),
        pltpu.VMEM((tiles, 8, 2 * QT), f32),
        pltpu.VMEM((KT, width), f32),
        pltpu.VMEM((KT, width), f32),
    ]
    return specs, scratch, whole


def outer_back(scalars, k, v, a, kseg, q, do, o, lse, qseg, weight, blocks, *deps):
    window, width = k.shape
    rows = q.shape[0]
    own = (2 * rows // KT, 3 * rows // KT)
    steps = window // KT - own[1] + own[0]

    def key(step):
        return jnp.where(step < own[0], step, step + own[1] - own[0])

    def at_key(step, begin, end, span, odd):
        return (jnp.clip(key(step), span[0], span[1] - 1), 0)

    specs, scratch, whole = back_specs(window, rows, width, own, at_key)
    return pl.pallas_call(
        functools.partial(outer_kernel, own=own),
        grid_spec=pltpu.PrefetchScalarGridSpec(
            num_scalar_prefetch=4,
            grid=(steps,),
            in_specs=specs
            + block_specs(width, key)
            + [pl.BlockSpec(memory_space=pl.ANY)] * len(deps),
            out_specs=block_specs(width, key) + [whole, whole, whole],
            scratch_shapes=scratch + [pltpu.VMEM((KT, width), bf)],
        ),
        out_shape=[
            *[jax.ShapeDtypeStruct((rows, width), bf)] * 4,
            jax.ShapeDtypeStruct((width, 2 * width), f32),
            jax.ShapeDtypeStruct((rows // QT, width, QT), f32),
            jax.ShapeDtypeStruct((8, width), f32),
        ],
        compiler_params=pltpu.CompilerParams(vmem_limit_bytes=50 * 1024 * 1024),
        cost_estimate=BRIEF,
        name="outer_back",
    )(*scalars, k, v, a, kseg, q, do, o, lse, qseg, weight, *blocks, *deps)


def inner_back(scalars, k, v, a, kseg, q, do, o, lse, qseg, weight, x_own, order, gain_grad,
               partial, *deps):
    window, width = k.shape
    rows = q.shape[0]
    own = (2 * rows // KT, 3 * rows // KT)
    half = width // 2
    columns = weight.shape[1]

    def at_key(step, *_):
        return (step + own[0], 0)

    specs, scratch, whole = back_specs(window, rows, width, own, at_key)
    scratch += [
        pltpu.VMEM((width, 2 * width), f32),
        pltpu.VMEM((rows // QT, width, QT), f32),
        pltpu.VMEM((columns - 3 * width, width), f32),
        pltpu.VMEM((rows, width), bf),
        pltpu.VMEM((rows, width), bf),
    ]
    return pl.pallas_call(
        functools.partial(inner_kernel, own=own),
        grid_spec=pltpu.PrefetchScalarGridSpec(
            num_scalar_prefetch=4,
            grid=(own[1] - own[0],),
            in_specs=specs + [whole] * 6 + [pl.BlockSpec(memory_space=pl.ANY)] * len(deps),
            out_specs=[whole, whole, whole],
            scratch_shapes=scratch,
        ),
        out_shape=[
            jax.ShapeDtypeStruct((rows, width), f32),
            jax.ShapeDtypeStruct((half, columns), bf),
            jax.ShapeDtypeStruct((half, columns), bf),
        ],
        compiler_params=pltpu.CompilerParams(vmem_limit_bytes=46 * 1024 * 1024),
        cost_estimate=BRIEF,
        name="inner_back",
    )(*scalars, k, v, a, kseg, q, do, o, lse, qseg, weight, x_own, order, gain_grad, *partial, *deps)


def middle_kernel(x_ref, o_ref, dz_ref, gain_ref, order_ref, wo_ref, wh_ref, wp_ref,
                  out_ref, hkeep_ref, hsend_ref, pkeep_ref, psend_ref, okeep_ref, osend_ref,
                  dx_ref, do_ref, gg_ref, normed, inverse, second, ordered, acc, dsec):
    step = pl.program_id(0)
    width = x_ref.shape[1]
    half = width // 2

    @pl.when(step == 0)
    def _():
        value = x_ref[...].astype(f32) + dot(o_ref[...], wo_ref[...])
        acc[...] = value
        n, r = normalize_parts(value)
        normed[...] = n
        inverse[...] = jnp.broadcast_to(r, inverse.shape)
        b = (n * gain_ref[1:2, :]).astype(bf)
        second[...] = b
        ordered[...] = dot(b, order_ref[...]).astype(bf)
        dsec[...] = jnp.zeros(dsec.shape, f32)

    dz = dz_ref[...]
    wh = wh_ref[...]
    wp = wp_ref[...]
    u = dot(second[...], wh)
    cdf = 0.5 * (1.0 + lax.erf(u * (0.5 ** 0.5)))
    pdf = jnp.exp(-0.5 * u * u) * 0.3989422804014327
    hid = (u * cdf).astype(bf)
    du = (contract_cols(dz, wp) * (cdf + u * pdf)).astype(bf)
    acc[...] += dot(hid, wp)

    def put(keep_ref, send_ref, grad):
        grad = grad.astype(bf)
        keep_ref[...] = grad[:half]
        send_ref[...] = grad[half:]

    put(hkeep_ref, hsend_ref, contract_rows(ordered[...], du))
    put(pkeep_ref, psend_ref, contract_rows(dot(hid, order_ref[...]).astype(bf), dz))
    dsec[...] += contract_cols(du, wh)

    @pl.when(step == pl.num_programs(0) - 1)
    def _():
        out_ref[...] = acc[...].astype(bf)
        n = normed[...]
        db = dsec[...]
        gg_ref[...] = jnp.broadcast_to(jnp.sum(db * n, axis=0, keepdims=True), gg_ref.shape)
        dx = dz.astype(f32) + normalize_back(db, n, inverse[:, 0:1], gain_ref[1:2, :])
        dx_ref[...] = dx
        dproj = dx.astype(bf)
        put(okeep_ref, osend_ref, contract_rows(dot(o_ref[...], order_ref[...]).astype(bf), dproj))
        do_ref[...] = contract_cols(dproj, wo_ref[...]).astype(bf)


def middle(x, o, dz, gains, order, packed):
    rows, width = x.shape
    ratio = (packed.shape[1] - width) // (2 * width)
    whole = pl.BlockSpec(memory_space=pltpu.VMEM)
    line = jax.ShapeDtypeStruct((rows, width), f32)
    low = jax.ShapeDtypeStruct((rows, width), bf)
    half = width // 2
    part = pl.BlockSpec((half, width), lambda s: (0, s))
    message = jax.ShapeDtypeStruct((half, ratio * width), bf)
    small = jax.ShapeDtypeStruct((half, width), bf)
    return pl.pallas_call(
        middle_kernel,
        grid=(ratio,),
        in_specs=[whole] * 5
        + [
            pl.BlockSpec((width, width), lambda s: (0, 0)),
            pl.BlockSpec((width, width), lambda s: (0, 1 + s)),
            pl.BlockSpec((width, width), lambda s: (0, 1 + ratio + s)),
        ],
        out_specs=[whole] + [part] * 4 + [whole] * 5,
        out_shape=[low] + [message] * 4 + [small, small, line, low, jax.ShapeDtypeStruct((8, width), f32)],
        scratch_shapes=[
            pltpu.VMEM((rows, width), f32),
            pltpu.VMEM((rows, 128), f32),
            pltpu.VMEM((rows, width), bf),
            pltpu.VMEM((rows, width), bf),
            pltpu.VMEM((rows, width), f32),
            pltpu.VMEM((rows, width), f32),
        ],
        compiler_params=pltpu.CompilerParams(vmem_limit_bytes=52 * 1024 * 1024),
        cost_estimate=BRIEF,
        name="middle",
    )(x, o, dz, gains, order, packed, packed, packed)


def add(*arrays):
    total = arrays[0].astype(f32)
    for array in arrays[1:]:
        total += array.astype(f32)
    return total


class Links:
    def __init__(self, wide):
        self.wide = wide
        self.outer = wide // 4

    def swap(self, array, name):
        if name == "y":
            return lax.ppermute(array, "narrow", [(0, 1), (1, 0)])
        flip = 1 if name == "core" else 2
        return lax.ppermute(array, "wide", [(j, j ^ flip) for j in range(self.wide)])

    def flip_z(self, array, s):
        return lax.ppermute(array, "wide", [(j, j ^ (4 * s)) for j in range(self.wide)])

    def distance(self, at):
        bits = self.outer.bit_length() - 1
        return sum(((at >> b) & 1) << (bits - 1 - b) for b in range(bits))

    def order(self, width):
        place = lax.axis_index("wide")
        rows = width // (2 * self.wide)
        at = jnp.arange(width, dtype=jnp.int32)
        row, at = at % rows, at // rows
        z, at = self.distance(at % self.outer) ^ (place // 4), at // self.outer
        y, at = (at + lax.axis_index("narrow")) % 2, at // 2
        x, at = (at + place // 2) % 2, at // 2
        core = (at + place) % 2
        source = (((z * 2 + x) * 2 + core) * 2 + y) * rows + row
        return (jnp.arange(width, dtype=jnp.int32)[:, None] == source[None, :]).astype(bf)

    def along_z(self, shard):
        parts = [shard] + [self.flip_z(shard, self.distance(j)) for j in range(1, self.outer)]
        return jnp.concatenate(parts, axis=0)

    def along_xy(self, mine):
        cut = halfway(mine)
        one, two = mine[:, :cut], mine[:, cut:]
        one = jnp.concatenate([one, self.swap(one, "x")], axis=0)
        two = jnp.concatenate([two, self.swap(two, "y")], axis=0)
        one = (one, self.swap(one, "y"))
        two = (two, self.swap(two, "x"))
        return (
            one + tuple(self.swap(piece, "core") for piece in one),
            two + tuple(self.swap(piece, "core") for piece in two),
        )

    def first(self, pairs, *deps):
        rows = pairs[0][0].shape[0] // 4
        cuts = [halfway(keep) for keep, _ in pairs]
        wide = [sum(cuts), sum(keep.shape[1] for keep, _ in pairs) - sum(cuts)]

        def kernel(*refs):
            count = 2 * len(pairs)
            keep_x, send_x, keep_y, send_y = refs[-4:]
            at = [0, 0]
            for keep, got, cut in zip(refs[0:count:2], refs[1:count:2], cuts):
                rest = keep.shape[1] - cut
                one, two = slice(0, cut), slice(cut, cut + rest)
                to = slice(at[0], at[0] + cut)
                keep_x[:, to] = add(keep[:2 * rows, one], got[:2 * rows, one]).astype(bf)
                send_x[:, to] = add(keep[2 * rows:, one], got[2 * rows:, one]).astype(bf)
                to = slice(at[1], at[1] + rest)
                for j, out in enumerate((keep_y, send_y, keep_y, send_y)):
                    of = slice(j * rows, (j + 1) * rows)
                    into = slice(j // 2 * rows, (j // 2 + 1) * rows)
                    out[into, to] = add(keep[of, two], got[of, two]).astype(bf)
                at = [at[0] + cut, at[1] + rest]

        shapes = [(2 * rows, wide[0])] * 2 + [(2 * rows, wide[1])] * 2
        keep_x, send_x, keep_y, send_y = stage(kernel, sum(pairs, ()), deps, shapes)
        return (keep_x, keep_y), (self.swap(send_x, "x"), self.swap(send_y, "y"))

    def second(self, keep, got, *deps):
        rows = keep[0].shape[0] // 2

        def kernel(keep_x, keep_y, got_x, got_y, *refs):
            for keep, got, hold, send in ((keep_x, got_x, *refs[-4:-2]), (keep_y, got_y, *refs[-2:])):
                hold[...] = add(keep[:rows], got[:rows]).astype(bf)
                send[...] = add(keep[rows:], got[rows:]).astype(bf)

        shapes = [(rows, keep[0].shape[1])] * 2 + [(rows, keep[1].shape[1])] * 2
        keep_x, send_x, keep_y, send_y = stage(kernel, keep + got, deps, shapes)
        return (keep_x, keep_y), (self.swap(send_x, "y"), self.swap(send_y, "x"))

    def third(self, keep, got, *deps):
        cut = keep[0].shape[1]
        rows = keep[0].shape[0] // 2

        def kernel(keep_x, keep_y, got_x, got_y, *refs):
            hold, send = refs[-2:]
            for cols, keep, got in ((slice(0, cut), keep_x, got_x), (slice(cut, None), keep_y, got_y)):
                hold[:, cols] = add(keep[:rows], got[:rows]).astype(bf)
                send[:, cols] = add(keep[rows:], got[rows:]).astype(bf)

        hold, send = stage(kernel, keep + got, deps, [(rows, cut + keep[1].shape[1])] * 2)
        return hold, self.flip_z(send, 1)

    def fourth(self, keep, got, *deps):
        for bit in range(1, self.outer.bit_length() - 1):
            rows = keep.shape[0] // 2
            if rows % 8:
                total = add(keep, got).astype(bf)
                keep, send = total[:rows], total[rows:]
            else:
                keep, send = stage(halves_kernel, (keep, got), deps, [(rows, keep.shape[1])] * 2)
            got = self.flip_z(send, 1 << bit)
        return keep, got


def halves_kernel(keep, got, *refs):
    hold, send = refs[-2:]
    total = add(keep[...], got[...])
    hold[...] = total[:hold.shape[0]].astype(bf)
    send[...] = total[hold.shape[0]:].astype(bf)


def first_kernel(hidk, hidg, projk, projg, outk_x, outg_x, outk_y, outg_y,
                 keep_x, send_x, keep_y, send_y):
    rows = hidk.shape[0] // 4
    last = pl.num_programs(0) - 1

    def write(one, two):
        cols = slice(0, one[0].shape[1])
        keep_x[:, cols] = add(*(v[:2 * rows, :] for v in one)).astype(bf)
        send_x[:, cols] = add(*(v[2 * rows:, :] for v in one)).astype(bf)
        for j, out in enumerate((keep_y, send_y, keep_y, send_y)):
            of = slice(j * rows, (j + 1) * rows)
            out[j // 2 * rows:(j // 2 + 1) * rows, cols] = add(*(v[of, :] for v in two)).astype(bf)

    @pl.when(pl.program_id(0) < last)
    def _():
        write((hidk, hidg), (projk, projg))

    @pl.when(pl.program_id(0) == last)
    def _():
        write((outk_x, outg_x), (outk_y, outg_y))


class Middle:
    def __init__(self, links):
        self.links = links

    def first(self, hid, proj, out):
        rows, columns = hid[0].shape
        block = out[0].shape[1]
        steps = columns // block
        tile = pl.BlockSpec((rows, block), lambda j: (0, jnp.minimum(j, steps - 1)))
        half = [pl.BlockSpec((rows, block // 2), lambda j, at=at: (0, at)) for at in range(2)]
        shape = jax.ShapeDtypeStruct((rows // 2, columns + block // 2), bf)
        keep_x, send_x, keep_y, send_y = pl.pallas_call(
            first_kernel,
            grid=(steps + 1,),
            in_specs=[tile] * 4 + [half[0]] * 2 + [half[1]] * 2,
            out_specs=[pl.BlockSpec((rows // 2, block), lambda j: (0, j))] * 4,
            out_shape=[shape] * 4,
            cost_estimate=BRIEF,
            name="first",
        )(*hid, *proj, *out, *out)
        return (keep_x, keep_y), (self.links.swap(send_x, "x"), self.links.swap(send_y, "y"))

    def second(self, keep, got, *deps):
        rows = keep[0].shape[0] // 4
        cut = keep[0].shape[1]

        def kernel(keep_x, keep_y, got_x, got_y, *refs):
            hold_x, hold_y, send = refs[-3:]
            halves = ((hold_x, slice(0, cut), keep_x, got_x), (hold_y, slice(cut, None), keep_y, got_y))
            for hold, cols, keep, got in halves:
                for j in range(2):
                    into = slice(j * rows, (j + 1) * rows)
                    of = slice(2 * j * rows, (2 * j + 1) * rows)
                    hold[into, :] = add(keep[of, :], got[of, :]).astype(bf)
                    of = slice((2 * j + 1) * rows, (2 * j + 2) * rows)
                    send[into, cols] = add(keep[of, :], got[of, :]).astype(bf)

        wide = keep[1].shape[1]
        shapes = [(2 * rows, cut), (2 * rows, wide), (2 * rows, cut + wide)]
        hold_x, hold_y, send = stage(kernel, keep + got, deps, shapes)
        return (hold_x, hold_y), self.links.flip_z(send, 1)

    def third(self, keep, got, *deps):
        rows = keep[0].shape[0] // 2
        cut = keep[0].shape[1]

        def kernel(keep_x, keep_y, got, *refs):
            for keep, cols, hold, send in (
                (keep_x, slice(0, cut), *refs[-4:-2]), (keep_y, slice(cut, None), *refs[-2:])
            ):
                hold[...] = add(keep[:rows, :], got[:rows, cols]).astype(bf)
                send[...] = add(keep[rows:, :], got[rows:, cols]).astype(bf)

        shapes = [(rows, cut)] * 2 + [(rows, keep[1].shape[1])] * 2
        hold_x, send_x, hold_y, send_y = stage(kernel, keep + (got,), deps, shapes)
        return (hold_x, hold_y), (self.links.swap(send_x, "y"), self.links.swap(send_y, "x"))

    def fourth(self, keep, got, *deps):
        rows = keep[0].shape[0] // 2
        cut = keep[0].shape[1]
        if rows % 8:
            total = jnp.concatenate([add(k, g).astype(bf) for k, g in zip(keep, got)], axis=1)
            hold, send = total[:rows], total[rows:]
        else:
            def kernel(keep_x, keep_y, got_x, got_y, *refs):
                hold, send = refs[-2:]
                for cols, keep, got in ((slice(0, cut), keep_x, got_x), (slice(cut, None), keep_y, got_y)):
                    total = add(keep[...], got[...])
                    hold[:, cols] = total[:rows].astype(bf)
                    send[:, cols] = total[rows:].astype(bf)

            hold, send = stage(kernel, keep + got, deps, [(rows, cut + keep[1].shape[1])] * 2)
        got = self.links.flip_z(send, 2)
        for bit in range(2, self.links.outer.bit_length() - 1):
            total = add(hold, got).astype(bf)
            rows = rows // 2
            hold, send = total[:rows], total[rows:]
            got = self.links.flip_z(send, 1 << bit)
        return hold, got


def collect(parts, *deps):
    def kernel(*refs):
        refs[-1][...] = add(*(ref[...] for ref in refs[:len(parts)]))

    return stage(kernel, parts, deps, [parts[0].shape], f32)[0]


def stage(kernel, operands, deps, shapes, kind=bf):
    whole = pl.BlockSpec(memory_space=pltpu.VMEM)
    elsewhere = pl.BlockSpec(memory_space=pl.ANY)
    return pl.pallas_call(
        kernel,
        in_specs=[whole] * len(operands) + [elsewhere] * len(deps),
        out_specs=[whole] * len(shapes),
        out_shape=[jax.ShapeDtypeStruct(shape, kind) for shape in shapes],
        compiler_params=pltpu.CompilerParams(vmem_limit_bytes=24 * 1024 * 1024),
        cost_estimate=BRIEF,
        name="stage",
    )(*operands, *deps)


def hold(values, *deps):
    count = len(values)

    def kernel(*refs):
        for source, out in zip(refs[:count], refs[-count:]):
            out[...] = source[...]

    whole = pl.BlockSpec(memory_space=pltpu.VMEM)
    elsewhere = pl.BlockSpec(memory_space=pl.ANY)
    return pl.pallas_call(
        kernel,
        in_specs=[whole] * count + [elsewhere] * len(deps),
        out_specs=[whole] * count,
        out_shape=[jax.ShapeDtypeStruct(v.shape, v.dtype) for v in values],
        cost_estimate=BRIEF,
        name="hold",
    )(*values, *deps)


def halfway(array):
    return (array.shape[1] // 2 + 127) // 128 * 128


def finish_kernel(x_ref, dx_ref, da_ref, gain_ref, out_ref):
    n, r = normalize_parts(x_ref[...].astype(f32))
    out_ref[...] = (dx_ref[...] + normalize_back(da_ref[...], n, r, gain_ref[0:1, :])).astype(bf)


def finish(x, dx, da, gains):
    rows, width = x.shape
    tile = pl.BlockSpec((QT, width), lambda i: (i, 0))
    return pl.pallas_call(
        finish_kernel,
        grid=(rows // QT,),
        in_specs=[tile] * 3 + [pl.BlockSpec(gains.shape, lambda i: (0, 0))],
        out_specs=tile,
        out_shape=jax.ShapeDtypeStruct((rows, width), bf),
        cost_estimate=BRIEF,
        name="finish",
    )(x, dx, da, gains)


def settle_kernel(own_ref, before_ref, partner_ref, across_ref, behind_ref, send_ref, *refs):
    own_out, send_out = refs[-2:]
    own_out[...] = add(*(r[...] for r in (own_ref, before_ref, partner_ref, across_ref, behind_ref)))
    send_out[...] = send_ref[...]


def settle(own, others, send, *deps):
    whole = pl.BlockSpec(memory_space=pltpu.VMEM)
    return pl.pallas_call(
        settle_kernel,
        in_specs=[whole] * 6 + [pl.BlockSpec(memory_space=pl.ANY)] * len(deps),
        out_specs=[whole] * 2,
        out_shape=[jax.ShapeDtypeStruct(v.shape, v.dtype) for v in (own, send)],
        compiler_params=pltpu.CompilerParams(vmem_limit_bytes=24 * 1024 * 1024),
        cost_estimate=BRIEF,
        name="settle",
    )(own, *others, send, *deps)


def update_kernel(rate_ref, sum_ref, hid_ref, proj_ref, mom_out, mom_hid, mom_proj,
                  step_out, step_hid, step_proj, next_out, next_hid, next_proj):
    rate = rate_ref[0]
    hidden = hid_ref.shape[1]
    width = mom_out.shape[1]
    half = width // 2
    far = hidden + half

    def put(step, following, at, momentum, grad):
        value = momentum_rate * momentum + grad
        following[at] = value
        step[at] = rate * value

    whole = slice(None)
    put(step_hid, next_hid, (whole, whole), mom_hid[...], hid_ref[...])
    for at, lo in ((slice(0, half), hidden), (slice(half, width), far + hidden)):
        put(step_out, next_out, (whole, at), mom_out[:, at], sum_ref[:, lo:lo + half])
    put(step_proj, next_proj, (whole, whole), mom_proj[...], proj_ref[...])


def update(rate, total, hid, proj, mom_out, mom_hid, mom_proj):
    whole = pl.BlockSpec(memory_space=pltpu.VMEM)
    moms = (mom_out, mom_hid, mom_proj)
    return pl.pallas_call(
        update_kernel,
        in_specs=[pl.BlockSpec(memory_space=pltpu.SMEM)] + [whole] * 6,
        out_specs=[whole] * 6,
        out_shape=[jax.ShapeDtypeStruct(m.shape, f32) for m in moms + moms],
        cost_estimate=BRIEF,
        name="update",
    )(rate, total, hid, proj, *moms)


def update_first_kernel(rate_ref, keep_ref, got_ref, mom_ref, step_ref, next_ref, gain_ref):
    total = add(keep_ref[...], got_ref[...])
    columns = mom_ref.shape[1]
    value = momentum_rate * mom_ref[...] + total[:, :columns]
    next_ref[...] = value
    step_ref[...] = rate_ref[0] * value
    gain_ref[...] = total[:, columns:]


def update_first(rate, keep, got, mom, *deps):
    whole = pl.BlockSpec(memory_space=pltpu.VMEM)
    rest = jax.ShapeDtypeStruct((mom.shape[0], keep.shape[1] - mom.shape[1]), f32)
    return pl.pallas_call(
        update_first_kernel,
        in_specs=[pl.BlockSpec(memory_space=pltpu.SMEM)] + [whole] * 3,
        out_specs=[whole] * 3,
        out_shape=[jax.ShapeDtypeStruct(mom.shape, f32)] * 2 + [rest],
        cost_estimate=BRIEF,
        name="update_first",
    )(rate, keep, got, mom)


def body(
    joint_in,
    cotangent,
    segment_ids,
    layer_index,
    step_index,
    gain_one,
    w_qkv,
    w_attn_out,
    gain_two,
    w_hidden,
    w_proj,
    mom_gain_one,
    mom_qkv,
    mom_attn_out,
    mom_gain_two,
    mom_hidden,
    mom_proj,
):
    rows, width = joint_in.shape
    wide = lax.axis_size("wide")
    both = ("wide", "narrow")
    shard = w_qkv.shape[0]
    hidden = w_hidden.shape[1]
    ratio = hidden // width
    odd = lax.axis_index("narrow")
    place = lax.axis_index("wide") * 2 + odd
    window = 5 * rows
    is_even = odd == 0

    links = Links(wide)
    order = links.order(width)
    gains = jnp.stack([gain_one, gain_two], axis=1)
    gains = jnp.pad(gains, ((0, 0), (0, 126)))
    pack_a = jnp.concatenate([w_qkv.astype(bf), gains.astype(bf)], axis=1)
    hid_order = w_hidden.astype(bf).reshape(shard, width, ratio).transpose(0, 2, 1)
    pack_b = jnp.concatenate(
        [
            w_attn_out.astype(bf),
            hid_order.reshape(shard, hidden),
            w_proj.astype(bf).reshape(shard, hidden),
        ],
        axis=1,
    )

    fill = jnp.full((2 * rows,), -1, jnp.int32)
    ids = jnp.concatenate([fill, segment_ids, fill])
    key_ids = lax.dynamic_slice_in_dim(ids, place * rows, window, 0)
    own_ids = lax.dynamic_slice_in_dim(segment_ids, place * rows, rows, 0)
    tiles = own_ids.reshape(rows // QT, QT)
    kseg = jnp.broadcast_to(key_ids[:, None], (window, QT))
    qseg = jnp.broadcast_to(tiles[:, None, :], (rows // QT, 8, QT))
    origin = (place - 2) * rows
    low = jnp.sum(segment_ids[None, :] < tiles[:, :1], axis=1, dtype=jnp.int32) - origin
    high = jnp.sum(segment_ids[None, :] <= tiles[:, -1:], axis=1, dtype=jnp.int32) - origin
    low = jnp.clip(low, 0, window)
    high = jnp.clip(high, 0, window)
    edges = jnp.arange(window // KT, dtype=jnp.int32)[:, None] * KT
    begin = jnp.sum(high[None, :] <= edges, axis=1, dtype=jnp.int32)
    end = jnp.sum(low[None, :] < edges + KT, axis=1, dtype=jnp.int32)
    span = jnp.stack([low[0] // KT, (high[-1] + KT - 1) // KT])
    scalars = (begin, end, span, odd.reshape(1))

    swap = [(0, 1), (1, 0)]
    up = [(j, j + 1) for j in range(wide - 1)]
    down = [(j + 1, j) for j in range(wide - 1)]
    across = [(2 * j, 2 * j + 2) for j in range(wide - 1)]
    across += [(2 * j + 3, 2 * j + 1) for j in range(wide - 1)]
    partner = lax.ppermute(joint_in, "narrow", swap)
    before = lax.ppermute(joint_in, "wide", up)
    behind = lax.ppermute(joint_in, "wide", down)
    mine_a = links.along_z(pack_a)
    fourth = lax.ppermute(partner, both, across)
    (mine_a,) = hold((mine_a,), order, kseg, qseg, *scalars)
    ones, twos = links.along_xy(mine_a)
    blocks = (before, partner, fourth, behind)
    (pack_b,) = hold((pack_b,), before, partner, behind, mine_a)
    full_b = lax.all_gather(pack_b, both, axis=0, tiled=True)

    weight, gains, a_win, k, v, q, o, lse = attend(
        scalars, blocks, kseg, joint_in, qseg, order, ones, twos
    )

    joint_out, hid_keep, hid_send, proj_keep, proj_send, out_keep, out_send, dx, do, gg_b = middle(
        joint_in, o, cotangent, gains, order, full_b
    )
    chain = Middle(links)
    keep_b, got_b = chain.first(
        (hid_keep, links.swap(hid_send, "core")),
        (proj_keep, links.swap(proj_send, "core")),
        (out_keep, links.swap(out_send, "core")),
    )
    args = (scalars, k, v, a_win, kseg, q, do, o, lse, qseg, weight)
    da_before, da_partner, da_fourth, da_behind, *partial = outer_back(*args, blocks, *keep_b)

    keep_b, got_b = chain.second(keep_b, got_b, da_before)
    home = [(2 * j + 2, 2 * j + 1) for j in range(wide - 1)]
    home += [(t, s) for s, t in home]
    others = (
        lax.ppermute(da_before, "wide", down),
        lax.ppermute(da_partner, "narrow", swap),
        lax.ppermute(da_fourth, both, home),
        lax.ppermute(da_behind, "wide", up),
    )
    da_own, keep_a, send_a = inner_back(*args, joint_in, order, gg_b, partial, *keep_b)

    keep_b, got_b = chain.third(keep_b, got_b, keep_a)
    da_own, send_a = settle(da_own, others, send_a, *keep_b)
    got_a = links.swap(send_a, "core")
    keep_a, got_a = links.first([(keep_a, got_a)])
    (gains,) = hold((gains,), *keep_a)
    grad_in = finish(joint_in, dx, da_own, gains)
    keep_a, got_a = links.second(keep_a, got_a, grad_in)
    keep_b, got_b = chain.fourth(keep_b, got_b, *keep_a)
    keep_a, got_a = links.third(keep_a, got_a, keep_b)
    keep_a, got_a = links.fourth(keep_a, got_a)
    sum_b = collect((keep_b, got_b), keep_a)

    rate = base_rate * jnp.power(jnp.float32(decay_rate), (11 - layer_index).astype(f32))
    rate = rate * jnp.power(1.0 - step_index.astype(f32) / total_steps, 0.9)
    sum_hid = sum_b[:, :hidden].reshape(shard, ratio, width).transpose(0, 2, 1)
    sum_hid = sum_hid.reshape(shard, hidden)
    far = hidden + width // 2
    sum_proj = sum_b[:, far:far + hidden].reshape(shard * ratio, width)
    step_out, step_hid, step_proj, next_out, next_hid, next_proj = update(
        rate, sum_b, sum_hid, sum_proj, mom_attn_out, mom_hidden, mom_proj
    )
    step_qkv, next_qkv, sum_gains = update_first(rate, keep_a, got_a, mom_qkv)
    next_g1 = momentum_rate * mom_gain_one + sum_gains[:, 0]
    next_g2 = momentum_rate * mom_gain_two + sum_gains[:, 1]
    return (
        joint_out,
        grad_in,
        rate * next_g1,
        step_qkv,
        step_out,
        rate * next_g2,
        step_hid,
        step_proj,
        next_g1,
        next_qkv,
        next_out,
        next_g2,
        next_hid,
        next_proj,
    )


def solution(mesh):
    split = P(("wide", "narrow"), None)
    line = P(("wide", "narrow"))
    params = (line, split, split, line, split, split)
    return jax.shard_map(
        body,
        mesh=mesh,
        in_specs=(split, split, P(), P(), P()) + params + params,
        out_specs=(split, split) + params + params,
        check_vma=False,
    )
```

profile of v0, /device:TPU:0, one launch (start us, length us, event | category | flops | bytes accessed | tf_op | source)
XLA Modules:
  0.0 378.9 jit_solution(10560390233399760471)
XLA Ops:
  9.7 4.0 %collective-permute-start.4 = (bf16[24,2432]{1,0:T(8,128)(2,1)}, bf16[24,2432]{1,0:T(8,128)(2,1)}, u32[]{:S(2)}, u32[]{:S(2)}) collective-permute-start(bf16[24,2432]{1,0:T(8,128)(2,1)} %pad_maximum_fusion.4), channel_id=1, source_target_pairs={{0,16},{2,18},{4,20},{6,22},{8,24},{10,26},{12,28},{14,30},{16,0},... | collective-permute-start | bytes 350216 | tf_op jit(solution)/shard_map/ppermute | solution.py:617
  13.7 1.6 collective-permute-start.5
  15.3 1.5 collective-permute-start.1
  16.8 1.3 collective-permute-start
  18.2 1.3 collective-permute-start.3
  19.6 1.4 fusion.refs_1_.refs_7_.order_ref
  22.0 1.2 copy.54
  23.1 1.6 copy.55
  24.8 1.0 convert_element_type.44
  26.8 1.3 convert_reduce_fusion
  31.6 4.1 %collective-permute-start.6 = (bf16[24,2432]{1,0:T(8,128)(2,1)}, bf16[24,2432]{1,0:T(8,128)(2,1)S(1)}, u32[]{:S(2)}, u32[]{:S(2)}) collective-permute-start(bf16[24,2432]{1,0:T(8,128)(2,1)} %pad_maximum_fusion.4), channel_id=1, source_target_pairs={{0,24},{2,26},{4,28},{6,30},{8,16},{10,18},{12,20},{14,22},{16,8},... | collective-permute-start | bytes 350216 | tf_op jit(solution)/shard_map/ppermute | solution.py:617
  36.9 1.9 collective-permute-done.6
  38.8 1.8 pad_maximum_fusion.1.refs_0_
  41.2 2.3 broadcast_in_dim.7.refs_2_.refs_4_.kseg_ref
  43.4 1.8 hold.3.refs_4_
  47.5 1.7 hold.4
  49.3 4.3 %collective-permute-start.7 = (bf16[96,1280]{1,0:T(8,128)(2,1)S(1)}, bf16[96,1280]{1,0:T(8,128)(2,1)S(1)}, u32[]{:S(2)}, u32[]{:S(2)}) collective-permute-start(bf16[96,1280]{1,0:T(8,128)(2,1)S(1)} %slice.40), channel_id=1, source_target_pairs={{0,4},{2,6},{4,0},{6,2},{8,12},{10,14},{12,8},{14,10},{16,20},{18,... | collective-permute-start | bytes 737288 | tf_op jit(solution)/shard_map/ppermute | solution.py:614
  54.1 4.4 %collective-permute-done.7 = bf16[96,1280]{1,0:T(8,128)(2,1)S(1)} collective-permute-done((bf16[96,1280]{1,0:T(8,128)(2,1)S(1)}, bf16[96,1280]{1,0:T(8,128)(2,1)S(1)}, u32[]{:S(2)}, u32[]{:S(2)}) %collective-permute-start.7) | collective-permute-done | bytes 245792 | tf_op jit(solution)/shard_map/ppermute | solution.py:614
  59.2 1.6 collective-permute-start.2
  61.0 1.7 collective-permute-start.12
  62.7 2.0 collective-permute-start.9
  64.7 7.8 %collective-permute-done.8.refs_9_ = bf16[192,1280]{1,0:T(8,128)(2,1)S(1)} collective-permute-done((bf16[192,1280]{1,0:T(8,128)(2,1)S(1)}, bf16[192,1280]{1,0:T(8,128)(2,1)S(1)}, u32[]{:S(2)}, u32[]{:S(2)}) %collective-permute-start.8) | collective-permute-done | bytes 491552 | tf_op jit(solution)/shard_map/ppermute | solution.py:612
  73.3 15.0 %collective-permute-start.14 = (bf16[192,1152]{1,0:T(8,128)(2,1)S(1)}, bf16[192,1152]{1,0:T(8,128)(2,1)S(1)}, u32[]{:S(2)}, u32[]{:S(2)}) collective-permute-start(bf16[192,1152]{1,0:T(8,128)(2,1)S(1)} %collective-permute-done.12.refs_13_), channel_id=1, source_target_pairs={{0,2},{2,0},{4,6},{6,4},{8,10},{10,8},{12,14},{14,12},{16,18},{18,... | collective-permute-start | bytes 1327112 | tf_op jit(solution)/shard_map/ppermute | solution.py:614
  88.3 1.4 collective-permute-done.14.refs_15_
  91.7 33.4 %attend.1 = (bf16[768,2432]{1,0:T(8,128)(2,1)}, f32[8,768]{1,0:T(8,128)}, bf16[3200,768]{1,0:T(8,128)(2,1)}, bf16[3200,768]{1,0:T(8,128)(2,1)}, bf16[3200,768]{1...) custom-call(s32[10]{0:T(128)} %convert_reduce_fusion.3.refs_4_.begin, ...), custom_call_target="tpu_custom_call" | custom-call | flops 1 | bytes 1 | tf_op jit(solution)/shard_map/attend/pallas_call | solution.py:221
  125.1 17.2 %all-gather.2.cloned.1.call-done.wo_ref.wh_ref.wp_ref = bf16[768,6912]{1,0:T(8,128)(2,1)} async-done(((bf16[24,6912]{1,0:T(8,128)(2,1)}), bf16[768,6912]{1,0:T(8,128)(2,1)}) %all-gather.2.cloned.1.call-update) | async-done | bytes 10616848 | tf_op jit(solution)/shard_map/all_gather | solution.py:1038
  143.0 36.3 %middle.1 = (bf16[640,768]{1,0:T(8,128)(2,1)}, bf16[384,3072]{1,0:T(8,128)(2,1)}, bf16[384,3072]{1,0:T(8,128)(2,1)}, bf16[384,3072]{1,0:T(8,128)(2,1)}, bf16[384...) custom-call(bf16[640,768]{1,0:T(8,128)(2,1)} %x_ref.5, ...), custom_call_target="tpu_custom_call" | custom-call | flops 1 | bytes 1 | tf_op jit(solution)/shard_map/middle/pallas_call | solution.py:573
  180.8 5.5 %collective-permute-done.17.outg_x.outg_y = bf16[384,768]{1,0:T(8,128)(2,1)S(1)} collective-permute-done((bf16[384,768]{1,0:T(8,128)(2,1)S(1)}, bf16[384,768]{1,0:T(8,128)(2,1)S(1)}, u32[]{:S(2)}, u32[]{:S(2)}) %collective-permute-start.17) | collective-permute-done | bytes 589856 | tf_op jit(solution)/shard_map/ppermute | solution.py:614
  186.3 2.7 collective-permute-done.16.projg
  189.0 1.4 copy-done.38
  190.5 7.3 %first.1 = (bf16[192,3456]{1,0:T(8,128)(2,1)}, bf16[192,3456]{1,0:T(8,128)(2,1)}, bf16[192,3456]{1,0:T(8,128)(2,1)}, bf16[192,3456]{1,0:T(8,128)(2,1)}) custom-call(bf16[384,3072]{1,0:T(8,128)(2,1)} %get-tuple-element.90.hidk, bf16[384,3072]{1,0:T(8,128)(2,1)} %copy-done.37, bf16[384,3072]{1,0:T(8,128)(2,1)} %get-tuple-element.92.projk, ...), custom_call_target="tpu_custom_call" | custom-call | flops 1 | bytes 1 | tf_op jit(solution)/shard_map/first/pallas_call | solution.py:754
  197.9 1.5 collective-permute-start.18
  199.3 3.5 collective-permute-start.19
  202.8 23.4 %outer_back.1 = (bf16[640,768]{1,0:T(8,128)(2,1)S(1)}, bf16[640,768]{1,0:T(8,128)(2,1)S(1)}, bf16[640,768]{1,0:T(8,128)(2,1)S(1)}, bf16[640,768]{1,0:T(8,128)(2,...) custom-call(s32[10]{0:T(128)S(1)} %copy-done.26, s32[10]{0:T(128)S(1)} %copy-done.24, ...), custom_call_target="tpu_custom_call" | custom-call | flops 1 | bytes 1 | tf_op jit(solution)/shard_map/outer_back/pallas_call | solution.py:450
  229.4 3.0 collective-permute-done.19.got_y
  232.4 1.5 stage.8
  234.0 15.2 %collective-permute-start.24 = (bf16[96,6912]{1,0:T(8,128)(2,1)}, bf16[96,6912]{1,0:T(8,128)(2,1)S(1)}, u32[]{:S(2)}, u32[]{:S(2)}) collective-permute-start(bf16[96,6912]{1,0:T(8,128)(2,1)} %get-tuple-element.111), channel_id=1, source_target_pairs={{0,8},{2,10},{4,12},{6,14},{8,0},{10,2},{12,4},{14,6},{16,24},{18,... | collective-permute-start | bytes 3981320 | tf_op jit(solution)/shard_map/ppermute | solution.py:617
  249.1 1.3 collective-permute-start.20
  250.4 9.3 %collective-permute-start.21 = (bf16[640,768]{1,0:T(8,128)(2,1)}, bf16[640,768]{1,0:T(8,128)(2,1)S(1)}, u32[]{:S(2)}, u32[]{:S(2)}) collective-permute-start(bf16[640,768]{1,0:T(8,128)(2,1)} %copy-done.29), channel_id=1, source_target_pairs={{0,1},{1,0},{2,3},{3,2},{4,5},{5,4},{6,7},{7,6},{8,9},{9,8},{10,11... | collective-permute-start | bytes 2949128 | tf_op jit(solution)/shard_map/ppermute | solution.py:1061
  260.5 4.0 %collective-permute-start.23 = (bf16[640,768]{1,0:T(8,128)(2,1)}, bf16[640,768]{1,0:T(8,128)(2,1)S(1)}, u32[]{:S(2)}, u32[]{:S(2)}) collective-permute-start(bf16[640,768]{1,0:T(8,128)(2,1)} %copy-done.27), channel_id=1, source_target_pairs={{0,2},{2,4},{4,6},{6,8},{8,10},{10,12},{12,14},{14,16},{16,18},{18... | collective-permute-start | bytes 2949128 | tf_op jit(solution)/shard_map/ppermute | solution.py:1063
  264.6 34.8 %inner_back.1 = (f32[640,768]{1,0:T(8,128)}, bf16[384,2432]{1,0:T(8,128)(2,1)}, bf16[384,2432]{1,0:T(8,128)(2,1)}) custom-call(s32[10]{0:T(128)S(1)} %copy-done.26, s32[10]{0:T(128)S(1)} %copy-done.24, s32[2]{0:T(128)S(1)} %copy-done.25, s32[1]{0:T(128)} %bitcast.7.refs_7_.odd, bf16[3200,768]{1,0:T(8,128)(2,1)} %get-tuple-element.82.k_ref, ...), custom_call_target="tpu_custom_call" | custom-call | flops 1 | bytes 1 | tf_op jit(solution)/shard_map/inner_back/pallas_call | solution.py:492
  299.4 1.5 copy-done.4
  300.9 1.0 stage.9
  303.8 1.3 copy-done.14
  305.4 3.5 collective-permute-done.25.refs_1_
  308.9 1.3 stage.10
  311.7 10.6 %collective-permute-start.26 = (bf16[192,1280]{1,0:T(8,128)(2,1)}, bf16[192,1280]{1,0:T(8,128)(2,1)S(1)}, u32[]{:S(2)}, u32[]{:S(2)}) collective-permute-start(bf16[192,1280]{1,0:T(8,128)(2,1)} %get-tuple-element.119), channel_id=1, source_target_pairs={{0,4},{2,6},{4,0},{6,2},{8,12},{10,14},{12,8},{14,10},{16,20},{18,... | collective-permute-start | bytes 1474568 | tf_op jit(solution)/shard_map/ppermute | solution.py:614
  322.4 1.8 collective-permute-start.27
  324.4 1.3 hold.5.gain_ref
  325.8 5.6 %finish.1.refs_0_ = bf16[640,768]{1,0:T(8,128)(2,1)} custom-call(bf16[640,768]{1,0:T(8,128)(2,1)} %x_ref.5, f32[640,768]{1,0:T(8,128)} %get-tuple-element.81.dx_ref, f32[640,768]{1,0:T(8,128)} %copy-done.14, f32[8,768]{1,0:T(8,128)} %hold.5.gain_ref), custom_call_target="tpu_custom_call" | custom-call | flops 1 | bytes 1 | tf_op jit(solution)/shard_map/finish/pallas_call | solution.py:876
  331.4 4.2 %collective-permute-done.27.got_y = bf16[192,1152]{1,0:T(8,128)(2,1)S(1)} collective-permute-done((bf16[192,1152]{1,0:T(8,128)(2,1)}, bf16[192,1152]{1,0:T(8,128)(2,1)S(1)}, u32[]{:S(2)}, u32[]{:S(2)}) %collective-permute-start.27) | collective-permute-done | bytes 442400 | tf_op jit(solution)/shard_map/ppermute | solution.py:612
  335.6 1.2 copy-done.11
  337.0 1.9 collective-permute-start.28
  338.9 1.0 collective-permute-start.29
  339.9 2.8 collective-permute-done.30.got_x
  342.9 1.1 collective-permute-start.34
  343.9 2.2 collective-permute-done.29.got_y
  347.2 1.7 collective-permute-start.32
  350.3 9.7 %collective-permute-done.32.got = bf16[48,2432]{1,0:T(8,128)(2,1)S(1)} collective-permute-done((bf16[48,2432]{1,0:T(8,128)(2,1)S(1)}, bf16[48,2432]{1,0:T(8,128)(2,1)S(1)}, u32[]{:S(2)}, u32[]{:S(2)}) %collective-permute-start.32) | collective-permute-done | bytes 233504 | tf_op jit(solution)/shard_map/ppermute | solution.py:617
  360.1 1.6 collective-permute-done.34.refs_1_
  362.7 1.2 copy.57.hid_ref
  364.7 2.6 update.1
  368.0 1.8 update_first.1
  369.8 1.0 slice_reduce_fusion
  (174 shorter events, 30.6 us)
Async XLA Ops:
  7.2 14.8 %copy-start.47 = (f32[24,3072]{1,0:T(8,128)S(1)}, f32[24,3072]{1,0:T(8,128)}, u32[]{:S(2)}) copy-start(f32[24,3072]{1,0:T(8,128)} %param.26) | copy-start | bytes 884740
  7.2 135.0 %all-gather.2.cloned.1.call-start = ((), (), s32[]{:S(2)}) async-start(), calls=%async_computation | async-start | bytes 10948608 | tf_op jit(solution)/shard_map/all_gather | solution.py:1038
  9.7 21.9 %collective-permute-start.4 = (bf16[24,2432]{1,0:T(8,128)(2,1)}, bf16[24,2432]{1,0:T(8,128)(2,1)}, u32[]{:S(2)}, u32[]{:S(2)}) collective-permute-start(bf16[24,2432]{1,0:T(8,128)(2,1)} %pad_maximum_fusion.4), channel_id=1, source_target_pairs={{0,16},{2,18},{4,20},{6,22},{8,24},{10,26},{12,28},{14,30},{16,0},... | collective-permute-start | bytes 350216 | tf_op jit(solution)/shard_map/ppermute | solution.py:617
  13.7 23.1 %collective-permute-start.5 = (bf16[24,2432]{1,0:T(8,128)(2,1)}, bf16[24,2432]{1,0:T(8,128)(2,1)}, u32[]{:S(2)}, u32[]{:S(2)}) collective-permute-start(bf16[24,2432]{1,0:T(8,128)(2,1)} %pad_maximum_fusion.4), channel_id=1, source_target_pairs={{0,8},{2,10},{4,12},{6,14},{8,0},{10,2},{12,4},{14,6},{16,24},{18,... | collective-permute-start | bytes 350216 | tf_op jit(solution)/shard_map/ppermute | solution.py:617
  15.3 30.0 %collective-permute-start.1 = (bf16[640,768]{1,0:T(8,128)(2,1)}, bf16[640,768]{1,0:T(8,128)(2,1)S(1)}, u32[]{:S(2)}, u32[]{:S(2)}) collective-permute-start(bf16[640,768]{1,0:T(8,128)(2,1)} %x_ref.5), channel_id=1, source_target_pairs={{0,1},{1,0},{2,3},{3,2},{4,5},{5,4},{6,7},{7,6},{8,9},{9,8},{10,11... | collective-permute-start | bytes 2949128 | tf_op jit(solution)/shard_map/ppermute | solution.py:1029
  16.8 28.4 %collective-permute-start = (bf16[640,768]{1,0:T(8,128)(2,1)}, bf16[640,768]{1,0:T(8,128)(2,1)S(1)}, u32[]{:S(2)}, u32[]{:S(2)}) collective-permute-start(bf16[640,768]{1,0:T(8,128)(2,1)} %x_ref.5), channel_id=1, source_target_pairs={{0,2},{2,4},{4,6},{6,8},{8,10},{10,12},{12,14},{14,16},{16,18},{18... | collective-permute-start | bytes 2949128 | tf_op jit(solution)/shard_map/ppermute | solution.py:1030
  18.2 27.1 %collective-permute-start.3 = (bf16[640,768]{1,0:T(8,128)(2,1)}, bf16[640,768]{1,0:T(8,128)(2,1)S(1)}, u32[]{:S(2)}, u32[]{:S(2)}) collective-permute-start(bf16[640,768]{1,0:T(8,128)(2,1)} %x_ref.5), channel_id=1, source_target_pairs={{2,0},{4,2},{6,4},{8,6},{10,8},{12,10},{14,12},{16,14},{18,16},{20... | collective-permute-start | bytes 2949128 | tf_op jit(solution)/shard_map/ppermute | solution.py:1031
  31.6 7.2 %collective-permute-start.6 = (bf16[24,2432]{1,0:T(8,128)(2,1)}, bf16[24,2432]{1,0:T(8,128)(2,1)S(1)}, u32[]{:S(2)}, u32[]{:S(2)}) collective-permute-start(bf16[24,2432]{1,0:T(8,128)(2,1)} %pad_maximum_fusion.4), channel_id=1, source_target_pairs={{0,24},{2,26},{4,28},{6,30},{8,16},{10,18},{12,20},{14,22},{16,8},... | collective-permute-start | bytes 350216 | tf_op jit(solution)/shard_map/ppermute | solution.py:617
  45.3 4.0 %copy-start.34 = (bf16[96,2432]{1,0:T(8,128)(2,1)S(1)}, bf16[96,2432]{1,0:T(8,128)(2,1)}, u32[]{:S(2)}) copy-start(bf16[96,2432]{1,0:T(8,128)(2,1)} %hold.3.refs_4_) | copy-start | bytes 1400836
  49.2 10.0 %copy-start.31 = (bf16[640,768]{1,0:T(8,128)(2,1)S(1)}, bf16[640,768]{1,0:T(8,128)(2,1)}, u32[]{:S(2)}) copy-start(bf16[640,768]{1,0:T(8,128)(2,1)} %copy-done.30) | copy-start | bytes 2949124
  49.3 9.3 %collective-permute-start.7 = (bf16[96,1280]{1,0:T(8,128)(2,1)S(1)}, bf16[96,1280]{1,0:T(8,128)(2,1)S(1)}, u32[]{:S(2)}, u32[]{:S(2)}) collective-permute-start(bf16[96,1280]{1,0:T(8,128)(2,1)S(1)} %slice.40), channel_id=1, source_target_pairs={{0,4},{2,6},{4,0},{6,2},{8,12},{10,14},{12,8},{14,10},{16,20},{18,... | collective-permute-start | bytes 737288 | tf_op jit(solution)/shard_map/ppermute | solution.py:614
  53.6 7.3 %collective-permute-start.11 = (bf16[96,1152]{1,0:T(8,128)(2,1)S(1)}, bf16[96,1152]{1,0:T(8,128)(2,1)S(1)}, u32[]{:S(2)}, u32[]{:S(2)}) collective-permute-start(bf16[96,1152]{1,0:T(8,128)(2,1)S(1)} %slice.41), channel_id=1, source_target_pairs={{0,1},{1,0},{2,3},{3,2},{4,5},{5,4},{6,7},{7,6},{8,9},{9,8},{10,11... | collective-permute-start | bytes 663560 | tf_op jit(solution)/shard_map/ppermute | solution.py:612
  58.6 31.1 %copy-start.39 = (bf16[192,1280]{1,0:T(8,128)(2,1)}, bf16[192,1280]{1,0:T(8,128)(2,1)S(1)}, u32[]{:S(2)}) copy-start(bf16[192,1280]{1,0:T(8,128)(2,1)S(1)} %pad_maximum_fusion.refs_8_) | copy-start | bytes 1474564
  58.6 13.8 %collective-permute-start.8 = (bf16[192,1280]{1,0:T(8,128)(2,1)S(1)}, bf16[192,1280]{1,0:T(8,128)(2,1)S(1)}, u32[]{:S(2)}, u32[]{:S(2)}) collective-permute-start(bf16[192,1280]{1,0:T(8,128)(2,1)S(1)} %pad_maximum_fusion.refs_8_), channel_id=1, source_target_pairs={{0,1},{1,0},{2,3},{3,2},{4,5},{5,4},{6,7},{7,6},{8,9},{9,8},{10,11... | collective-permute-start | bytes 1474568 | tf_op jit(solution)/shard_map/ppermute | solution.py:612
  59.2 30.5 %collective-permute-start.2 = (bf16[640,768]{1,0:T(8,128)(2,1)S(1)}, bf16[640,768]{1,0:T(8,128)(2,1)S(1)}, u32[]{:S(2)}, u32[]{:S(2)}) collective-permute-start(bf16[640,768]{1,0:T(8,128)(2,1)S(1)} %copy-done.31), channel_id=1, source_target_pairs={{0,2},{2,4},{4,6},{6,8},{8,10},{10,12},{12,14},{14,16},{16,18},{18... | collective-permute-start | bytes 2949128 | tf_op jit(solution)/shard_map/ppermute | solution.py:1033
  60.9 28.8 %copy-start.40 = (bf16[192,1152]{1,0:T(8,128)(2,1)}, bf16[192,1152]{1,0:T(8,128)(2,1)S(1)}, u32[]{:S(2)}) copy-start(bf16[192,1152]{1,0:T(8,128)(2,1)S(1)} %pad_maximum_fusion.2.refs_12_) | copy-start | bytes 1327108
  61.0 12.3 %collective-permute-start.12 = (bf16[192,1152]{1,0:T(8,128)(2,1)S(1)}, bf16[192,1152]{1,0:T(8,128)(2,1)S(1)}, u32[]{:S(2)}, u32[]{:S(2)}) collective-permute-start(bf16[192,1152]{1,0:T(8,128)(2,1)S(1)} %pad_maximum_fusion.2.refs_12_), channel_id=1, source_target_pairs={{0,4},{2,6},{4,0},{6,2},{8,12},{10,14},{12,8},{14,10},{16,20},{18,... | collective-permute-start | bytes 1327112 | tf_op jit(solution)/shard_map/ppermute | solution.py:614
  62.7 25.6 %collective-permute-start.9 = (bf16[192,1280]{1,0:T(8,128)(2,1)S(1)}, bf16[192,1280]{1,0:T(8,128)(2,1)S(1)}, u32[]{:S(2)}, u32[]{:S(2)}) collective-permute-start(bf16[192,1280]{1,0:T(8,128)(2,1)S(1)} %pad_maximum_fusion.refs_8_), channel_id=1, source_target_pairs={{0,2},{2,0},{4,6},{6,4},{8,10},{10,8},{12,14},{14,12},{16,18},{18,... | collective-permute-start | bytes 1474568 | tf_op jit(solution)/shard_map/ppermute | solution.py:614
  72.5 17.3 %copy-start.41 = (bf16[192,1280]{1,0:T(8,128)(2,1)}, bf16[192,1280]{1,0:T(8,128)(2,1)S(1)}, u32[]{:S(2)}) copy-start(bf16[192,1280]{1,0:T(8,128)(2,1)S(1)} %collective-permute-done.8.refs_9_) | copy-start | bytes 1474564
  72.5 17.3 %collective-permute-start.10 = (bf16[192,1280]{1,0:T(8,128)(2,1)S(1)}, bf16[192,1280]{1,0:T(8,128)(2,1)S(1)}, u32[]{:S(2)}, u32[]{:S(2)}) collective-permute-start(bf16[192,1280]{1,0:T(8,128)(2,1)S(1)} %collective-permute-done.8.refs_9_), channel_id=1, source_target_pairs={{0,2},{2,0},{4,6},{6,4},{8,10},{10,8},{12,14},{14,12},{16,18},{18,... | collective-permute-start | bytes 1474568 | tf_op jit(solution)/shard_map/ppermute | solution.py:614
  72.5 15.8 %collective-permute-start.13 = (bf16[192,1152]{1,0:T(8,128)(2,1)S(1)}, bf16[192,1152]{1,0:T(8,128)(2,1)S(1)}, u32[]{:S(2)}, u32[]{:S(2)}) collective-permute-start(bf16[192,1152]{1,0:T(8,128)(2,1)S(1)} %pad_maximum_fusion.2.refs_12_), channel_id=1, source_target_pairs={{0,2},{2,0},{4,6},{6,4},{8,10},{10,8},{12,14},{14,12},{16,18},{18,... | collective-permute-start | bytes 1327112 | tf_op jit(solution)/shard_map/ppermute | solution.py:614
  73.3 16.5 %copy-start.44 = (bf16[192,1152]{1,0:T(8,128)(2,1)}, bf16[192,1152]{1,0:T(8,128)(2,1)S(1)}, u32[]{:S(2)}) copy-start(bf16[192,1152]{1,0:T(8,128)(2,1)S(1)} %collective-permute-done.12.refs_13_) | copy-start | bytes 1327108
  73.3 16.5 %collective-permute-start.14 = (bf16[192,1152]{1,0:T(8,128)(2,1)S(1)}, bf16[192,1152]{1,0:T(8,128)(2,1)S(1)}, u32[]{:S(2)}, u32[]{:S(2)}) collective-permute-start(bf16[192,1152]{1,0:T(8,128)(2,1)S(1)} %collective-permute-done.12.refs_13_), channel_id=1, source_target_pairs={{0,2},{2,0},{4,6},{6,4},{8,10},{10,8},{12,14},{14,12},{16,18},{18,... | collective-permute-start | bytes 1327112 | tf_op jit(solution)/shard_map/ppermute | solution.py:614
  180.1 6.2 %collective-permute-start.15 = (bf16[384,3072]{1,0:T(8,128)(2,1)}, bf16[384,3072]{1,0:T(8,128)(2,1)S(1)}, u32[]{:S(2)}, u32[]{:S(2)}) collective-permute-start(bf16[384,3072]{1,0:T(8,128)(2,1)} %get-tuple-element.91), channel_id=1, source_target_pairs={{0,2},{2,0},{4,6},{6,4},{8,10},{10,8},{12,14},{14,12},{16,18},{18,... | collective-permute-start | bytes 7077896 | tf_op jit(solution)/shard_map/ppermute | solution.py:614
  180.3 8.7 %collective-permute-start.16 = (bf16[384,3072]{1,0:T(8,128)(2,1)}, bf16[384,3072]{1,0:T(8,128)(2,1)S(1)}, u32[]{:S(2)}, u32[]{:S(2)}) collective-permute-start(bf16[384,3072]{1,0:T(8,128)(2,1)} %get-tuple-element.93), channel_id=1, source_target_pairs={{0,2},{2,0},{4,6},{6,4},{8,10},{10,8},{12,14},{14,12},{16,18},{18,... | collective-permute-start | bytes 7077896 | tf_op jit(solution)/shard_map/ppermute | solution.py:614
  180.6 5.7 %collective-permute-start.17 = (bf16[384,768]{1,0:T(8,128)(2,1)S(1)}, bf16[384,768]{1,0:T(8,128)(2,1)S(1)}, u32[]{:S(2)}, u32[]{:S(2)}) collective-permute-start(bf16[384,768]{1,0:T(8,128)(2,1)S(1)} %get-tuple-element.95), channel_id=1, source_target_pairs={{0,2},{2,0},{4,6},{6,4},{8,10},{10,8},{12,14},{14,12},{16,18},{18,... | collective-permute-start | bytes 1769480 | tf_op jit(solution)/shard_map/ppermute | solution.py:614
  186.3 4.2 %copy-start.36 = (bf16[384,768]{1,0:T(8,128)(2,1)}, bf16[384,768]{1,0:T(8,128)(2,1)S(1)}, u32[]{:S(2)}) copy-start(bf16[384,768]{1,0:T(8,128)(2,1)S(1)} %collective-permute-done.17.outg_x.outg_y) | copy-start | bytes 1769476
  186.3 4.2 %copy-start.37 = (bf16[384,3072]{1,0:T(8,128)(2,1)}, bf16[384,3072]{1,0:T(8,128)(2,1)S(1)}, u32[]{:S(2)}) copy-start(bf16[384,3072]{1,0:T(8,128)(2,1)S(1)} %collective-permute-done.15.hidg) | copy-start | bytes 7077892
  190.5 12.3 %copy-start.20 = (s32[5,8,128]{2,1,0:T(8,128)S(1)}, s32[5,8,128]{2,1,0:T(8,128)}, u32[]{:S(2)}) copy-start(s32[5,8,128]{2,1,0:T(8,128)} %broadcast_in_dim.8.refs_3_.refs_6_.qseg_ref) | copy-start | bytes 61444
  190.5 12.3 %copy-start.22 = (f32[5,6,1,256]{3,2,1,0:T(1,128)S(1)}, f32[5,6,1,256]{3,2,1,0:T(1,128)}, u32[]{:S(2)}) copy-start(f32[5,6,1,256]{3,2,1,0:T(1,128)} %get-tuple-element.87.lse_ref) | copy-start | bytes 92164
  190.5 12.3 %copy-start.24 = (s32[10]{0:T(128)S(1)}, s32[10]{0:T(128)}, u32[]{:S(2)}) copy-start(s32[10]{0:T(128)} %convert_reduce_fusion.2.refs_5_.end) | copy-start | bytes 124
  190.5 12.3 %copy-start.25 = (s32[2]{0:T(128)S(1)}, s32[2]{0:T(128)}, u32[]{:S(2)}) copy-start(s32[2]{0:T(128)} %pad_add_fusion.refs_6_.span) | copy-start | bytes 28
  190.5 12.3 %copy-start.26 = (s32[10]{0:T(128)S(1)}, s32[10]{0:T(128)}, u32[]{:S(2)}) copy-start(s32[10]{0:T(128)} %convert_reduce_fusion.3.refs_4_.begin) | copy-start | bytes 124
  197.9 31.5 %collective-permute-start.18 = (bf16[192,3456]{1,0:T(8,128)(2,1)}, bf16[192,3456]{1,0:T(8,128)(2,1)S(1)}, u32[]{:S(2)}, u32[]{:S(2)}) collective-permute-start(bf16[192,3456]{1,0:T(8,128)(2,1)} %get-tuple-element.101), channel_id=1, source_target_pairs={{0,4},{2,6},{4,0},{6,2},{8,12},{10,14},{12,8},{14,10},{16,20},{18,... | collective-permute-start | bytes 3981320 | tf_op jit(solution)/shard_map/ppermute | solution.py:614
  199.3 33.0 %collective-permute-start.19 = (bf16[192,3456]{1,0:T(8,128)(2,1)}, bf16[192,3456]{1,0:T(8,128)(2,1)S(1)}, u32[]{:S(2)}, u32[]{:S(2)}) collective-permute-start(bf16[192,3456]{1,0:T(8,128)(2,1)} %get-tuple-element.102), channel_id=1, source_target_pairs={{0,1},{1,0},{2,3},{3,2},{4,5},{5,4},{6,7},{7,6},{8,9},{9,8},{10,11... | collective-permute-start | bytes 3981320 | tf_op jit(solution)/shard_map/ppermute | solution.py:612
  202.8 29.6 %copy-start.7 = (bf16[192,3456]{1,0:T(8,128)(2,1)S(1)}, bf16[192,3456]{1,0:T(8,128)(2,1)}, u32[]{:S(2)}) copy-start(bf16[192,3456]{1,0:T(8,128)(2,1)} %get-tuple-element.96.refs_0_.keep_x) | copy-start | bytes 3981316
  202.8 29.6 %copy-start.8 = (bf16[192,3456]{1,0:T(8,128)(2,1)S(1)}, bf16[192,3456]{1,0:T(8,128)(2,1)}, u32[]{:S(2)}) copy-start(bf16[192,3456]{1,0:T(8,128)(2,1)} %get-tuple-element.97.refs_1_.keep_y) | copy-start | bytes 3981316
  202.8 61.7 %copy-start.10 = (bf16[640,768]{1,0:T(8,128)(2,1)S(1)}, bf16[640,768]{1,0:T(8,128)(2,1)}, u32[]{:S(2)}) copy-start(bf16[640,768]{1,0:T(8,128)(2,1)} %get-tuple-element.86.do_ref) | copy-start | bytes 2949124
  232.4 32.1 %copy-start = (s32[3200,128]{1,0:T(8,128)S(1)}, s32[3200,128]{1,0:T(8,128)}, u32[]{:S(2)}) copy-start(s32[3200,128]{1,0:T(8,128)} %broadcast_in_dim.7.refs_2_.refs_4_.kseg_ref) | copy-start | bytes 4915204
  232.4 32.2 %copy-start.1 = (bf16[768,768]{1,0:T(8,128)(2,1)S(1)}, bf16[768,768]{1,0:T(8,128)(2,1)}, u32[]{:S(2)}) copy-start(bf16[768,768]{1,0:T(8,128)(2,1)} %fusion.refs_1_.refs_7_.order_ref) | copy-start | bytes 3538948
  232.4 32.2 %copy-start.2 = (bf16[640,768]{1,0:T(8,128)(2,1)S(1)}, bf16[640,768]{1,0:T(8,128)(2,1)}, u32[]{:S(2)}) copy-start(bf16[640,768]{1,0:T(8,128)(2,1)} %x_ref.5) | copy-start | bytes 2949124
  232.4 32.2 %copy-start.3 = (bf16[640,768]{1,0:T(8,128)(2,1)S(1)}, bf16[640,768]{1,0:T(8,128)(2,1)}, u32[]{:S(2)}) copy-start(bf16[640,768]{1,0:T(8,128)(2,1)} %get-tuple-element.78.o_ref) | copy-start | bytes 2949124
  232.4 32.2 %copy-start.9 = (bf16[640,768]{1,0:T(8,128)(2,1)S(1)}, bf16[640,768]{1,0:T(8,128)(2,1)}, u32[]{:S(2)}) copy-start(bf16[640,768]{1,0:T(8,128)(2,1)} %get-tuple-element.85.q_ref) | copy-start | bytes 2949124
  234.0 65.4 %collective-permute-start.24 = (bf16[96,6912]{1,0:T(8,128)(2,1)}, bf16[96,6912]{1,0:T(8,128)(2,1)S(1)}, u32[]{:S(2)}, u32[]{:S(2)}) collective-permute-start(bf16[96,6912]{1,0:T(8,128)(2,1)} %get-tuple-element.111), channel_id=1, source_target_pairs={{0,8},{2,10},{4,12},{6,14},{8,0},{10,2},{12,4},{14,6},{16,24},{18,... | collective-permute-start | bytes 3981320 | tf_op jit(solution)/shard_map/ppermute | solution.py:617
  249.1 52.7 %collective-permute-start.20 = (bf16[640,768]{1,0:T(8,128)(2,1)S(1)}, bf16[640,768]{1,0:T(8,128)(2,1)S(1)}, u32[]{:S(2)}, u32[]{:S(2)}) collective-permute-start(bf16[640,768]{1,0:T(8,128)(2,1)S(1)} %get-tuple-element.103.refs_0_), channel_id=1, source_target_pairs={{2,0},{4,2},{6,4},{8,6},{10,8},{12,10},{14,12},{16,14},{18,16},{20... | collective-permute-start | bytes 2949128 | tf_op jit(solution)/shard_map/ppermute | solution.py:1060
  250.4 51.4 %collective-permute-start.21 = (bf16[640,768]{1,0:T(8,128)(2,1)}, bf16[640,768]{1,0:T(8,128)(2,1)S(1)}, u32[]{:S(2)}, u32[]{:S(2)}) collective-permute-start(bf16[640,768]{1,0:T(8,128)(2,1)} %copy-done.29), channel_id=1, source_target_pairs={{0,1},{1,0},{2,3},{3,2},{4,5},{5,4},{6,7},{7,6},{8,9},{9,8},{10,11... | collective-permute-start | bytes 2949128 | tf_op jit(solution)/shard_map/ppermute | solution.py:1061
  259.8 42.1 %collective-permute-start.22 = (bf16[640,768]{1,0:T(8,128)(2,1)}, bf16[640,768]{1,0:T(8,128)(2,1)S(1)}, u32[]{:S(2)}, u32[]{:S(2)}) collective-permute-start(bf16[640,768]{1,0:T(8,128)(2,1)} %copy-done.28), channel_id=1, source_target_pairs={{2,1},{4,3},{6,5},{8,7},{10,9},{12,11},{14,13},{16,15},{18,17},{20... | collective-permute-start | bytes 2949128 | tf_op jit(solution)/shard_map/ppermute | solution.py:1062
  260.5 41.4 %collective-permute-start.23 = (bf16[640,768]{1,0:T(8,128)(2,1)}, bf16[640,768]{1,0:T(8,128)(2,1)S(1)}, u32[]{:S(2)}, u32[]{:S(2)}) collective-permute-start(bf16[640,768]{1,0:T(8,128)(2,1)} %copy-done.27), channel_id=1, source_target_pairs={{0,2},{2,4},{4,6},{6,8},{8,10},{10,12},{12,14},{14,16},{16,18},{18... | collective-permute-start | bytes 2949128 | tf_op jit(solution)/shard_map/ppermute | solution.py:1063
  303.1 5.8 %copy-start.5 = (bf16[384,2432]{1,0:T(8,128)(2,1)S(1)}, bf16[384,2432]{1,0:T(8,128)(2,1)}, u32[]{:S(2)}) copy-start(bf16[384,2432]{1,0:T(8,128)(2,1)} %get-tuple-element.112.refs_0_) | copy-start | bytes 5603332
  305.0 3.8 %collective-permute-start.25 = (bf16[384,2432]{1,0:T(8,128)(2,1)S(1)}, bf16[384,2432]{1,0:T(8,128)(2,1)S(1)}, u32[]{:S(2)}, u32[]{:S(2)}) collective-permute-start(bf16[384,2432]{1,0:T(8,128)(2,1)S(1)} %get-tuple-element.116), channel_id=1, source_target_pairs={{0,2},{2,0},{4,6},{6,4},{8,10},{10,8},{12,14},{14,12},{16,18},{18,... | collective-permute-start | bytes 5603336 | tf_op jit(solution)/shard_map/ppermute | solution.py:614
  311.7 23.9 %collective-permute-start.26 = (bf16[192,1280]{1,0:T(8,128)(2,1)}, bf16[192,1280]{1,0:T(8,128)(2,1)S(1)}, u32[]{:S(2)}, u32[]{:S(2)}) collective-permute-start(bf16[192,1280]{1,0:T(8,128)(2,1)} %get-tuple-element.119), channel_id=1, source_target_pairs={{0,4},{2,6},{4,0},{6,2},{8,12},{10,14},{12,8},{14,10},{16,20},{18,... | collective-permute-start | bytes 1474568 | tf_op jit(solution)/shard_map/ppermute | solution.py:614
  322.4 13.2 %collective-permute-start.27 = (bf16[192,1152]{1,0:T(8,128)(2,1)}, bf16[192,1152]{1,0:T(8,128)(2,1)S(1)}, u32[]{:S(2)}, u32[]{:S(2)}) collective-permute-start(bf16[192,1152]{1,0:T(8,128)(2,1)} %get-tuple-element.120), channel_id=1, source_target_pairs={{0,1},{1,0},{2,3},{3,2},{4,5},{5,4},{6,7},{7,6},{8,9},{9,8},{10,11... | collective-permute-start | bytes 1327112 | tf_op jit(solution)/shard_map/ppermute | solution.py:612
  324.2 18.5 %collective-permute-start.30 = (bf16[48,3456]{1,0:T(8,128)(2,1)}, bf16[48,3456]{1,0:T(8,128)(2,1)S(1)}, u32[]{:S(2)}, u32[]{:S(2)}) collective-permute-start(bf16[48,3456]{1,0:T(8,128)(2,1)} %get-tuple-element.125), channel_id=1, source_target_pairs={{0,1},{1,0},{2,3},{3,2},{4,5},{5,4},{6,7},{7,6},{8,9},{9,8},{10,11... | collective-permute-start | bytes 995336 | tf_op jit(solution)/shard_map/ppermute | solution.py:612
  324.4 18.3 %collective-permute-start.31 = (bf16[48,3456]{1,0:T(8,128)(2,1)S(1)}, bf16[48,3456]{1,0:T(8,128)(2,1)S(1)}, u32[]{:S(2)}, u32[]{:S(2)}) collective-permute-start(bf16[48,3456]{1,0:T(8,128)(2,1)S(1)} %get-tuple-element.126), channel_id=1, source_target_pairs={{0,4},{2,6},{4,0},{6,2},{8,12},{10,14},{12,8},{14,10},{16,20},{18,... | collective-permute-start | bytes 995336 | tf_op jit(solution)/shard_map/ppermute | solution.py:614
  325.7 9.9 %copy-start.16 = (bf16[192,1280]{1,0:T(8,128)(2,1)S(1)}, bf16[192,1280]{1,0:T(8,128)(2,1)}, u32[]{:S(2)}) copy-start(bf16[192,1280]{1,0:T(8,128)(2,1)} %copy-done.15) | copy-start | bytes 1474564
  325.7 9.9 %copy-start.19 = (bf16[192,1152]{1,0:T(8,128)(2,1)S(1)}, bf16[192,1152]{1,0:T(8,128)(2,1)}, u32[]{:S(2)}) copy-start(bf16[192,1152]{1,0:T(8,128)(2,1)} %copy-done.18) | copy-start | bytes 1327108
  337.0 10.1 %collective-permute-start.28 = (bf16[96,1280]{1,0:T(8,128)(2,1)S(1)}, bf16[96,1280]{1,0:T(8,128)(2,1)S(1)}, u32[]{:S(2)}, u32[]{:S(2)}) collective-permute-start(bf16[96,1280]{1,0:T(8,128)(2,1)S(1)} %get-tuple-element.123), channel_id=1, source_target_pairs={{0,1},{1,0},{2,3},{3,2},{4,5},{5,4},{6,7},{7,6},{8,9},{9,8},{10,11... | collective-permute-start | bytes 737288 | tf_op jit(solution)/shard_map/ppermute | solution.py:612
  338.9 7.2 %collective-permute-start.29 = (bf16[96,1152]{1,0:T(8,128)(2,1)S(1)}, bf16[96,1152]{1,0:T(8,128)(2,1)S(1)}, u32[]{:S(2)}, u32[]{:S(2)}) collective-permute-start(bf16[96,1152]{1,0:T(8,128)(2,1)S(1)} %get-tuple-element.124), channel_id=1, source_target_pairs={{0,4},{2,6},{4,0},{6,2},{8,12},{10,14},{12,8},{14,10},{16,20},{18,... | collective-permute-start | bytes 663560 | tf_op jit(solution)/shard_map/ppermute | solution.py:614
  342.9 18.8 %collective-permute-start.34 = (bf16[24,6912]{1,0:T(8,128)(2,1)S(1)}, bf16[24,6912]{1,0:T(8,128)(2,1)S(1)}, u32[]{:S(2)}, u32[]{:S(2)}) collective-permute-start(bf16[24,6912]{1,0:T(8,128)(2,1)S(1)} %get-tuple-element.134), channel_id=1, source_target_pairs={{0,16},{2,18},{4,20},{6,22},{8,24},{10,26},{12,28},{14,30},{16,0},... | collective-permute-start | bytes 995336 | tf_op jit(solution)/shard_map/ppermute | solution.py:617
  347.2 12.7 %collective-permute-start.32 = (bf16[48,2432]{1,0:T(8,128)(2,1)S(1)}, bf16[48,2432]{1,0:T(8,128)(2,1)S(1)}, u32[]{:S(2)}, u32[]{:S(2)}) collective-permute-start(bf16[48,2432]{1,0:T(8,128)(2,1)S(1)} %get-tuple-element.129), channel_id=1, source_target_pairs={{0,8},{2,10},{4,12},{6,14},{8,0},{10,2},{12,4},{14,6},{16,24},{18,... | collective-permute-start | bytes 700424 | tf_op jit(solution)/shard_map/ppermute | solution.py:617
  360.0 2.7 copy-start.21
  360.0 7.3 %collective-permute-start.33 = (bf16[24,2432]{1,0:T(8,128)(2,1)S(1)}, bf16[24,2432]{1,0:T(8,128)(2,1)S(1)}, u32[]{:S(2)}, u32[]{:S(2)}) collective-permute-start(bf16[24,2432]{1,0:T(8,128)(2,1)S(1)} %get-tuple-element.131), channel_id=1, source_target_pairs={{0,16},{2,18},{4,20},{6,22},{8,24},{10,26},{12,28},{14,30},{16,0},... | collective-permute-start | bytes 350216 | tf_op jit(solution)/shard_map/ppermute | solution.py:617
  362.7 8.1 %copy-start.49 = (f32[24]{0:T(128)S(1)}, f32[24]{0:T(128)}, u32[]{:S(2)}) copy-start(f32[24]{0:T(128)} %param.31) | copy-start | bytes 292
  363.9 7.4 %copy-start.50 = (f32[24]{0:T(128)S(1)}, f32[24]{0:T(128)}, u32[]{:S(2)}) copy-start(f32[24]{0:T(128)} %param.28) | copy-start | bytes 292
  (23 other events, 26.9 us)
Sparse Core Ops, SparseCore 0:
  49.4 92.8 all-gather.1
where the time goes:
time: 380 us; the launch traced here: 379 us
  Pallas kernels  155 us (41%)
  starting transfers between devices  95.2 us (25%)
  waiting for transfers between devices  69.4 us (18%)
  local copies, waits for them, and re-layouts  28.7 us (8%)
  between operations  17.2 us (5%)
  other arithmetic  13.2 us (3%)
    ppermute x14, starting transfers between devices, swap(): lax.ppermute(array, 'wide', [(j, j ^ flip) for j in range(self.wide)])  37.7 us
    pallas_call x1, Pallas kernels, middle(): pl.pallas_call(middle_kernel, grid=(ratio,), in_specs=[whole] * 5 + [pl.B...  36.3 us
    pallas_call x1, Pallas kernels, inner_back(): pl.pallas_call(functools.partial(inner_kernel, own=own), grid_spec=pltpu....  34.8 us
    pallas_call x1, Pallas kernels, attend(): pl.pallas_call(kernel, grid_spec=pltpu.PrefetchScalarGridSpec(num_scalar_...  33.4 us
    ppermute x7, starting transfers between devices, flip_z(): lax.ppermute(array, 'wide', [(j, j ^ 4 * s) for j in range(self.wide)])  27.7 us
    pallas_call x1, Pallas kernels, outer_back(): pl.pallas_call(functools.partial(outer_kernel, own=own), grid_spec=pltpu....  23.4 us
    ppermute x14, waiting for transfers between devices, swap(): lax.ppermute(array, 'wide', [(j, j ^ flip) for j in range(self.wide)])  20.3 us
    ppermute x6, waiting for transfers between devices, swap(): return lax.ppermute(array, 'narrow', [(0, 1), (1, 0)])  18.7 us
  transfers between devices with their start and end apart: 36, of which 17 were waited for; matrix products, arithmetic and copies ran while one was open for 5% of the time, Pallas kernels for 28%

commit v1 on v0

v1 whole, which is shorter than its diff:
```python
import functools

import jax
import jax.numpy as jnp
from jax import lax
from jax.experimental import pallas as pl
from jax.experimental.pallas import tpu as pltpu
from jax.sharding import PartitionSpec as P

HEAD = 64
PAIR = 2 * HEAD
QT = 128
OWN = 320
OUTER = 256
GROUP = 3
BRIEF = pl.CostEstimate(flops=1, bytes_accessed=1, transcendentals=0)

eps = 1e-06
base_rate = 0.01
decay_rate = 0.65
total_steps = 100000.0
momentum_rate = 0.9

bf = jnp.bfloat16
f32 = jnp.float32


def dot(left, right):
    return jnp.dot(left, right, preferred_element_type=f32)


def contract_rows(left, right):
    return lax.dot_general(
        left, right, (((0,), (0,)), ((), ())), preferred_element_type=f32
    )


def contract_cols(left, right):
    return lax.dot_general(
        left, right, (((1,), (1,)), ((), ())), preferred_element_type=f32
    )


def normalize_parts(values):
    centre = jnp.mean(values, axis=-1, keepdims=True)
    centred = values - centre
    inverse = lax.rsqrt(jnp.mean(centred * centred, axis=-1, keepdims=True) + eps)
    return (centred * inverse, inverse)


def normalize_back(grad_out, normed, inverse, gain):
    grad_normed = grad_out * gain
    inner = grad_normed - jnp.mean(grad_normed, axis=-1, keepdims=True)
    inner = inner - normed * jnp.mean(grad_normed * normed, axis=-1, keepdims=True)
    return inverse * inner


def diag_wide(block):
    row = lax.broadcasted_iota(jnp.int32, block.shape, 0)
    zero = jnp.zeros_like(block)
    return jnp.concatenate(
        [jnp.where(row < HEAD, block, zero), jnp.where(row >= HEAD, block, zero)], axis=1
    )


def diag_tall(block):
    col = lax.broadcasted_iota(jnp.int32, block.shape, 1)
    zero = jnp.zeros_like(block)
    return jnp.concatenate(
        [jnp.where(col < HEAD, block, zero), jnp.where(col >= HEAD, block, zero)], axis=0
    )


def tile_bias(segments, qseg_ref, t):
    bias = jnp.where(segments == qseg_ref[t, 0:1, :], 0.0, -1e30).astype(f32)
    return jnp.concatenate([bias, bias], axis=1)


def columns_of(pair):
    return slice(pair * PAIR, (pair + 1) * PAIR)


def block_starts(odd, size):
    return (0, (2 - odd) * size, (1 + odd) * size, 3 * size)


def pieces_of(tile, odd, refs, size):
    for part in range(OUTER // QT):
        at = tile * (OUTER // QT) + part
        for ref, start in zip(refs, block_starts(odd, size)):
            yield (at >= start) & (at < start + size), ref, at - start, part


def copy_rows(tile, odd, refs, size, out):
    for number, (here, _, _, part) in enumerate(pieces_of(tile, odd, refs[:4], size)):
        ref = refs[number]

        @pl.when(here)
        def _(ref=ref, part=part):
            out[part * QT:(part + 1) * QT, :] = ref[...]


def block_specs(width, size, key):
    def spec(part, number):
        def index(step, begin, end, span, odd, places):
            at = key(step) * (OUTER // QT) + part
            return (jnp.clip(at - block_starts(odd[0], size)[number], 0, size - 1), 0)

        return pl.BlockSpec((QT, width), index)

    return [spec(part, number) for part in range(OUTER // QT) for number in range(4)]


def in_pairs(first, last, visit):
    twos = (last - first) // 2

    def two(j, carry):
        visit([first + 2 * j, first + 2 * j + 1])
        return carry

    lax.fori_loop(0, twos, two, 0)

    @pl.when(first + 2 * twos < last)
    def _():
        visit([last - 1])


def attend_kernel(begin, end, span, odd, places, *refs, pieces):
    count = 4 * OUTER // QT
    blocks, (kseg_ref, oseg_ref, own_ref, qseg_ref, order_ref) = refs[:count], refs[count:count + 5]
    parts = refs[count + 5:count + 5 + 2 * pieces]
    (w_ref, gains_ref, ao_ref, ko_ref, vo_ref, a_ref, k_ref, v_ref, q_ref, o_ref, lse_ref,
     qbd, top, total, acc, x_ref, rel_ref) = refs[count + 5 + 2 * pieces:]
    step = pl.program_id(0)
    rows, width = own_ref.shape
    pairs = width // PAIR
    tiles = qseg_ref.shape[0]
    scale = HEAD ** (-0.5)

    def project(x):
        n, _ = normalize_parts(x.astype(f32))
        a = (n * gains_ref[0:1, :]).astype(bf)
        k = dot(a, w_ref[:, width:2 * width]).astype(bf)
        return a, k, dot(a, w_ref[:, 2 * width:3 * width]).astype(bf)

    def visit(queries, keys, values, segments):
        group = [(t, p) for t in queries for p in range(pairs)]
        bias = [tile_bias(segments, qseg_ref, t) for t in queries]
        scores = [
            dot(keys(columns_of(p)), qbd[t, p]) + bias[j // pairs] for j, (t, p) in enumerate(group)
        ]
        olds = [top[t, p:p + 1, :] for t, p in group]
        news = [jnp.maximum(old, jnp.max(s, axis=0, keepdims=True)) for old, s in zip(olds, scores)]
        expo = [jnp.exp(s - new) for s, new in zip(scores, news)]
        shrinks = [jnp.exp(old - new) for old, new in zip(olds, news)]
        sums = [
            total[t, p:p + 1, :] * shrink + jnp.sum(e, axis=0, keepdims=True)
            for (t, p), shrink, e in zip(group, shrinks, expo)
        ]
        gots = [
            contract_rows(values(columns_of(p)), e.astype(bf)) for (t, p), e in zip(group, expo)
        ]
        for (t, p), new, shrink, summed, got in zip(group, news, shrinks, sums, gots):
            top[t, p:p + 1, :] = new
            total[t, p:p + 1, :] = summed
            lo, mid, hi = p * PAIR, p * PAIR + HEAD, (p + 1) * PAIR
            acc[t, lo:mid, :] = acc[t, lo:mid, :] * shrink[:, :QT] + got[:HEAD, :QT]
            acc[t, mid:hi, :] = acc[t, mid:hi, :] * shrink[:, QT:] + got[HEAD:, QT:]

    @pl.when(step == 0)
    def _():
        size = parts[0].shape[0] // 2
        cut = parts[0].shape[1]
        shard = size // (places.shape[0] // 8)
        halves = (slice(0, cut), slice(cut, rel_ref.shape[1]))
        for j in range(pieces):
            for h in range(2):
                of = slice(h * size, (h + 1) * size)
                core, other = j // 2 * 4, j % 2
                for block, cols, part in (
                    (core + 2 * h + other, halves[0], parts[j]),
                    (core + 2 * other + h, halves[1], parts[pieces + j]),
                ):
                    value = part[of, :].astype(f32)
                    if shard % 8:
                        rel_ref[block * size:(block + 1) * size, cols] = value
                        continue
                    for z in range(size // shard):
                        to = pl.multiple_of(places[block * (size // shard) + z] * shard, 8)
                        rel_ref[pl.ds(to, shard), cols] = value[z * shard:(z + 1) * shard]
        if shard % 8:
            w_ref[...] = dot(order_ref[...], rel_ref[...].astype(bf)).astype(bf)
        else:
            w_ref[...] = rel_ref[...].astype(bf)
        gains_ref[...] = w_ref[:, 3 * width:].astype(f32).T[:8]
        a, k, v = project(own_ref[...])
        ao_ref[...] = a
        ko_ref[...] = k
        vo_ref[...] = v
        q = dot(a, w_ref[:, :width]).astype(bf)
        q_ref[...] = q
        q = q.astype(f32) * scale
        for t in range(tiles):
            for p in range(pairs):
                qbd[t, p] = diag_wide(q[t * QT:(t + 1) * QT, columns_of(p)].T.astype(bf))
        top[...] = jnp.full(top.shape, -1e30, f32)
        total[...] = jnp.zeros(total.shape, f32)
        acc[...] = jnp.zeros(acc.shape, f32)

        def own(h, carry):
            at = pl.ds(pl.multiple_of(h * OWN, OWN), OWN)
            in_pairs(
                begin[h], end[h],
                lambda ts: visit(
                    ts, lambda c: ko_ref[at, c], lambda c: vo_ref[at, c], oseg_ref[at, :]
                ),
            )
            return carry

        lax.fori_loop(0, rows // OWN, own, 0)

    number = step - 1 + rows // OWN

    @pl.when((step > 0) & (begin[number] < end[number]))
    def _():
        copy_rows(step - 1, odd[0], blocks, rows // QT, x_ref)
        a, k, v = project(x_ref[...])
        a_ref[...] = a
        k_ref[...] = k
        v_ref[...] = v
        in_pairs(
            begin[number], end[number],
            lambda ts: visit(ts, lambda c: k_ref[:, c], lambda c: v_ref[:, c], kseg_ref[...]),
        )

    @pl.when(step == pl.num_programs(0) - 1)
    def _():
        for t in range(tiles):
            for p in range(pairs):
                sums = total[t, p:p + 1, :]
                lse_ref[t, p] = top[t, p:p + 1, :] + jnp.log(sums)
                inv = 1.0 / sums
                lo, mid, hi = p * PAIR, p * PAIR + HEAD, (p + 1) * PAIR
                out = jnp.concatenate(
                    [acc[t, lo:mid, :] * inv[:, :QT], acc[t, mid:hi, :] * inv[:, QT:]], axis=0
                )
                o_ref[t * QT:(t + 1) * QT, lo:hi] = out.T.astype(bf)


def attend(scalars, blocks, kseg, oseg, x_own, qseg, order, ones, twos):
    rows, width = x_own.shape
    outer = 4 * rows
    tiles = rows // QT
    pairs = width // PAIR
    columns = ones[0].shape[1] + twos[0].shape[1]
    whole = pl.BlockSpec(memory_space=pltpu.VMEM)

    def at_used(step, begin, end, span, odd, places):
        return (jnp.clip(step - 1, span[0], span[1]), 0)

    tile = pl.BlockSpec((OUTER, width), at_used)
    own = jax.ShapeDtypeStruct((rows, width), bf)
    far = jax.ShapeDtypeStruct((outer, width), bf)
    return pl.pallas_call(
        functools.partial(attend_kernel, pieces=len(ones)),
        grid_spec=pltpu.PrefetchScalarGridSpec(
            num_scalar_prefetch=5,
            grid=(1 + outer // OUTER,),
            in_specs=block_specs(width, rows // QT, lambda step: step - 1)
            + [pl.BlockSpec((OUTER, QT), at_used)]
            + [whole] * (4 + 2 * len(ones)),
            out_specs=[whole] * 5 + [tile] * 3 + [whole] * 3,
            scratch_shapes=[
                pltpu.VMEM((tiles, pairs, PAIR, 2 * QT), bf),
                pltpu.VMEM((tiles, 8, 2 * QT), f32),
                pltpu.VMEM((tiles, 8, 2 * QT), f32),
                pltpu.VMEM((tiles, width, QT), f32),
                pltpu.VMEM((OUTER, width), bf),
                pltpu.VMEM((width, columns), f32),
            ],
        ),
        out_shape=[
            jax.ShapeDtypeStruct((width, columns), bf),
            jax.ShapeDtypeStruct((8, width), f32),
            own,
            own,
            own,
            far,
            far,
            far,
            own,
            own,
            jax.ShapeDtypeStruct((tiles, pairs, 1, 2 * QT), f32),
        ],
        compiler_params=pltpu.CompilerParams(vmem_limit_bytes=56 * 1024 * 1024),
        cost_estimate=BRIEF,
        name="attend",
    )(*scalars, *(blocks * (OUTER // QT)), kseg, oseg, x_own, qseg, order, *ones, *twos)


def back_tile(first, last, refs, scratch):
    k_ref, v_ref, kseg_ref, qseg_ref, lse_ref = refs
    qbd, dobd, qn, don, delta, dq_acc, dk_acc, dv_acc = scratch
    pairs = qbd.shape[1]
    dk_acc[...] = jnp.zeros(dk_acc.shape, f32)
    dv_acc[...] = jnp.zeros(dv_acc.shape, f32)

    def visit(t):
        bias = tile_bias(kseg_ref[...], qseg_ref, t)
        for base in range(0, pairs, GROUP):
            group = range(base, min(pairs, base + GROUP))
            keys = [k_ref[:, columns_of(p)] for p in group]
            scores = [dot(kp, qbd[t, p]) for kp, p in zip(keys, group)]
            dprobs = [dot(v_ref[:, columns_of(p)], dobd[t, p]) for p in group]
            probs = [jnp.exp(s + bias - lse_ref[t, p]) for s, p in zip(scores, group)]
            ds = [
                (pr * (dp - delta[t, p:p + 1, :])).astype(bf)
                for pr, dp, p in zip(probs, dprobs, group)
            ]
            got_v = [dot(pr.astype(bf), don[t, p]) for pr, p in zip(probs, group)]
            got_k = [dot(d, qn[t, p]) for d, p in zip(ds, group)]
            got_q = [contract_rows(kp, d) for kp, d in zip(keys, ds)]
            for i, p in enumerate(group):
                lo, mid, hi = p * PAIR, p * PAIR + HEAD, (p + 1) * PAIR
                dv_acc[:, lo:hi] += got_v[i]
                dk_acc[:, lo:hi] += got_k[i]
                dq_acc[t, lo:mid, :] += got_q[i][:HEAD, :QT]
                dq_acc[t, mid:hi, :] += got_q[i][HEAD:, QT:]

    def visits(ts):
        for t in ts:
            visit(t)

    in_pairs(first, last, visits)
    return dk_acc[...].astype(bf), dv_acc[...].astype(bf)


def back_prepare(q_ref, do_ref, o_ref, scratch):
    qbd, dobd, qn, don, delta = scratch
    tiles, pairs = qbd.shape[:2]
    scale = HEAD ** (-0.5)
    for t in range(tiles):
        at = slice(t * QT, (t + 1) * QT)
        for p in range(pairs):
            cols = columns_of(p)
            q = q_ref[at, cols].astype(f32) * scale
            do = do_ref[at, cols].astype(f32)
            do_t = do.T
            qbd[t, p] = diag_wide(q.T.astype(bf))
            dobd[t, p] = diag_wide(do_t.astype(bf))
            qn[t, p] = diag_tall(q.astype(bf))
            don[t, p] = diag_tall(do.astype(bf))
            both = do_t * o_ref[at, cols].astype(f32).T
            delta[t, p:p + 1, :QT] = jnp.sum(both[:HEAD], axis=0, keepdims=True)
            delta[t, p:p + 1, QT:] = jnp.sum(both[HEAD:], axis=0, keepdims=True)


def back_input(w_ref, *grads):
    width = w_ref.shape[0]
    total = 0.0
    for number, grad in grads:
        total += contract_cols(grad, w_ref[:, number * width:(number + 1) * width])
    return total


def back_weights(dk, dv, a, acc, lo):
    width = dk.shape[1]
    acc[:, lo:lo + width] += contract_rows(a, dk)
    acc[:, lo + width:lo + 2 * width] += contract_rows(a, dv)


def outer_kernel(begin, end, span, odd, places, k_ref, v_ref, a_ref, kseg_ref, q_ref, do_ref, o_ref,
                 lse_ref, qseg_ref, w_ref, *refs):
    da_refs = refs[-13:-9]
    acc_ref, dq_ref, qbd, dobd, qn, don, delta, dk_acc, dv_acc = refs[-9:]
    step = pl.program_id(0)
    size = q_ref.shape[0] // QT
    number = step + q_ref.shape[0] // OWN

    @pl.when(step == 0)
    def _():
        back_prepare(q_ref, do_ref, o_ref, (qbd, dobd, qn, don, delta))
        acc_ref[...] = jnp.zeros(acc_ref.shape, f32)
        dq_ref[...] = jnp.zeros(dq_ref.shape, f32)

    used = begin[number] < end[number]

    def put(value):
        for here, ref, at, part in pieces_of(step, odd[0], da_refs, size):
            @pl.when(here)
            def _(ref=ref, at=at, part=part):
                ref[pl.ds(pl.multiple_of(at * QT, QT), QT), :] = value[part * QT:(part + 1) * QT]

    @pl.when(used)
    def _():
        dk, dv = back_tile(
            begin[number], end[number], (k_ref, v_ref, kseg_ref, qseg_ref, lse_ref),
            (qbd, dobd, qn, don, delta, dq_ref, dk_acc, dv_acc),
        )
        back_weights(dk, dv, a_ref[...], acc_ref, 0)
        put(back_input(w_ref, (1, dk), (2, dv)).astype(bf))

    @pl.when(jnp.logical_not(used))
    def _():
        put(jnp.zeros(k_ref.shape, bf))


def inner_kernel(begin, end, span, odd, places, k_ref, v_ref, a_ref, kseg_ref, q_ref, do_ref, o_ref,
                 lse_ref, qseg_ref, order_ref, acc_in, dq_in, *refs):
    (dk_ref, dv_ref, dq_ref, keep_ref, send_ref, token_ref,
     qbd, dobd, qn, don, delta, dk_acc, dv_acc, acc, dq_acc, a_all) = refs[-16:]
    step = pl.program_id(0)
    width = k_ref.shape[1]
    half = width // 2
    tiles, pairs = qbd.shape[:2]

    @pl.when(step == 0)
    def _():
        back_prepare(q_ref, do_ref, o_ref, (qbd, dobd, qn, don, delta))
        token_ref[...] = jnp.zeros(token_ref.shape, f32)
        acc[:, width:3 * width] = acc_in[...]
        dq_acc[...] = dq_in[...]

    dk, dv = back_tile(
        begin[step], end[step], (k_ref, v_ref, kseg_ref, qseg_ref, lse_ref),
        (qbd, dobd, qn, don, delta, dq_acc, dk_acc, dv_acc),
    )
    dk_ref[...] = dk
    dv_ref[...] = dv
    back_weights(dk, dv, a_ref[...], acc, width)
    a_all[pl.ds(pl.multiple_of(step * OWN, OWN), OWN), :] = a_ref[...]

    @pl.when(step == pl.num_programs(0) - 1)
    def _():
        scale = HEAD ** (-0.5)
        for t in range(tiles):
            for p in range(pairs):
                cols = columns_of(p)
                dq_ref[t * QT:(t + 1) * QT, cols] = (dq_acc[t, cols, :] * scale).T.astype(bf)
        acc[:, :width] = contract_rows(a_all[...], dq_ref[...])
        blocks = places.shape[0]
        shard = width // blocks
        if shard % 8:
            both = contract_rows(order_ref[...], acc[...].astype(bf)).astype(bf)
            keep_ref[...] = both[:half]
            send_ref[...] = both[half:]
            return
        for j in range(0, blocks, 2):
            both = [
                acc[pl.ds(pl.multiple_of(places[j + i] * shard, 8), shard), :] for i in range(2)
            ]
            out, to = (keep_ref, j) if j < blocks // 2 else (send_ref, j - blocks // 2)
            out[to * shard:(to + 2) * shard, :] = jnp.concatenate(both, axis=0).astype(bf)


def back_specs(rows, width, tile_rows, at_key):
    tiles = rows // QT
    pairs = width // PAIR
    whole = pl.BlockSpec(memory_space=pltpu.VMEM)
    tile = pl.BlockSpec((tile_rows, width), at_key)
    specs = [tile, tile, tile, pl.BlockSpec((tile_rows, QT), at_key)] + [whole] * 5
    scratch = [
        pltpu.VMEM((tiles, pairs, PAIR, 2 * QT), bf),
        pltpu.VMEM((tiles, pairs, PAIR, 2 * QT), bf),
        pltpu.VMEM((tiles, pairs, 2 * QT, PAIR), bf),
        pltpu.VMEM((tiles, pairs, 2 * QT, PAIR), bf),
        pltpu.VMEM((tiles, 8, 2 * QT), f32),
        pltpu.VMEM((tile_rows, width), f32),
        pltpu.VMEM((tile_rows, width), f32),
    ]
    return specs, scratch, whole


def outer_back(scalars, k, v, a, kseg, q, do, o, lse, qseg, weight, *deps):
    rows, width = q.shape

    def at_key(step, begin, end, span, odd, places):
        return (jnp.clip(step, span[0], span[1]), 0)

    specs, scratch, whole = back_specs(rows, width, OUTER, at_key)
    return pl.pallas_call(
        outer_kernel,
        grid_spec=pltpu.PrefetchScalarGridSpec(
            num_scalar_prefetch=5,
            grid=(k.shape[0] // OUTER,),
            in_specs=specs + [whole] + [pl.BlockSpec(memory_space=pl.ANY)] * len(deps),
            out_specs=[whole] * 6,
            scratch_shapes=scratch,
        ),
        out_shape=[
            *[jax.ShapeDtypeStruct((rows, width), bf)] * 4,
            jax.ShapeDtypeStruct((width, 2 * width), f32),
            jax.ShapeDtypeStruct((rows // QT, width, QT), f32),
        ],
        compiler_params=pltpu.CompilerParams(vmem_limit_bytes=50 * 1024 * 1024),
        cost_estimate=BRIEF,
        name="outer_back",
    )(*scalars, k, v, a, kseg, q, do, o, lse, qseg, weight, *deps)


def inner_back(scalars, k, v, a, kseg, q, do, o, lse, qseg, order, partial, *deps):
    rows, width = q.shape
    half = width // 2
    specs, scratch, whole = back_specs(rows, width, OWN, lambda step, *_: (step, 0))
    scratch += [
        pltpu.VMEM((width, 3 * width), f32),
        pltpu.VMEM((rows // QT, width, QT), f32),
        pltpu.VMEM((rows, width), bf),
    ]
    own = jax.ShapeDtypeStruct((rows, width), bf)
    message = jax.ShapeDtypeStruct((half, 3 * width), bf)
    return pl.pallas_call(
        inner_kernel,
        grid_spec=pltpu.PrefetchScalarGridSpec(
            num_scalar_prefetch=5,
            grid=(rows // OWN,),
            in_specs=specs + [whole] * 3 + [pl.BlockSpec(memory_space=pl.ANY)] * len(deps),
            out_specs=[specs[0], specs[0], whole, whole, whole, whole],
            scratch_shapes=scratch,
        ),
        out_shape=[own, own, own, message, message, jax.ShapeDtypeStruct((8, 128), f32)],
        compiler_params=pltpu.CompilerParams(vmem_limit_bytes=46 * 1024 * 1024),
        cost_estimate=BRIEF,
        name="inner_back",
    )(*scalars, k, v, a, kseg, q, do, o, lse, qseg, order, *partial, *deps)


def middle_kernel(places, x_ref, o_ref, dz_ref, gain_ref, order_ref, wo_ref, wh_ref, wp_ref,
                  mid_ref, hid_ref, hkeep_ref, hsend_ref, pkeep_ref, psend_ref, okeep_ref, osend_ref,
                  dx_ref, do_ref, normed, inverse, second, ordered, dsec, grads):
    step = pl.program_id(0)
    width = x_ref.shape[1]
    half = width // 2

    @pl.when(step == 0)
    def _():
        value = x_ref[...].astype(f32) + dot(o_ref[...], wo_ref[...])
        mid_ref[...] = value
        n, r = normalize_parts(value)
        normed[...] = n
        inverse[...] = jnp.broadcast_to(r, inverse.shape)
        b = (n * gain_ref[1:2, :]).astype(bf)
        second[...] = b
        ordered[...] = dot(b, order_ref[...]).astype(bf)
        dsec[...] = jnp.zeros(dsec.shape, f32)

    dz = dz_ref[...]
    wh = wh_ref[...]
    wp = wp_ref[...]
    u = dot(second[...], wh)
    cdf = 0.5 * (1.0 + lax.erf(u * (0.5 ** 0.5)))
    pdf = jnp.exp(-0.5 * u * u) * 0.3989422804014327
    hid = (u * cdf).astype(bf)
    du = (contract_cols(dz, wp) * (cdf + u * pdf)).astype(bf)
    hid_ref[...] = hid

    def put(keep_ref, send_ref, grad):
        grad = grad.astype(bf)
        keep_ref[...] = grad[:half]
        send_ref[...] = grad[half:]

    def put_rows(keep_ref, send_ref, left, right):
        blocks = places.shape[0]
        shard = width // blocks
        if shard % 8:
            put(keep_ref, send_ref, contract_rows(dot(left, order_ref[...]).astype(bf), right))
            return
        grads[...] = contract_rows(left, right)
        for j in range(0, blocks, 2):
            both = [
                grads[pl.ds(pl.multiple_of(places[j + i] * shard, 8), shard), :] for i in range(2)
            ]
            out, to = (keep_ref, j) if j < blocks // 2 else (send_ref, j - blocks // 2)
            out[to * shard:(to + 2) * shard, :] = jnp.concatenate(both, axis=0).astype(bf)

    put(hkeep_ref, hsend_ref, contract_rows(ordered[...], du))
    put_rows(pkeep_ref, psend_ref, hid, dz)
    dsec[...] += contract_cols(du, wh)

    @pl.when(step == pl.num_programs(0) - 1)
    def _():
        n = normed[...]
        db = dsec[...]
        dx = dz.astype(f32) + normalize_back(db, n, inverse[:, 0:1], gain_ref[1:2, :])
        dx_ref[...] = dx
        dproj = dx.astype(bf)
        put_rows(okeep_ref, osend_ref, o_ref[...], dproj)
        do_ref[...] = contract_cols(dproj, wo_ref[...]).astype(bf)


def middle(places, x, o, dz, gains, order, packed):
    rows, width = x.shape
    ratio = (packed.shape[1] - width) // (2 * width)
    whole = pl.BlockSpec(memory_space=pltpu.VMEM)
    line = jax.ShapeDtypeStruct((rows, width), f32)
    low = jax.ShapeDtypeStruct((rows, width), bf)
    half = width // 2
    part = pl.BlockSpec((half, width), lambda s, *_: (0, s))
    message = jax.ShapeDtypeStruct((half, ratio * width), bf)
    small = jax.ShapeDtypeStruct((half, width), bf)
    return pl.pallas_call(
        middle_kernel,
        grid_spec=pltpu.PrefetchScalarGridSpec(
            num_scalar_prefetch=1,
            grid=(ratio,),
            in_specs=[whole] * 5
            + [
                pl.BlockSpec((width, width), lambda s, *_: (0, 0)),
                pl.BlockSpec((width, width), lambda s, *_: (0, 1 + s)),
                pl.BlockSpec((width, width), lambda s, *_: (0, 1 + ratio + s)),
            ],
            out_specs=[whole, pl.BlockSpec((rows, width), lambda s, *_: (0, s))]
            + [part] * 4
            + [whole] * 4,
            scratch_shapes=[
                pltpu.VMEM((rows, width), f32),
                pltpu.VMEM((rows, 128), f32),
                pltpu.VMEM((rows, width), bf),
                pltpu.VMEM((rows, width), bf),
                pltpu.VMEM((rows, width), f32),
                pltpu.VMEM((width, width), f32),
            ],
        ),
        out_shape=[line, jax.ShapeDtypeStruct((rows, ratio * width), bf)]
        + [message] * 4
        + [small, small, line, low],
        compiler_params=pltpu.CompilerParams(vmem_limit_bytes=52 * 1024 * 1024),
        cost_estimate=BRIEF,
        name="middle",
    )(places, x, o, dz, gains, order, packed, packed, packed)


def out_kernel(mid_ref, hid_ref, wp_ref, out_ref, acc):
    step = pl.program_id(0)

    @pl.when(step == 0)
    def _():
        acc[...] = mid_ref[...]

    acc[...] += dot(hid_ref[...], wp_ref[...])

    @pl.when(step == pl.num_programs(0) - 1)
    def _():
        out_ref[...] = acc[...].astype(bf)


def layer_out(mid, hid, packed):
    rows, width = mid.shape
    ratio = hid.shape[1] // width
    whole = pl.BlockSpec(memory_space=pltpu.VMEM)
    return pl.pallas_call(
        out_kernel,
        grid=(ratio,),
        in_specs=[
            whole,
            pl.BlockSpec((rows, width), lambda s: (0, s)),
            pl.BlockSpec((width, width), lambda s: (0, 1 + ratio + s)),
        ],
        out_specs=whole,
        out_shape=jax.ShapeDtypeStruct((rows, width), bf),
        scratch_shapes=[pltpu.VMEM((rows, width), f32)],
        compiler_params=pltpu.CompilerParams(vmem_limit_bytes=24 * 1024 * 1024),
        cost_estimate=BRIEF,
        name="layer_out",
    )(mid, hid, packed)


def add(*arrays):
    total = arrays[0].astype(f32)
    for array in arrays[1:]:
        total += array.astype(f32)
    return total


class Links:
    def __init__(self, wide):
        self.wide = wide
        self.outer = wide // 4

    def swap(self, array, name):
        if name == "y":
            return lax.ppermute(array, "narrow", [(0, 1), (1, 0)])
        flip = 1 if name == "core" else 2
        return lax.ppermute(array, "wide", [(j, j ^ flip) for j in range(self.wide)])

    def flip_z(self, array, s):
        return lax.ppermute(array, "wide", [(j, j ^ (4 * s)) for j in range(self.wide)])

    def distance(self, at):
        bits = self.outer.bit_length() - 1
        return sum(((at >> b) & 1) << (bits - 1 - b) for b in range(bits))

    def order(self, width):
        place = lax.axis_index("wide")
        count = 2 * self.wide
        rows = width // count
        at = jnp.arange(count, dtype=jnp.int32)
        z, at = self.distance(at % self.outer) ^ (place // 4), at // self.outer
        y, at = (at + lax.axis_index("narrow")) % 2, at // 2
        x, at = (at + place // 2) % 2, at // 2
        core = (at + place) % 2
        places = ((z * 2 + x) * 2 + core) * 2 + y
        source = (places[:, None] * rows + jnp.arange(rows, dtype=jnp.int32)[None, :]).reshape(width)
        matrix = (jnp.arange(width, dtype=jnp.int32)[:, None] == source[None, :]).astype(bf)
        return places, matrix

    def along_z(self, shard):
        parts = [shard] + [self.flip_z(shard, self.distance(j)) for j in range(1, self.outer)]
        return jnp.concatenate(parts, axis=0)

    def along_xy(self, mine):
        cut = halfway(mine)
        one, two = mine[:, :cut], mine[:, cut:]
        one = jnp.concatenate([one, self.swap(one, "x")], axis=0)
        two = jnp.concatenate([two, self.swap(two, "y")], axis=0)
        one = (one, self.swap(one, "y"))
        two = (two, self.swap(two, "x"))
        return (
            one + tuple(self.swap(piece, "core") for piece in one),
            two + tuple(self.swap(piece, "core") for piece in two),
        )

    def first(self, pairs, *deps):
        rows = pairs[0][0].shape[0] // 4
        cuts = [halfway(keep) for keep, _ in pairs]
        wide = [sum(cuts), sum(keep.shape[1] for keep, _ in pairs) - sum(cuts)]

        def kernel(*refs):
            count = 2 * len(pairs)
            keep_x, send_x, keep_y, send_y = refs[-4:]
            at = [0, 0]
            for keep, got, cut in zip(refs[0:count:2], refs[1:count:2], cuts):
                rest = keep.shape[1] - cut
                one, two = slice(0, cut), slice(cut, cut + rest)
                to = slice(at[0], at[0] + cut)
                keep_x[:, to] = add(keep[:2 * rows, one], got[:2 * rows, one]).astype(bf)
                send_x[:, to] = add(keep[2 * rows:, one], got[2 * rows:, one]).astype(bf)
                to = slice(at[1], at[1] + rest)
                for j, out in enumerate((keep_y, send_y, keep_y, send_y)):
                    of = slice(j * rows, (j + 1) * rows)
                    into = slice(j // 2 * rows, (j // 2 + 1) * rows)
                    out[into, to] = add(keep[of, two], got[of, two]).astype(bf)
                at = [at[0] + cut, at[1] + rest]

        shapes = [(2 * rows, wide[0])] * 2 + [(2 * rows, wide[1])] * 2
        keep_x, send_x, keep_y, send_y = stage(kernel, sum(pairs, ()), deps, shapes)
        return (keep_x, keep_y), (self.swap(send_x, "x"), self.swap(send_y, "y"))

    def second(self, keep, got, *deps):
        rows = keep[0].shape[0] // 2

        def kernel(keep_x, keep_y, got_x, got_y, *refs):
            for keep, got, hold, send in ((keep_x, got_x, *refs[-4:-2]), (keep_y, got_y, *refs[-2:])):
                hold[...] = add(keep[:rows], got[:rows]).astype(bf)
                send[...] = add(keep[rows:], got[rows:]).astype(bf)

        shapes = [(rows, keep[0].shape[1])] * 2 + [(rows, keep[1].shape[1])] * 2
        keep_x, send_x, keep_y, send_y = stage(kernel, keep + got, deps, shapes)
        return (keep_x, keep_y), (self.swap(send_x, "y"), self.swap(send_y, "x"))

    def third(self, keep, got, *deps):
        cut = keep[0].shape[1]
        rows = keep[0].shape[0] // 2

        def kernel(keep_x, keep_y, got_x, got_y, *refs):
            hold, send = refs[-2:]
            for cols, keep, got in ((slice(0, cut), keep_x, got_x), (slice(cut, None), keep_y, got_y)):
                hold[:, cols] = add(keep[:rows], got[:rows]).astype(bf)
                send[:, cols] = add(keep[rows:], got[rows:]).astype(bf)

        hold, send = stage(kernel, keep + got, deps, [(rows, cut + keep[1].shape[1])] * 2)
        return hold, self.flip_z(send, 1)

    def fourth(self, keep, got, *deps):
        for bit in range(1, self.outer.bit_length() - 1):
            rows = keep.shape[0] // 2
            if rows % 8:
                total = add(keep, got).astype(bf)
                keep, send = total[:rows], total[rows:]
            else:
                keep, send = stage(halves_kernel, (keep, got), deps, [(rows, keep.shape[1])] * 2)
            got = self.flip_z(send, 1 << bit)
        return keep, got


def halves_kernel(keep, got, *refs):
    hold, send = refs[-2:]
    total = add(keep[...], got[...])
    hold[...] = total[:hold.shape[0]].astype(bf)
    send[...] = total[hold.shape[0]:].astype(bf)


def first_kernel(hidk, hidg, projk, projg, outk_x, outg_x, outk_y, outg_y, *refs):
    keep_x, send_x, keep_y, send_y = refs[-4:]
    rows = hidk.shape[0] // 4
    last = pl.num_programs(0) - 1

    def write(one, two):
        cols = slice(0, one[0].shape[1])
        keep_x[:, cols] = add(*(v[:2 * rows, :] for v in one)).astype(bf)
        send_x[:, cols] = add(*(v[2 * rows:, :] for v in one)).astype(bf)
        for j, out in enumerate((keep_y, send_y, keep_y, send_y)):
            of = slice(j * rows, (j + 1) * rows)
            out[j // 2 * rows:(j // 2 + 1) * rows, cols] = add(*(v[of, :] for v in two)).astype(bf)

    @pl.when(pl.program_id(0) < last)
    def _():
        write((hidk, hidg), (projk, projg))

    @pl.when(pl.program_id(0) == last)
    def _():
        write((outk_x, outg_x), (outk_y, outg_y))


class Middle:
    def __init__(self, links):
        self.links = links

    def first(self, hid, proj, out, *deps):
        rows, columns = hid[0].shape
        block = out[0].shape[1]
        steps = columns // block
        tile = pl.BlockSpec((rows, block), lambda j: (0, jnp.minimum(j, steps - 1)))
        half = [pl.BlockSpec((rows, block // 2), lambda j, at=at: (0, at)) for at in range(2)]
        shape = jax.ShapeDtypeStruct((rows // 2, columns + block // 2), bf)
        keep_x, send_x, keep_y, send_y = pl.pallas_call(
            first_kernel,
            grid=(steps + 1,),
            in_specs=[tile] * 4
            + [half[0]] * 2
            + [half[1]] * 2
            + [pl.BlockSpec(memory_space=pl.ANY)] * len(deps),
            out_specs=[pl.BlockSpec((rows // 2, block), lambda j: (0, j))] * 4,
            out_shape=[shape] * 4,
            cost_estimate=BRIEF,
            name="first",
        )(*hid, *proj, *out, *out, *deps)
        return (keep_x, keep_y), (self.links.swap(send_x, "x"), self.links.swap(send_y, "y"))

    def second(self, keep, got, *deps):
        rows = keep[0].shape[0] // 4
        cut = keep[0].shape[1]

        def kernel(keep_x, keep_y, got_x, got_y, *refs):
            hold_x, hold_y, send = refs[-3:]
            halves = ((hold_x, slice(0, cut), keep_x, got_x), (hold_y, slice(cut, None), keep_y, got_y))
            for hold, cols, keep, got in halves:
                for j in range(2):
                    into = slice(j * rows, (j + 1) * rows)
                    of = slice(2 * j * rows, (2 * j + 1) * rows)
                    hold[into, :] = add(keep[of, :], got[of, :]).astype(bf)
                    of = slice((2 * j + 1) * rows, (2 * j + 2) * rows)
                    send[into, cols] = add(keep[of, :], got[of, :]).astype(bf)

        wide = keep[1].shape[1]
        shapes = [(2 * rows, cut), (2 * rows, wide), (2 * rows, cut + wide)]
        hold_x, hold_y, send = stage(kernel, keep + got, deps, shapes)
        return (hold_x, hold_y), self.links.flip_z(send, 1)

    def third(self, keep, got, *deps):
        rows = keep[0].shape[0] // 2
        cut = keep[0].shape[1]

        def kernel(keep_x, keep_y, got, *refs):
            for keep, cols, hold, send in (
                (keep_x, slice(0, cut), *refs[-4:-2]), (keep_y, slice(cut, None), *refs[-2:])
            ):
                hold[...] = add(keep[:rows, :], got[:rows, cols]).astype(bf)
                send[...] = add(keep[rows:, :], got[rows:, cols]).astype(bf)

        shapes = [(rows, cut)] * 2 + [(rows, keep[1].shape[1])] * 2
        hold_x, send_x, hold_y, send_y = stage(kernel, keep + (got,), deps, shapes)
        return (hold_x, hold_y), (self.links.swap(send_x, "y"), self.links.swap(send_y, "x"))

    def fourth(self, keep, got, *deps):
        rows = keep[0].shape[0] // 2
        cut = keep[0].shape[1]
        if rows % 8:
            total = jnp.concatenate([add(k, g).astype(bf) for k, g in zip(keep, got)], axis=1)
            hold, send = total[:rows], total[rows:]
        else:
            def kernel(keep_x, keep_y, got_x, got_y, *refs):
                hold, send = refs[-2:]
                for cols, keep, got in ((slice(0, cut), keep_x, got_x), (slice(cut, None), keep_y, got_y)):
                    total = add(keep[...], got[...])
                    hold[:, cols] = total[:rows].astype(bf)
                    send[:, cols] = total[rows:].astype(bf)

            hold, send = stage(kernel, keep + got, deps, [(rows, cut + keep[1].shape[1])] * 2)
        got = self.links.flip_z(send, 2)
        for bit in range(2, self.links.outer.bit_length() - 1):
            total = add(hold, got).astype(bf)
            rows = rows // 2
            hold, send = total[:rows], total[rows:]
            got = self.links.flip_z(send, 1 << bit)
        return hold, got


def collect(parts, *deps):
    def kernel(*refs):
        refs[-1][...] = add(*(ref[...] for ref in refs[:len(parts)]))

    return stage(kernel, parts, deps, [parts[0].shape], f32)[0]


def stage(kernel, operands, deps, shapes, kind=bf):
    whole = pl.BlockSpec(memory_space=pltpu.VMEM)
    elsewhere = pl.BlockSpec(memory_space=pl.ANY)
    return pl.pallas_call(
        kernel,
        in_specs=[whole] * len(operands) + [elsewhere] * len(deps),
        out_specs=[whole] * len(shapes),
        out_shape=[jax.ShapeDtypeStruct(shape, kind) for shape in shapes],
        compiler_params=pltpu.CompilerParams(vmem_limit_bytes=24 * 1024 * 1024),
        cost_estimate=BRIEF,
        name="stage",
    )(*operands, *deps)


def hold(values, *deps):
    count = len(values)
    elsewhere = pl.BlockSpec(memory_space=pl.ANY)
    return pl.pallas_call(
        lambda *refs: None,
        in_specs=[elsewhere] * (count + len(deps)),
        out_specs=[elsewhere] * count,
        out_shape=[jax.ShapeDtypeStruct(v.shape, v.dtype) for v in values],
        input_output_aliases={j: j for j in range(count)},
        cost_estimate=BRIEF,
        name="hold",
    )(*values, *deps)


def halfway(array):
    return (array.shape[1] // 2 + 127) // 128 * 128


def share_kernel(dq_ref, dk_ref, dv_ref, w_ref, *refs):
    refs[-1][...] = back_input(w_ref, (0, dq_ref[...]), (1, dk_ref[...]), (2, dv_ref[...]))


def own_share(own, weight, *deps):
    rows, width = own[0].shape
    tile = pl.BlockSpec((OWN, width), lambda i: (i, 0))
    return pl.pallas_call(
        share_kernel,
        grid=(rows // OWN,),
        in_specs=[tile] * 3
        + [pl.BlockSpec(memory_space=pltpu.VMEM)]
        + [pl.BlockSpec(memory_space=pl.ANY)] * len(deps),
        out_specs=tile,
        out_shape=jax.ShapeDtypeStruct((rows, width), f32),
        compiler_params=pltpu.CompilerParams(vmem_limit_bytes=58 * 1024 * 1024),
        cost_estimate=BRIEF,
        name="own_share",
    )(*own, weight, *deps)


def finish_kernel(x_ref, dx_ref, own_ref, b0, b1, b2, b3, gain_ref, out_ref):
    n, r = normalize_parts(x_ref[...].astype(f32))
    da = add(own_ref[...], b0[...], b1[...], b2[...], b3[...])
    out_ref[...] = (dx_ref[...] + normalize_back(da, n, r, gain_ref[0:1, :])).astype(bf)


def finish(x, dx, own, others, gains):
    rows, width = x.shape
    tile = pl.BlockSpec((OWN, width), lambda i: (i, 0))
    return pl.pallas_call(
        finish_kernel,
        grid=(rows // OWN,),
        in_specs=[tile] * 7 + [pl.BlockSpec(gains.shape, lambda i: (0, 0))],
        out_specs=tile,
        out_shape=jax.ShapeDtypeStruct((rows, width), bf),
        compiler_params=pltpu.CompilerParams(vmem_limit_bytes=58 * 1024 * 1024),
        cost_estimate=BRIEF,
        name="finish",
    )(x, dx, own, *others, gains)


def gain_sums(w_ref, grad, shape):
    product = w_ref[...].astype(bf).astype(f32) * grad
    return jnp.broadcast_to(jnp.sum(product, axis=1, keepdims=True), shape)


def update_kernel(rate_ref, sum_ref, hid_ref, proj_ref, w_ref, mom_out, mom_hid, mom_proj,
                  step_out, step_hid, step_proj, next_out, next_hid, next_proj, gain_ref):
    rate = rate_ref[0]
    hidden = hid_ref.shape[1]
    width = mom_out.shape[1]
    half = width // 2
    far = hidden + half

    def put(step, following, at, momentum, grad):
        value = momentum_rate * momentum + grad
        following[at] = value
        step[at] = rate * value

    gain_ref[...] = gain_sums(w_ref, hid_ref[...], gain_ref.shape)
    whole = slice(None)
    put(step_hid, next_hid, (whole, whole), mom_hid[...], hid_ref[...])
    for at, lo in ((slice(0, half), hidden), (slice(half, width), far + hidden)):
        put(step_out, next_out, (whole, at), mom_out[:, at], sum_ref[:, lo:lo + half])
    put(step_proj, next_proj, (whole, whole), mom_proj[...], proj_ref[...])


def update(rate, total, hid, proj, w_hid, mom_out, mom_hid, mom_proj):
    whole = pl.BlockSpec(memory_space=pltpu.VMEM)
    moms = (mom_out, mom_hid, mom_proj)
    return pl.pallas_call(
        update_kernel,
        in_specs=[pl.BlockSpec(memory_space=pltpu.SMEM)] + [whole] * 7,
        out_specs=[whole] * 7,
        out_shape=[jax.ShapeDtypeStruct(m.shape, f32) for m in moms + moms]
        + [jax.ShapeDtypeStruct((hid.shape[0], 128), f32)],
        cost_estimate=BRIEF,
        name="update",
    )(rate, total, hid, proj, w_hid, *moms)


def update_first_kernel(rate_ref, keep_ref, got_ref, w_ref, mom_ref, step_ref, next_ref, gain_ref):
    total = add(keep_ref[...], got_ref[...])
    gain_ref[...] = gain_sums(w_ref, total, gain_ref.shape)
    value = momentum_rate * mom_ref[...] + total
    next_ref[...] = value
    step_ref[...] = rate_ref[0] * value


def update_first(rate, keep, got, weight, mom):
    whole = pl.BlockSpec(memory_space=pltpu.VMEM)
    return pl.pallas_call(
        update_first_kernel,
        in_specs=[pl.BlockSpec(memory_space=pltpu.SMEM)] + [whole] * 4,
        out_specs=[whole] * 3,
        out_shape=[jax.ShapeDtypeStruct(mom.shape, f32)] * 2
        + [jax.ShapeDtypeStruct((mom.shape[0], 128), f32)],
        cost_estimate=BRIEF,
        name="update_first",
    )(rate, keep, got, weight, mom)


def body(
    joint_in,
    cotangent,
    segment_ids,
    layer_index,
    step_index,
    gain_one,
    w_qkv,
    w_attn_out,
    gain_two,
    w_hidden,
    w_proj,
    mom_gain_one,
    mom_qkv,
    mom_attn_out,
    mom_gain_two,
    mom_hidden,
    mom_proj,
):
    rows, width = joint_in.shape
    wide = lax.axis_size("wide")
    both = ("wide", "narrow")
    shard = w_qkv.shape[0]
    hidden = w_hidden.shape[1]
    ratio = hidden // width
    odd = lax.axis_index("narrow")
    place = lax.axis_index("wide") * 2 + odd
    window = 5 * rows
    is_even = odd == 0

    links = Links(wide)
    places, order = links.order(width)
    gains = jnp.stack([gain_one, gain_two], axis=1)
    gains = jnp.pad(gains, ((0, 0), (0, 126)))
    pack_a = jnp.concatenate([w_qkv.astype(bf), gains.astype(bf)], axis=1)
    hid_order = w_hidden.astype(bf).reshape(shard, width, ratio).transpose(0, 2, 1)
    pack_b = jnp.concatenate(
        [
            w_attn_out.astype(bf),
            hid_order.reshape(shard, hidden),
            w_proj.astype(bf).reshape(shard, hidden),
        ],
        axis=1,
    )

    fill = jnp.full((2 * rows,), -1, jnp.int32)
    ids = jnp.concatenate([fill, segment_ids, fill])
    key_ids = lax.dynamic_slice_in_dim(ids, place * rows, window, 0)
    own_ids = lax.dynamic_slice_in_dim(segment_ids, place * rows, rows, 0)
    tiles = own_ids.reshape(rows // QT, QT)
    far_ids = jnp.concatenate([key_ids[:2 * rows], key_ids[3 * rows:]])
    kseg = jnp.broadcast_to(far_ids[:, None], (4 * rows, QT))
    oseg = jnp.broadcast_to(own_ids[:, None], (rows, QT))
    qseg = jnp.broadcast_to(tiles[:, None, :], (rows // QT, 8, QT))
    origin = (place - 2) * rows
    low = jnp.sum(segment_ids[None, :] < tiles[:, :1], axis=1, dtype=jnp.int32) - origin
    high = jnp.sum(segment_ids[None, :] <= tiles[:, -1:], axis=1, dtype=jnp.int32) - origin
    low = jnp.clip(low, 0, window)
    high = jnp.clip(high, 0, window)
    side = 2 * rows // OUTER
    starts = [2 * rows + j * OWN for j in range(rows // OWN)]
    starts += [j * OUTER for j in range(side)] + [3 * rows + j * OUTER for j in range(side)]
    sizes = [OWN] * (rows // OWN) + [OUTER] * (2 * side)
    edges = jnp.asarray(starts, jnp.int32)[:, None]
    tops = jnp.asarray([at + size for at, size in zip(starts, sizes)], jnp.int32)[:, None]
    begin = jnp.sum(high[None, :] <= edges, axis=1, dtype=jnp.int32)
    end = jnp.sum(low[None, :] < tops, axis=1, dtype=jnp.int32)
    near = jnp.minimum(low[0] // OUTER, side)
    last = side - 1 + jnp.maximum(high[-1] - 3 * rows + OUTER - 1, 0) // OUTER
    span = jnp.stack([near, jnp.maximum(last, near)])
    scalars = (begin, end, span, odd.reshape(1), places)

    swap = [(0, 1), (1, 0)]
    up = [(j, j + 1) for j in range(wide - 1)]
    down = [(j + 1, j) for j in range(wide - 1)]
    across = [(2 * j, 2 * j + 2) for j in range(wide - 1)]
    across += [(2 * j + 3, 2 * j + 1) for j in range(wide - 1)]
    partner = lax.ppermute(joint_in, "narrow", swap)
    before = lax.ppermute(joint_in, "wide", up)
    behind = lax.ppermute(joint_in, "wide", down)
    mine_a = links.along_z(pack_a)
    fourth = lax.ppermute(partner, both, across)
    ones, twos = links.along_xy(mine_a)
    blocks = (before, partner, fourth, behind)
    (pack_b,) = hold((pack_b,), before, partner, behind, mine_a)
    full_b = lax.all_gather(pack_b, both, axis=0, tiled=True)

    weight, gains, a_own, k_own, v_own, a_far, k_far, v_far, q, o, lse = attend(
        scalars, blocks, kseg, oseg, joint_in, qseg, order, ones, twos
    )

    mid, hid, hid_keep, hid_send, proj_keep, proj_send, out_keep, out_send, dx, do = middle(
        places, joint_in, o, cotangent, gains, order, full_b
    )
    joint_out = layer_out(mid, hid, full_b)
    chain = Middle(links)
    keep_b, got_b = chain.first(
        (hid_keep, links.swap(hid_send, "core")),
        (proj_keep, links.swap(proj_send, "core")),
        (out_keep, links.swap(out_send, "core")),
        joint_out,
    )
    args = (q, do, o, lse, qseg)
    da_before, da_partner, da_fourth, da_behind, *partial = outer_back(
        scalars, k_far, v_far, a_far, kseg, *args, weight, *keep_b
    )

    keep_b, got_b = chain.second(keep_b, got_b, da_before)
    home = [(2 * j + 2, 2 * j + 1) for j in range(wide - 1)]
    home += [(t, s) for s, t in home]
    others = (
        lax.ppermute(da_before, "wide", down),
        lax.ppermute(da_partner, "narrow", swap),
        lax.ppermute(da_fourth, both, home),
        lax.ppermute(da_behind, "wide", up),
    )
    dk, dv, dq, keep_a, send_a, token = inner_back(
        scalars, k_own, v_own, a_own, oseg, *args, order, partial, *keep_b
    )

    keep_b, got_b = chain.third(keep_b, got_b, token)
    da_own = own_share((dq, dk, dv), weight, *keep_b)
    (send_a,) = hold((send_a,), da_own, *others, *keep_b)
    got_a = links.swap(send_a, "core")
    keep_b, got_b = chain.fourth(keep_b, got_b, send_a)
    keep_a, got_a = links.first([(keep_a, got_a)], keep_b)
    (gains,) = hold((gains,), *keep_a)
    grad_in = finish(joint_in, dx, da_own, others, gains)
    keep_a, got_a = links.second(keep_a, got_a, grad_in)
    sum_b = collect((keep_b, got_b), *keep_a)
    keep_a, got_a = links.third(keep_a, got_a, sum_b)
    keep_a, got_a = links.fourth(keep_a, got_a)

    rate = base_rate * jnp.power(jnp.float32(decay_rate), (11 - layer_index).astype(f32))
    rate = rate * jnp.power(1.0 - step_index.astype(f32) / total_steps, 0.9)
    sum_hid = sum_b[:, :hidden].reshape(shard, ratio, width).transpose(0, 2, 1)
    sum_hid = sum_hid.reshape(shard, hidden)
    far = hidden + width // 2
    sum_proj = sum_b[:, far:far + hidden].reshape(shard * ratio, width)
    step_out, step_hid, step_proj, next_out, next_hid, next_proj, gain_b = update(
        rate, sum_b, sum_hid, sum_proj, w_hidden, mom_attn_out, mom_hidden, mom_proj
    )
    step_qkv, next_qkv, gain_a = update_first(rate, keep_a, got_a, w_qkv, mom_qkv)
    next_g1 = momentum_rate * mom_gain_one + gain_a[:, 0] / gain_one.astype(bf).astype(f32)
    next_g2 = momentum_rate * mom_gain_two + gain_b[:, 0] / gain_two.astype(bf).astype(f32)
    return (
        joint_out,
        grad_in,
        rate * next_g1,
        step_qkv,
        step_out,
        rate * next_g2,
        step_hid,
        step_proj,
        next_g1,
        next_qkv,
        next_out,
        next_g2,
        next_hid,
        next_proj,
    )


def solution(mesh):
    split = P(("wide", "narrow"), None)
    line = P(("wide", "narrow"))
    params = (line, split, split, line, split, split)
    return jax.shard_map(
        body,
        mesh=mesh,
        in_specs=(split, split, P(), P(), P()) + params + params,
        out_specs=(split, split) + params + params,
        check_vma=False,
    )
```

time: 380 us -> 352 us (0.926)
  Pallas kernels: 155 us -> 132 us
  starting transfers between devices: 95.2 us -> 84.8 us
  waiting for transfers between devices: 69.4 us -> 76.5 us
    pallas_call x9 -> x10, Pallas kernels: 139 us -> 118 us  [the longest x1 31.2 us: middle(): pl.pallas_call(middle_kernel, grid_spec=pltpu.PrefetchScalarGridSpec(num_...]
    ppermute x7, starting transfers between devices: 27.7 us -> 11.8 us  [flip_z(): lax.ppermute(array, 'wide', [(j, j ^ 4 * s) for j in range(self.wide)])]
    ppermute x14, waiting for transfers between devices: 20.3 us -> 25.3 us  [swap(): lax.ppermute(array, 'wide', [(j, j ^ flip) for j in range(self.wide)])]
    ppermute x7, waiting for transfers between devices: 13.2 us -> 18 us  [flip_z(): lax.ppermute(array, 'wide', [(j, j ^ 4 * s) for j in range(self.wide)])]
    ppermute x14, starting transfers between devices: 37.7 us -> 42 us  [swap(): lax.ppermute(array, 'wide', [(j, j ^ flip) for j in range(self.wide)])]
    unnamed x103 -> x115, local copies, waits for them, and re-layouts: 17.4 us -> 17.7 us
  transfers between devices with their start and end apart: 36 -> 36, of which waited for: 17 -> 16; matrix products, arithmetic and copies ran while one was open for 5% -> 6% of each run, Pallas kernels for 28% -> 25%
where the time goes in v1:
time: 352 us; the launch traced here: 353 us
  Pallas kernels  132 us (38%)
  starting transfers between devices  84.8 us (24%)
  waiting for transfers between devices  76.5 us (22%)
  local copies, waits for them, and re-layouts  29.6 us (8%)
  between operations  17.2 us (5%)
  other arithmetic  12.2 us (3%)
    ppermute x14, starting transfers between devices, swap(): lax.ppermute(array, 'wide', [(j, j ^ flip) for j in range(self.wide)])  42 us
    pallas_call x1, Pallas kernels, middle(): pl.pallas_call(middle_kernel, grid_spec=pltpu.PrefetchScalarGridSpec(num_...  31.2 us
    pallas_call x1, Pallas kernels, attend(): pl.pallas_call(functools.partial(attend_kernel, pieces=len(ones)), grid_s...  28.3 us
    pallas_call x1, Pallas kernels, inner_back(): pl.pallas_call(inner_kernel, grid_spec=pltpu.PrefetchScalarGridSpec(num_s...  26.7 us
    ppermute x14, waiting for transfers between devices, swap(): lax.ppermute(array, 'wide', [(j, j ^ flip) for j in range(self.wide)])  25.3 us
    ppermute x6, waiting for transfers between devices, swap(): return lax.ppermute(array, 'narrow', [(0, 1), (1, 0)])  18.5 us
    ppermute x7, waiting for transfers between devices, flip_z(): lax.ppermute(array, 'wide', [(j, j ^ 4 * s) for j in range(self.wide)])  18 us
    unnamed x115, local copies, waits for them, and re-layouts  17.7 us
  transfers between devices with their start and end apart: 36, of which 16 were waited for; matrix products, arithmetic and copies ran while one was open for 6% of the time, Pallas kernels for 25%

profile of v1, /device:TPU:0, one launch (start us, length us, event | category | flops | bytes accessed | tf_op | source)
XLA Modules:
  0.0 352.7 jit_solution(2026798145089441927)
XLA Ops:
  8.0 0.9 convert_element_type.49
  9.6 5.0 %collective-permute-start.6 = (bf16[24,2432]{1,0:T(8,128)(2,1)}, bf16[24,2432]{1,0:T(8,128)(2,1)S(1)}, u32[]{:S(2)}, u32[]{:S(2)}) collective-permute-start(bf16[24,2432]{1,0:T(8,128)(2,1)} %pad_maximum_fusion.4), channel_id=1, source_target_pairs={{0,24},{2,26},{4,28},{6,30},{8,16},{10,18},{12,20},{14,22},{16,8},... | collective-permute-start | bytes 350216 | tf_op jit(solution)/shard_map/ppermute | solution.py:687
  14.7 1.5 collective-permute-start
  16.2 1.6 collective-permute-start.1
  17.8 1.3 collective-permute-start.3
  19.1 3.0 collective-permute-start.5
  22.1 1.0 convert_element_type.52
  23.2 1.0 convert_element_type.51
  24.1 1.2 copy.59
  25.3 1.6 copy.60
  27.0 1.3 collective-permute-start.4
  29.0 10.0 %collective-permute-done.5 = bf16[24,2432]{1,0:T(8,128)(2,1)} collective-permute-done((bf16[24,2432]{1,0:T(8,128)(2,1)}, bf16[24,2432]{1,0:T(8,128)(2,1)}, u32[]{:S(2)}, u32[]{:S(2)}) %collective-permute-start.5) | collective-permute-done | bytes 116768 | tf_op jit(solution)/shard_map/ppermute | solution.py:687
  39.3 1.7 pad_maximum_fusion.1.refs_4_
  42.3 0.9 copy-done.35
  44.6 1.4 collective-permute-start.7
  46.6 1.6 collective-permute-start.11
  48.2 3.9 %collective-permute-done.7 = bf16[96,1280]{1,0:T(8,128)(2,1)S(1)} collective-permute-done((bf16[96,1280]{1,0:T(8,128)(2,1)S(1)}, bf16[96,1280]{1,0:T(8,128)(2,1)S(1)}, u32[]{:S(2)}, u32[]{:S(2)}) %collective-permute-start.7) | collective-permute-done | bytes 245792 | tf_op jit(solution)/shard_map/ppermute | solution.py:684
  52.2 1.6 collective-permute-start.8
  53.8 1.5 collective-permute-start.2
  56.4 1.0 collective-permute-start.9
  57.4 8.4 %collective-permute-done.8.refs_14_ = bf16[192,1280]{1,0:T(8,128)(2,1)} collective-permute-done((bf16[192,1280]{1,0:T(8,128)(2,1)S(1)}, bf16[192,1280]{1,0:T(8,128)(2,1)}, u32[]{:S(2)}, u32[]{:S(2)}) %collective-permute-start.8) | collective-permute-done | bytes 491552 | tf_op jit(solution)/shard_map/ppermute | solution.py:682
  68.6 17.5 %collective-permute-start.14 = (bf16[192,1152]{1,0:T(8,128)(2,1)}, bf16[192,1152]{1,0:T(8,128)(2,1)S(1)}, u32[]{:S(2)}, u32[]{:S(2)}) collective-permute-start(bf16[192,1152]{1,0:T(8,128)(2,1)} %collective-permute-done.12.refs_18_), channel_id=1, source_target_pairs={{0,2},{2,0},{4,6},{6,4},{8,10},{10,8},{12,14},{14,12},{16,18},{18,... | collective-permute-start | bytes 1327112 | tf_op jit(solution)/shard_map/ppermute | solution.py:684
  87.2 1.5 fusion.refs_12_.order_ref
  88.8 2.0 broadcast_in_dim.9.refs_8_.kseg_ref
  92.2 28.3 %attend.1 = (bf16[768,2432]{1,0:T(8,128)(2,1)}, f32[8,768]{1,0:T(8,128)}, bf16[640,768]{1,0:T(8,128)(2,1)}, bf16[640,768]{1,0:T(8,128)(2,1)}, bf16[640,768]{1,0:...) custom-call(s32[12]{0:T(128)} %convert_reduce_fusion.3.begin, ...), custom_call_target="tpu_custom_call" | custom-call | flops 1 | bytes 1 | tf_op jit(solution)/shard_map/attend/pallas_call | solution.py:264
  120.5 14.6 %all-gather.2.cloned.1.call-done.wo_ref.wh_ref.wp_ref = bf16[768,6912]{1,0:T(8,128)(2,1)} async-done(((bf16[24,6912]{1,0:T(8,128)(2,1)}), bf16[768,6912]{1,0:T(8,128)(2,1)}) %all-gather.2.cloned.1.call-update) | async-done | bytes 10616848 | tf_op jit(solution)/shard_map/all_gather | solution.py:1126
  136.1 31.2 %middle.1 = (f32[640,768]{1,0:T(8,128)}, bf16[640,3072]{1,0:T(8,128)(2,1)}, bf16[384,3072]{1,0:T(8,128)(2,1)}, bf16[384,3072]{1,0:T(8,128)(2,1)}, bf16[384,3072]...) custom-call(s32[32]{0:T(128)S(1)} %copy-done.28, ...), custom_call_target="tpu_custom_call" | custom-call | flops 1 | bytes 1 | tf_op jit(solution)/shard_map/middle/pallas_call | solution.py:601
  168.1 2.1 copy-done.4
  170.2 1.5 copy-done.12
  171.7 5.5 %layer_out.1.refs_0_ = bf16[640,768]{1,0:T(8,128)(2,1)} custom-call(f32[640,768]{1,0:T(8,128)S(1)} %copy-done.12, bf16[640,3072]{1,0:T(8,128)(2,1)S(1)} %copy-done.4, bf16[768,6912]{1,0:T(8,128)(2,1)S(1)} %bitcast.23), custom_call_target="tpu_custom_call" | custom-call | flops 1 | bytes 1 | tf_op jit(solution)/shard_map/layer_out/pallas_call | solution.py:651
  177.3 1.5 copy-done.39
  179.7 7.4 %first.1 = (bf16[192,3456]{1,0:T(8,128)(2,1)}, bf16[192,3456]{1,0:T(8,128)(2,1)}, bf16[192,3456]{1,0:T(8,128)(2,1)}, bf16[192,3456]{1,0:T(8,128)(2,1)}) custom-call(bf16[384,3072]{1,0:T(8,128)(2,1)} %get-tuple-element.97.hidk, bf16[384,3072]{1,0:T(8,128)(2,1)} %copy-done.39, bf16[384,3072]{1,0:T(8,128)(2,1)} %get-tuple-element.99.projk, ...), custom_call_target="tpu_custom_call" | custom-call | flops 1 | bytes 1 | tf_op jit(solution)/shard_map/first/pallas_call | solution.py:826
  187.0 8.0 %collective-permute-start.18 = (bf16[192,3456]{1,0:T(8,128)(2,1)}, bf16[192,3456]{1,0:T(8,128)(2,1)S(1)}, u32[]{:S(2)}, u32[]{:S(2)}) collective-permute-start(bf16[192,3456]{1,0:T(8,128)(2,1)} %get-tuple-element.107), channel_id=1, source_target_pairs={{0,4},{2,6},{4,0},{6,2},{8,12},{10,14},{12,8},{14,10},{16,20},{18,... | collective-permute-start | bytes 3981320 | tf_op jit(solution)/shard_map/ppermute | solution.py:684
  195.1 14.0 %outer_back.1 = (bf16[640,768]{1,0:T(8,128)(2,1)S(1)}, bf16[640,768]{1,0:T(8,128)(2,1)}, bf16[640,768]{1,0:T(8,128)(2,1)}, bf16[640,768]{1,0:T(8,128)(2,1)S(1)},...) custom-call(s32[12]{0:T(128)S(1)} %copy-done.29, s32[12]{0:T(128)S(1)} %copy-done.31, s32[2]{0:T(128)S(1)} %copy-done.30, ...), custom_call_target="tpu_custom_call" | custom-call | flops 1 | bytes 1 | tf_op jit(solution)/shard_map/outer_back/pallas_call | solution.py:481
  209.1 15.9 %collective-permute-done.18.got_x = bf16[192,3456]{1,0:T(8,128)(2,1)S(1)} collective-permute-done((bf16[192,3456]{1,0:T(8,128)(2,1)}, bf16[192,3456]{1,0:T(8,128)(2,1)S(1)}, u32[]{:S(2)}, u32[]{:S(2)}) %collective-permute-start.18) | collective-permute-done | bytes 1327136 | tf_op jit(solution)/shard_map/ppermute | solution.py:684
  225.0 1.5 collective-permute-done.19.got_y
  227.2 1.4 collective-permute-start.21
  228.6 7.9 %collective-permute-start.22 = (bf16[640,768]{1,0:T(8,128)(2,1)}, bf16[640,768]{1,0:T(8,128)(2,1)}, u32[]{:S(2)}, u32[]{:S(2)}) collective-permute-start(bf16[640,768]{1,0:T(8,128)(2,1)} %get-tuple-element.119), channel_id=1, source_target_pairs={{0,1},{1,0},{2,3},{3,2},{4,5},{5,4},{6,7},{7,6},{8,9},{9,8},{10,11... | collective-permute-start | bytes 2949128 | tf_op jit(solution)/shard_map/ppermute | solution.py:1153
  236.5 1.6 collective-permute-start.23
  238.1 4.0 %collective-permute-start.24 = (bf16[640,768]{1,0:T(8,128)(2,1)S(1)}, bf16[640,768]{1,0:T(8,128)(2,1)}, u32[]{:S(2)}, u32[]{:S(2)}) collective-permute-start(bf16[640,768]{1,0:T(8,128)(2,1)S(1)} %get-tuple-element.121), channel_id=1, source_target_pairs={{0,2},{2,4},{4,6},{6,8},{8,10},{10,12},{12,14},{14,16},{16,18},{18... | collective-permute-start | bytes 2949128 | tf_op jit(solution)/shard_map/ppermute | solution.py:1155
  242.1 26.7 %inner_back.1 = (bf16[640,768]{1,0:T(8,128)(2,1)S(1)}, bf16[640,768]{1,0:T(8,128)(2,1)S(1)}, bf16[640,768]{1,0:T(8,128)(2,1)S(1)}, bf16[384,2304]{1,0:T(8,128)(2...) custom-call(s32[12]{0:T(128)S(1)} %copy-done.29, s32[12]{0:T(128)S(1)} %copy-done.31, s32[2]{0:T(128)S(1)} %copy-done.30, ...), custom_call_target="tpu_custom_call" | custom-call | flops 1 | bytes 1 | tf_op jit(solution)/shard_map/inner_back/pallas_call | solution.py:512
  268.9 0.9 copy-done.23
  272.2 6.4 %own_share.1.refs_1_.own_ref = f32[640,768]{1,0:T(8,128)} custom-call(bf16[640,768]{1,0:T(8,128)(2,1)} %copy-done.23, bf16[640,768]{1,0:T(8,128)(2,1)} %copy-done.21, bf16[640,768]{1,0:T(8,128)(2,1)} %copy-done.22, bf16[768,2432]{1,0:T(8,128)(2,1)} %get-tuple-element.96.w_ref, bf16[48,3456]{1,0:T(8,128)(2,1)} %copy-done.6, bf16[48,3456]{1,0:T(8,128)(2,1)} %copy-done.8), custom_call_target="tpu_custom_call" | custom-call | flops 1 | bytes 1 | tf_op jit(solution)/shard_map/own_share/pallas_call | solution.py:945
  278.7 7.7 %collective-permute-start.25 = (bf16[384,2304]{1,0:T(8,128)(2,1)}, bf16[384,2304]{1,0:T(8,128)(2,1)S(1)}, u32[]{:S(2)}, u32[]{:S(2)}) collective-permute-start(bf16[384,2304]{1,0:T(8,128)(2,1)} %hold.4.refs_0_), channel_id=1, source_target_pairs={{0,2},{2,0},{4,6},{6,4},{8,10},{10,8},{12,14},{14,12},{16,18},{18,... | collective-permute-start | bytes 5308424 | tf_op jit(solution)/shard_map/ppermute | solution.py:684
  286.4 4.0 %collective-permute-start.26 = (bf16[48,3456]{1,0:T(8,128)(2,1)S(1)}, bf16[48,3456]{1,0:T(8,128)(2,1)S(1)}, u32[]{:S(2)}, u32[]{:S(2)}) collective-permute-start(bf16[48,3456]{1,0:T(8,128)(2,1)S(1)} %get-tuple-element.124), channel_id=1, source_target_pairs={{0,1},{1,0},{2,3},{3,2},{4,5},{5,4},{6,7},{7,6},{8,9},{9,8},{10,11... | collective-permute-start | bytes 995336 | tf_op jit(solution)/shard_map/ppermute | solution.py:682
  290.4 1.7 collective-permute-start.27
  292.1 6.7 %collective-permute-done.26.got_x = bf16[48,3456]{1,0:T(8,128)(2,1)S(1)} collective-permute-done((bf16[48,3456]{1,0:T(8,128)(2,1)S(1)}, bf16[48,3456]{1,0:T(8,128)(2,1)S(1)}, u32[]{:S(2)}, u32[]{:S(2)}) %collective-permute-start.26) | collective-permute-done | bytes 331808 | tf_op jit(solution)/shard_map/ppermute | solution.py:682
  298.8 1.5 collective-permute-done.27.got_y
  300.3 1.5 copy-done.1
  301.9 1.1 stage.11
  304.6 1.7 collective-permute-start.28
  306.3 1.7 collective-permute-start.29
  308.4 5.6 %finish.1.refs_0_ = bf16[640,768]{1,0:T(8,128)(2,1)} custom-call(bf16[640,768]{1,0:T(8,128)(2,1)} %x_ref.3, f32[640,768]{1,0:T(8,128)} %get-tuple-element.86.dx_ref, f32[640,768]{1,0:T(8,128)} %own_share.1.refs_1_.own_ref, bf16[640,768]{1,0:T(8,128)(2,1)} %collective-permute-done.21.refs_2_.b0, bf16[640,768]{1,0:T(8,128)(2,1)} %collective-permute-done.22.refs_3_.b1, ...), custom_call_target="tpu_custom_call" | custom-call | flops 1 | bytes 1 | tf_op jit(solution)/shard_map/finish/pallas_call | solution.py:968
  314.0 2.2 collective-permute-done.28.got_x
  316.2 1.2 collective-permute-done.29.got_y
  317.4 1.2 copy-done.5
  318.8 1.3 collective-permute-start.30
  322.1 1.9 collective-permute-done.32.refs_1_
  324.8 1.3 collective-permute-done.31.got_y
  326.2 1.9 collective-permute-start.33
  329.0 1.1 copy.62.hid_ref
  331.0 2.7 update.1
  335.8 5.9 %collective-permute-done.34.got_ref = bf16[24,2304]{1,0:T(8,128)(2,1)S(1)} collective-permute-done((bf16[24,2304]{1,0:T(8,128)(2,1)S(1)}, bf16[24,2304]{1,0:T(8,128)(2,1)S(1)}, u32[]{:S(2)}, u32[]{:S(2)}) %collective-permute-start.34) | collective-permute-done | bytes 110624 | tf_op jit(solution)/shard_map/ppermute | solution.py:687
  342.3 2.0 update_first.1
  (193 shorter events, 26.8 us)
Async XLA Ops:
  7.2 128.0 %all-gather.2.cloned.1.call-start = ((), (), s32[]{:S(2)}) async-start(), calls=%async_computation | async-start | bytes 10948608 | tf_op jit(solution)/shard_map/all_gather | solution.py:1126
  7.9 19.0 %copy-start.47 = (f32[24,768]{1,0:T(8,128)S(1)}, f32[24,768]{1,0:T(8,128)}, u32[]{:S(2)}) copy-start(f32[24,768]{1,0:T(8,128)} %param.26) | copy-start | bytes 221188
  9.6 17.3 %collective-permute-start.6 = (bf16[24,2432]{1,0:T(8,128)(2,1)}, bf16[24,2432]{1,0:T(8,128)(2,1)S(1)}, u32[]{:S(2)}, u32[]{:S(2)}) collective-permute-start(bf16[24,2432]{1,0:T(8,128)(2,1)} %pad_maximum_fusion.4), channel_id=1, source_target_pairs={{0,24},{2,26},{4,28},{6,30},{8,16},{10,18},{12,20},{14,22},{16,8},... | collective-permute-start | bytes 350216 | tf_op jit(solution)/shard_map/ppermute | solution.py:687
  14.7 26.3 %collective-permute-start = (bf16[640,768]{1,0:T(8,128)(2,1)}, bf16[640,768]{1,0:T(8,128)(2,1)S(1)}, u32[]{:S(2)}, u32[]{:S(2)}) collective-permute-start(bf16[640,768]{1,0:T(8,128)(2,1)} %x_ref.3), channel_id=1, source_target_pairs={{0,2},{2,4},{4,6},{6,8},{8,10},{10,12},{12,14},{14,16},{16,18},{18... | collective-permute-start | bytes 2949128 | tf_op jit(solution)/shard_map/ppermute | solution.py:1119
  16.2 24.8 %collective-permute-start.1 = (bf16[640,768]{1,0:T(8,128)(2,1)}, bf16[640,768]{1,0:T(8,128)(2,1)S(1)}, u32[]{:S(2)}, u32[]{:S(2)}) collective-permute-start(bf16[640,768]{1,0:T(8,128)(2,1)} %x_ref.3), channel_id=1, source_target_pairs={{0,1},{1,0},{2,3},{3,2},{4,5},{5,4},{6,7},{7,6},{8,9},{9,8},{10,11... | collective-permute-start | bytes 2949128 | tf_op jit(solution)/shard_map/ppermute | solution.py:1118
  17.8 23.2 %collective-permute-start.3 = (bf16[640,768]{1,0:T(8,128)(2,1)}, bf16[640,768]{1,0:T(8,128)(2,1)S(1)}, u32[]{:S(2)}, u32[]{:S(2)}) collective-permute-start(bf16[640,768]{1,0:T(8,128)(2,1)} %x_ref.3), channel_id=1, source_target_pairs={{2,0},{4,2},{6,4},{8,6},{10,8},{12,10},{14,12},{16,14},{18,16},{20... | collective-permute-start | bytes 2949128 | tf_op jit(solution)/shard_map/ppermute | solution.py:1120
  19.1 20.0 %collective-permute-start.5 = (bf16[24,2432]{1,0:T(8,128)(2,1)}, bf16[24,2432]{1,0:T(8,128)(2,1)}, u32[]{:S(2)}, u32[]{:S(2)}) collective-permute-start(bf16[24,2432]{1,0:T(8,128)(2,1)} %pad_maximum_fusion.4), channel_id=1, source_target_pairs={{0,8},{2,10},{4,12},{6,14},{8,0},{10,2},{12,4},{14,6},{16,24},{18,... | collective-permute-start | bytes 350216 | tf_op jit(solution)/shard_map/ppermute | solution.py:687
  27.0 12.3 %collective-permute-start.4 = (bf16[24,2432]{1,0:T(8,128)(2,1)}, bf16[24,2432]{1,0:T(8,128)(2,1)S(1)}, u32[]{:S(2)}, u32[]{:S(2)}) collective-permute-start(bf16[24,2432]{1,0:T(8,128)(2,1)} %pad_maximum_fusion.4), channel_id=1, source_target_pairs={{0,16},{2,18},{4,20},{6,22},{8,24},{10,26},{12,28},{14,30},{16,0},... | collective-permute-start | bytes 350216 | tf_op jit(solution)/shard_map/ppermute | solution.py:687
  43.2 10.6 %copy-start.34 = (bf16[640,768]{1,0:T(8,128)(2,1)S(1)}, bf16[640,768]{1,0:T(8,128)(2,1)}, u32[]{:S(2)}) copy-start(bf16[640,768]{1,0:T(8,128)(2,1)} %copy-done.33) | copy-start | bytes 2949124
  43.2 43.4 %copy-start.52 = (s32[12]{0:T(128)S(1)}, s32[12]{0:T(128)}, u32[]{:S(2)}) copy-start(s32[12]{0:T(128)} %constant.179.clone) | copy-start | bytes 148
  44.6 7.5 %collective-permute-start.7 = (bf16[96,1280]{1,0:T(8,128)(2,1)S(1)}, bf16[96,1280]{1,0:T(8,128)(2,1)S(1)}, u32[]{:S(2)}, u32[]{:S(2)}) collective-permute-start(bf16[96,1280]{1,0:T(8,128)(2,1)S(1)} %slice.50), channel_id=1, source_target_pairs={{0,4},{2,6},{4,0},{6,2},{8,12},{10,14},{12,8},{14,10},{16,20},{18,... | collective-permute-start | bytes 737288 | tf_op jit(solution)/shard_map/ppermute | solution.py:684
  46.6 8.7 %collective-permute-start.11 = (bf16[96,1152]{1,0:T(8,128)(2,1)S(1)}, bf16[96,1152]{1,0:T(8,128)(2,1)S(1)}, u32[]{:S(2)}, u32[]{:S(2)}) collective-permute-start(bf16[96,1152]{1,0:T(8,128)(2,1)S(1)} %slice.51), channel_id=1, source_target_pairs={{0,1},{1,0},{2,3},{3,2},{4,5},{5,4},{6,7},{7,6},{8,9},{9,8},{10,11... | collective-permute-start | bytes 663560 | tf_op jit(solution)/shard_map/ppermute | solution.py:682
  52.2 39.4 %copy-start.41 = (bf16[192,1280]{1,0:T(8,128)(2,1)}, bf16[192,1280]{1,0:T(8,128)(2,1)S(1)}, u32[]{:S(2)}) copy-start(bf16[192,1280]{1,0:T(8,128)(2,1)S(1)} %pad_maximum_fusion.refs_13_) | copy-start | bytes 1474564
  52.2 13.6 %collective-permute-start.8 = (bf16[192,1280]{1,0:T(8,128)(2,1)S(1)}, bf16[192,1280]{1,0:T(8,128)(2,1)}, u32[]{:S(2)}, u32[]{:S(2)}) collective-permute-start(bf16[192,1280]{1,0:T(8,128)(2,1)S(1)} %pad_maximum_fusion.refs_13_), channel_id=1, source_target_pairs={{0,1},{1,0},{2,3},{3,2},{4,5},{5,4},{6,7},{7,6},{8,9},{9,8},{10,11... | collective-permute-start | bytes 1474568 | tf_op jit(solution)/shard_map/ppermute | solution.py:682
  53.8 35.0 %collective-permute-start.2 = (bf16[640,768]{1,0:T(8,128)(2,1)S(1)}, bf16[640,768]{1,0:T(8,128)(2,1)S(1)}, u32[]{:S(2)}, u32[]{:S(2)}) collective-permute-start(bf16[640,768]{1,0:T(8,128)(2,1)S(1)} %copy-done.34), channel_id=1, source_target_pairs={{0,2},{2,4},{4,6},{6,8},{8,10},{10,12},{12,14},{14,16},{16,18},{18... | collective-permute-start | bytes 2949128 | tf_op jit(solution)/shard_map/ppermute | solution.py:1122
  55.4 36.9 %copy-start.42 = (bf16[192,1152]{1,0:T(8,128)(2,1)}, bf16[192,1152]{1,0:T(8,128)(2,1)S(1)}, u32[]{:S(2)}) copy-start(bf16[192,1152]{1,0:T(8,128)(2,1)S(1)} %pad_maximum_fusion.2.refs_17_) | copy-start | bytes 1327108
  55.4 13.2 %collective-permute-start.12 = (bf16[192,1152]{1,0:T(8,128)(2,1)S(1)}, bf16[192,1152]{1,0:T(8,128)(2,1)}, u32[]{:S(2)}, u32[]{:S(2)}) collective-permute-start(bf16[192,1152]{1,0:T(8,128)(2,1)S(1)} %pad_maximum_fusion.2.refs_17_), channel_id=1, source_target_pairs={{0,4},{2,6},{4,0},{6,2},{8,12},{10,14},{12,8},{14,10},{16,20},{18,... | collective-permute-start | bytes 1327112 | tf_op jit(solution)/shard_map/ppermute | solution.py:684
  56.4 32.3 %collective-permute-start.9 = (bf16[192,1280]{1,0:T(8,128)(2,1)S(1)}, bf16[192,1280]{1,0:T(8,128)(2,1)}, u32[]{:S(2)}, u32[]{:S(2)}) collective-permute-start(bf16[192,1280]{1,0:T(8,128)(2,1)S(1)} %pad_maximum_fusion.refs_13_), channel_id=1, source_target_pairs={{0,2},{2,0},{4,6},{6,4},{8,10},{10,8},{12,14},{14,12},{16,18},{18,... | collective-permute-start | bytes 1474568 | tf_op jit(solution)/shard_map/ppermute | solution.py:684
  65.8 22.9 %collective-permute-start.10 = (bf16[192,1280]{1,0:T(8,128)(2,1)}, bf16[192,1280]{1,0:T(8,128)(2,1)}, u32[]{:S(2)}, u32[]{:S(2)}) collective-permute-start(bf16[192,1280]{1,0:T(8,128)(2,1)} %collective-permute-done.8.refs_14_), channel_id=1, source_target_pairs={{0,2},{2,0},{4,6},{6,4},{8,10},{10,8},{12,14},{14,12},{16,18},{18,... | collective-permute-start | bytes 1474568 | tf_op jit(solution)/shard_map/ppermute | solution.py:684
  67.5 21.3 %collective-permute-start.13 = (bf16[192,1152]{1,0:T(8,128)(2,1)S(1)}, bf16[192,1152]{1,0:T(8,128)(2,1)S(1)}, u32[]{:S(2)}, u32[]{:S(2)}) collective-permute-start(bf16[192,1152]{1,0:T(8,128)(2,1)S(1)} %pad_maximum_fusion.2.refs_17_), channel_id=1, source_target_pairs={{0,2},{2,0},{4,6},{6,4},{8,10},{10,8},{12,14},{14,12},{16,18},{18,... | collective-permute-start | bytes 1327112 | tf_op jit(solution)/shard_map/ppermute | solution.py:684
  68.6 20.2 %collective-permute-start.14 = (bf16[192,1152]{1,0:T(8,128)(2,1)}, bf16[192,1152]{1,0:T(8,128)(2,1)S(1)}, u32[]{:S(2)}, u32[]{:S(2)}) collective-permute-start(bf16[192,1152]{1,0:T(8,128)(2,1)} %collective-permute-done.12.refs_18_), channel_id=1, source_target_pairs={{0,2},{2,0},{4,6},{6,4},{8,10},{10,8},{12,14},{14,12},{16,18},{18,... | collective-permute-start | bytes 1327112 | tf_op jit(solution)/shard_map/ppermute | solution.py:684
  92.2 43.0 %copy-start.28 = (s32[32]{0:T(128)S(1)}, s32[32]{0:T(128)}, u32[]{:S(2)}) copy-start(s32[32]{0:T(128)} %get-tuple-element.159.places) | copy-start | bytes 388
  135.2 32.9 %slice-start = ((s8[10616832]{0:T(1024)(128)(4,1)}), s8[4194304]{0:T(1024)(128)(4,1)S(1)}, s32[]{:S(2)}) async-start(s8[10616832]{0:T(1024)(128)(4,1)} %bitcast.22), calls=%async_computation.1 | async-start | bytes 8388608
  136.1 32.0 %slice-start.1 = ((s8[10616832]{0:T(1024)(128)(4,1)}), s8[4194304]{0:T(1024)(128)(4,1)S(1)}, s32[]{:S(2)}) async-start(s8[10616832]{0:T(1024)(128)(4,1)} %bitcast.22), calls=%async_computation.2 | async-start | bytes 8388608
  136.1 32.0 %slice-start.2 = ((s8[10616832]{0:T(1024)(128)(4,1)}), s8[2228224]{0:T(1024)(128)(4,1)S(1)}, s32[]{:S(2)}) async-start(s8[10616832]{0:T(1024)(128)(4,1)} %bitcast.22), calls=%async_computation.3 | async-start | bytes 4456448
  167.2 10.1 %copy-start.11 = (bf16[384,768]{1,0:T(8,128)(2,1)}, bf16[384,768]{1,0:T(8,128)(2,1)S(1)}, u32[]{:S(2)}) copy-start(bf16[384,768]{1,0:T(8,128)(2,1)S(1)} %get-tuple-element.101.outk_x.outk_y) | copy-start | bytes 1769476
  167.2 10.1 %collective-permute-start.15 = (bf16[384,3072]{1,0:T(8,128)(2,1)}, bf16[384,3072]{1,0:T(8,128)(2,1)S(1)}, u32[]{:S(2)}, u32[]{:S(2)}) collective-permute-start(bf16[384,3072]{1,0:T(8,128)(2,1)} %get-tuple-element.98), channel_id=1, source_target_pairs={{0,2},{2,0},{4,6},{6,4},{8,10},{10,8},{12,14},{14,12},{16,18},{18,... | collective-permute-start | bytes 7077896 | tf_op jit(solution)/shard_map/ppermute | solution.py:684
  167.6 9.7 %collective-permute-start.16 = (bf16[384,3072]{1,0:T(8,128)(2,1)}, bf16[384,3072]{1,0:T(8,128)(2,1)S(1)}, u32[]{:S(2)}, u32[]{:S(2)}) collective-permute-start(bf16[384,3072]{1,0:T(8,128)(2,1)} %get-tuple-element.100), channel_id=1, source_target_pairs={{0,2},{2,0},{4,6},{6,4},{8,10},{10,8},{12,14},{14,12},{16,18},{18,... | collective-permute-start | bytes 7077896 | tf_op jit(solution)/shard_map/ppermute | solution.py:684
  167.8 9.5 %collective-permute-start.17 = (bf16[384,768]{1,0:T(8,128)(2,1)S(1)}, bf16[384,768]{1,0:T(8,128)(2,1)S(1)}, u32[]{:S(2)}, u32[]{:S(2)}) collective-permute-start(bf16[384,768]{1,0:T(8,128)(2,1)S(1)} %get-tuple-element.102), channel_id=1, source_target_pairs={{0,2},{2,0},{4,6},{6,4},{8,10},{10,8},{12,14},{14,12},{16,18},{18,... | collective-permute-start | bytes 1769480 | tf_op jit(solution)/shard_map/ppermute | solution.py:684
  179.6 15.4 %copy-start.24 = (s32[5,8,128]{2,1,0:T(8,128)S(1)}, s32[5,8,128]{2,1,0:T(8,128)}, u32[]{:S(2)}) copy-start(s32[5,8,128]{2,1,0:T(8,128)} %broadcast_in_dim.11.refs_11_.qseg_ref) | copy-start | bytes 61444
  179.6 15.4 %copy-start.26 = (f32[5,6,1,256]{3,2,1,0:T(1,128)S(1)}, f32[5,6,1,256]{3,2,1,0:T(1,128)}, u32[]{:S(2)}) copy-start(f32[5,6,1,256]{3,2,1,0:T(1,128)} %get-tuple-element.92.lse_ref) | copy-start | bytes 92164
  179.6 15.4 %copy-start.29 = (s32[12]{0:T(128)S(1)}, s32[12]{0:T(128)}, u32[]{:S(2)}) copy-start(s32[12]{0:T(128)} %convert_reduce_fusion.3.begin) | copy-start | bytes 148
  179.7 15.4 %copy-start.30 = (s32[2]{0:T(128)S(1)}, s32[2]{0:T(128)}, u32[]{:S(2)}) copy-start(s32[2]{0:T(128)} %pad_add_fusion.1.span) | copy-start | bytes 28
  179.7 15.4 %copy-start.31 = (s32[12]{0:T(128)S(1)}, s32[12]{0:T(128)}, u32[]{:S(2)}) copy-start(s32[12]{0:T(128)} %convert_reduce_fusion.2.end) | copy-start | bytes 148
  187.0 38.0 %collective-permute-start.18 = (bf16[192,3456]{1,0:T(8,128)(2,1)}, bf16[192,3456]{1,0:T(8,128)(2,1)S(1)}, u32[]{:S(2)}, u32[]{:S(2)}) collective-permute-start(bf16[192,3456]{1,0:T(8,128)(2,1)} %get-tuple-element.107), channel_id=1, source_target_pairs={{0,4},{2,6},{4,0},{6,2},{8,12},{10,14},{12,8},{14,10},{16,20},{18,... | collective-permute-start | bytes 3981320 | tf_op jit(solution)/shard_map/ppermute | solution.py:684
  195.1 31.4 %collective-permute-start.19 = (bf16[192,3456]{1,0:T(8,128)(2,1)}, bf16[192,3456]{1,0:T(8,128)(2,1)S(1)}, u32[]{:S(2)}, u32[]{:S(2)}) collective-permute-start(bf16[192,3456]{1,0:T(8,128)(2,1)} %get-tuple-element.108), channel_id=1, source_target_pairs={{0,1},{1,0},{2,3},{3,2},{4,5},{5,4},{6,7},{7,6},{8,9},{9,8},{10,11... | collective-permute-start | bytes 3981320 | tf_op jit(solution)/shard_map/ppermute | solution.py:682
  195.1 31.4 %copy-start.2 = (bf16[192,3456]{1,0:T(8,128)(2,1)S(1)}, bf16[192,3456]{1,0:T(8,128)(2,1)}, u32[]{:S(2)}) copy-start(bf16[192,3456]{1,0:T(8,128)(2,1)} %get-tuple-element.103.refs_0_.keep_x) | copy-start | bytes 3981316
  195.1 31.4 %copy-start.3 = (bf16[192,3456]{1,0:T(8,128)(2,1)S(1)}, bf16[192,3456]{1,0:T(8,128)(2,1)}, u32[]{:S(2)}) copy-start(bf16[192,3456]{1,0:T(8,128)(2,1)} %get-tuple-element.104.refs_1_.keep_y) | copy-start | bytes 3981316
  226.5 15.7 %copy-start.10 = (s32[640,128]{1,0:T(8,128)S(1)}, s32[640,128]{1,0:T(8,128)}, u32[]{:S(2)}) copy-start(s32[640,128]{1,0:T(8,128)} %broadcast_in_dim.10.refs_9_.kseg_ref) | copy-start | bytes 983044
  226.5 15.7 %copy-start.18 = (bf16[640,768]{1,0:T(8,128)(2,1)S(1)}, bf16[640,768]{1,0:T(8,128)(2,1)}, u32[]{:S(2)}) copy-start(bf16[640,768]{1,0:T(8,128)(2,1)} %get-tuple-element.89.a_ref) | copy-start | bytes 2949124
  226.5 15.7 %copy-start.19 = (bf16[640,768]{1,0:T(8,128)(2,1)S(1)}, bf16[640,768]{1,0:T(8,128)(2,1)}, u32[]{:S(2)}) copy-start(bf16[640,768]{1,0:T(8,128)(2,1)} %get-tuple-element.87.k_ref) | copy-start | bytes 2949124
  226.5 15.6 %copy-start.20 = (bf16[640,768]{1,0:T(8,128)(2,1)S(1)}, bf16[640,768]{1,0:T(8,128)(2,1)}, u32[]{:S(2)}) copy-start(bf16[640,768]{1,0:T(8,128)(2,1)} %get-tuple-element.88.v_ref) | copy-start | bytes 2949124
  227.1 42.7 %collective-permute-start.20 = (bf16[96,6912]{1,0:T(8,128)(2,1)S(1)}, bf16[96,6912]{1,0:T(8,128)(2,1)S(1)}, u32[]{:S(2)}, u32[]{:S(2)}) collective-permute-start(bf16[96,6912]{1,0:T(8,128)(2,1)S(1)} %get-tuple-element.115), channel_id=1, source_target_pairs={{0,8},{2,10},{4,12},{6,14},{8,0},{10,2},{12,4},{14,6},{16,24},{18,... | collective-permute-start | bytes 3981320 | tf_op jit(solution)/shard_map/ppermute | solution.py:687
  227.2 51.4 %collective-permute-start.21 = (bf16[640,768]{1,0:T(8,128)(2,1)S(1)}, bf16[640,768]{1,0:T(8,128)(2,1)}, u32[]{:S(2)}, u32[]{:S(2)}) collective-permute-start(bf16[640,768]{1,0:T(8,128)(2,1)S(1)} %get-tuple-element.109.refs_0_), channel_id=1, source_target_pairs={{2,0},{4,2},{6,4},{8,6},{10,8},{12,10},{14,12},{16,14},{18,16},{20... | collective-permute-start | bytes 2949128 | tf_op jit(solution)/shard_map/ppermute | solution.py:1152
  228.6 50.0 %collective-permute-start.22 = (bf16[640,768]{1,0:T(8,128)(2,1)}, bf16[640,768]{1,0:T(8,128)(2,1)}, u32[]{:S(2)}, u32[]{:S(2)}) collective-permute-start(bf16[640,768]{1,0:T(8,128)(2,1)} %get-tuple-element.119), channel_id=1, source_target_pairs={{0,1},{1,0},{2,3},{3,2},{4,5},{5,4},{6,7},{7,6},{8,9},{9,8},{10,11... | collective-permute-start | bytes 2949128 | tf_op jit(solution)/shard_map/ppermute | solution.py:1153
  236.5 42.1 %collective-permute-start.23 = (bf16[640,768]{1,0:T(8,128)(2,1)}, bf16[640,768]{1,0:T(8,128)(2,1)}, u32[]{:S(2)}, u32[]{:S(2)}) collective-permute-start(bf16[640,768]{1,0:T(8,128)(2,1)} %get-tuple-element.120), channel_id=1, source_target_pairs={{2,1},{4,3},{6,5},{8,7},{10,9},{12,11},{14,13},{16,15},{18,17},{20... | collective-permute-start | bytes 2949128 | tf_op jit(solution)/shard_map/ppermute | solution.py:1154
  238.1 40.5 %collective-permute-start.24 = (bf16[640,768]{1,0:T(8,128)(2,1)S(1)}, bf16[640,768]{1,0:T(8,128)(2,1)}, u32[]{:S(2)}, u32[]{:S(2)}) collective-permute-start(bf16[640,768]{1,0:T(8,128)(2,1)S(1)} %get-tuple-element.121), channel_id=1, source_target_pairs={{0,2},{2,4},{4,6},{6,8},{8,10},{10,12},{12,14},{14,16},{16,18},{18... | collective-permute-start | bytes 2949128 | tf_op jit(solution)/shard_map/ppermute | solution.py:1155
  278.6 21.6 %copy-start.7 = (bf16[48,3456]{1,0:T(8,128)(2,1)S(1)}, bf16[48,3456]{1,0:T(8,128)(2,1)}, u32[]{:S(2)}) copy-start(bf16[48,3456]{1,0:T(8,128)(2,1)} %copy-done.6) | copy-start | bytes 995332
  278.6 21.6 %copy-start.9 = (bf16[48,3456]{1,0:T(8,128)(2,1)S(1)}, bf16[48,3456]{1,0:T(8,128)(2,1)}, u32[]{:S(2)}) copy-start(bf16[48,3456]{1,0:T(8,128)(2,1)} %copy-done.8) | copy-start | bytes 995332
  278.6 23.3 %copy-start.13 = (bf16[384,2304]{1,0:T(8,128)(2,1)S(1)}, bf16[384,2304]{1,0:T(8,128)(2,1)}, u32[]{:S(2)}) copy-start(bf16[384,2304]{1,0:T(8,128)(2,1)} %get-tuple-element.122.refs_0_) | copy-start | bytes 5308420
  278.7 23.2 %collective-permute-start.25 = (bf16[384,2304]{1,0:T(8,128)(2,1)}, bf16[384,2304]{1,0:T(8,128)(2,1)S(1)}, u32[]{:S(2)}, u32[]{:S(2)}) collective-permute-start(bf16[384,2304]{1,0:T(8,128)(2,1)} %hold.4.refs_0_), channel_id=1, source_target_pairs={{0,2},{2,0},{4,6},{6,4},{8,10},{10,8},{12,14},{14,12},{16,18},{18,... | collective-permute-start | bytes 5308424 | tf_op jit(solution)/shard_map/ppermute | solution.py:684
  286.4 12.4 %collective-permute-start.26 = (bf16[48,3456]{1,0:T(8,128)(2,1)S(1)}, bf16[48,3456]{1,0:T(8,128)(2,1)S(1)}, u32[]{:S(2)}, u32[]{:S(2)}) collective-permute-start(bf16[48,3456]{1,0:T(8,128)(2,1)S(1)} %get-tuple-element.124), channel_id=1, source_target_pairs={{0,1},{1,0},{2,3},{3,2},{4,5},{5,4},{6,7},{7,6},{8,9},{9,8},{10,11... | collective-permute-start | bytes 995336 | tf_op jit(solution)/shard_map/ppermute | solution.py:682
  290.4 9.9 %collective-permute-start.27 = (bf16[48,3456]{1,0:T(8,128)(2,1)S(1)}, bf16[48,3456]{1,0:T(8,128)(2,1)S(1)}, u32[]{:S(2)}, u32[]{:S(2)}) collective-permute-start(bf16[48,3456]{1,0:T(8,128)(2,1)S(1)} %get-tuple-element.125), channel_id=1, source_target_pairs={{0,4},{2,6},{4,0},{6,2},{8,12},{10,14},{12,8},{14,10},{16,20},{18,... | collective-permute-start | bytes 995336 | tf_op jit(solution)/shard_map/ppermute | solution.py:684
  304.6 11.6 %collective-permute-start.28 = (bf16[192,1152]{1,0:T(8,128)(2,1)}, bf16[192,1152]{1,0:T(8,128)(2,1)S(1)}, u32[]{:S(2)}, u32[]{:S(2)}) collective-permute-start(bf16[192,1152]{1,0:T(8,128)(2,1)} %get-tuple-element.129), channel_id=1, source_target_pairs={{0,4},{2,6},{4,0},{6,2},{8,12},{10,14},{12,8},{14,10},{16,20},{18,... | collective-permute-start | bytes 1327112 | tf_op jit(solution)/shard_map/ppermute | solution.py:684
  306.3 11.1 %collective-permute-start.29 = (bf16[192,1152]{1,0:T(8,128)(2,1)S(1)}, bf16[192,1152]{1,0:T(8,128)(2,1)S(1)}, u32[]{:S(2)}, u32[]{:S(2)}) collective-permute-start(bf16[192,1152]{1,0:T(8,128)(2,1)S(1)} %get-tuple-element.130), channel_id=1, source_target_pairs={{0,1},{1,0},{2,3},{3,2},{4,5},{5,4},{6,7},{7,6},{8,9},{9,8},{10,11... | collective-permute-start | bytes 1327112 | tf_op jit(solution)/shard_map/ppermute | solution.py:682
  307.9 16.1 %collective-permute-start.32 = (bf16[24,6912]{1,0:T(8,128)(2,1)S(1)}, bf16[24,6912]{1,0:T(8,128)(2,1)S(1)}, u32[]{:S(2)}, u32[]{:S(2)}) collective-permute-start(bf16[24,6912]{1,0:T(8,128)(2,1)S(1)} %get-tuple-element.135), channel_id=1, source_target_pairs={{0,16},{2,18},{4,20},{6,22},{8,24},{10,26},{12,28},{14,30},{16,0},... | collective-permute-start | bytes 995336 | tf_op jit(solution)/shard_map/ppermute | solution.py:687
  308.4 9.0 %copy-start.15 = (bf16[192,1152]{1,0:T(8,128)(2,1)S(1)}, bf16[192,1152]{1,0:T(8,128)(2,1)}, u32[]{:S(2)}) copy-start(bf16[192,1152]{1,0:T(8,128)(2,1)} %copy-done.14) | copy-start | bytes 1327108
  308.4 9.0 %copy-start.17 = (bf16[192,1152]{1,0:T(8,128)(2,1)S(1)}, bf16[192,1152]{1,0:T(8,128)(2,1)}, u32[]{:S(2)}) copy-start(bf16[192,1152]{1,0:T(8,128)(2,1)} %copy-done.16) | copy-start | bytes 1327108
  318.8 6.0 %collective-permute-start.30 = (bf16[96,1152]{1,0:T(8,128)(2,1)S(1)}, bf16[96,1152]{1,0:T(8,128)(2,1)S(1)}, u32[]{:S(2)}, u32[]{:S(2)}) collective-permute-start(bf16[96,1152]{1,0:T(8,128)(2,1)S(1)} %get-tuple-element.133), channel_id=1, source_target_pairs={{0,1},{1,0},{2,3},{3,2},{4,5},{5,4},{6,7},{7,6},{8,9},{9,8},{10,11... | collective-permute-start | bytes 663560 | tf_op jit(solution)/shard_map/ppermute | solution.py:682
  320.1 5.9 %collective-permute-start.31 = (bf16[96,1152]{1,0:T(8,128)(2,1)S(1)}, bf16[96,1152]{1,0:T(8,128)(2,1)S(1)}, u32[]{:S(2)}, u32[]{:S(2)}) collective-permute-start(bf16[96,1152]{1,0:T(8,128)(2,1)S(1)} %get-tuple-element.134), channel_id=1, source_target_pairs={{0,4},{2,6},{4,0},{6,2},{8,12},{10,14},{12,8},{14,10},{16,20},{18,... | collective-permute-start | bytes 663560 | tf_op jit(solution)/shard_map/ppermute | solution.py:684
  326.2 8.3 %collective-permute-start.33 = (bf16[48,2304]{1,0:T(8,128)(2,1)S(1)}, bf16[48,2304]{1,0:T(8,128)(2,1)S(1)}, u32[]{:S(2)}, u32[]{:S(2)}) collective-permute-start(bf16[48,2304]{1,0:T(8,128)(2,1)S(1)} %get-tuple-element.137), channel_id=1, source_target_pairs={{0,8},{2,10},{4,12},{6,14},{8,0},{10,2},{12,4},{14,6},{16,24},{18,... | collective-permute-start | bytes 663560 | tf_op jit(solution)/shard_map/ppermute | solution.py:687
  330.2 14.9 %copy-start.49 = (f32[24]{0:T(128)S(1)}, f32[24]{0:T(128)}, u32[]{:S(2)}) copy-start(f32[24]{0:T(128)} %param.24) | copy-start | bytes 292
  330.2 14.9 %copy-start.51 = (f32[24]{0:T(128)S(1)}, f32[24]{0:T(128)}, u32[]{:S(2)}) copy-start(f32[24]{0:T(128)} %param.30) | copy-start | bytes 292
  335.2 6.4 %collective-permute-start.34 = (bf16[24,2304]{1,0:T(8,128)(2,1)S(1)}, bf16[24,2304]{1,0:T(8,128)(2,1)S(1)}, u32[]{:S(2)}, u32[]{:S(2)}) collective-permute-start(bf16[24,2304]{1,0:T(8,128)(2,1)S(1)} %get-tuple-element.139), channel_id=1, source_target_pairs={{0,16},{2,18},{4,20},{6,22},{8,24},{10,26},{12,28},{14,30},{16,0},... | collective-permute-start | bytes 331784 | tf_op jit(solution)/shard_map/ppermute | solution.py:687
  (29 other events, 59.4 us)
Sparse Core Ops, SparseCore 0:
  43.4 91.7 all-gather.1
